TPU v7x, 32 devices: a whole 2x2x4 slice. The times are simulated.
32 devices in a mesh: gx: 4 (over z), gy: 8 (over y, x, core).
Axes of the slice: x: 2, y: 2, z: 4, core: 2. Of those that a mesh axis runs over, the one named last changes fastest.
Arguments:
- flow_populations: float32 [19, 64, 64, 128], P(None, 'gx', 'gy'), may hold values from 0 to 1, as said below
- solute_populations: float32 [7, 64, 64, 128], P(None, 'gx', 'gy'), may hold values from 0 to 1, as said below
- voxel_kind: int32 [64, 64, 128], P('gx', 'gy'), may hold values from 0 to 3, as said below
Outputs:
- density: float32 [64, 64, 128], P('gx', 'gy')
- momentum: float32 [3, 64, 64, 128], P(None, 'gx', 'gy')
- concentration: float32 [64, 64, 128], P('gx', 'gy')
Inputs may be any that keep to these rules, and one draw needn't show every extreme that they name: `flow_populations`: each flow population is its lattice weight w_i times a factor between 0.5 and 1.5. `solute_populations`: each solute population is its lattice weight v_k times a positive factor of at most 1.9. `voxel_kind`: the first z plane holds only inlet and solid voxels, the last z plane only outlet and solid voxels, every other plane only pore and solid voxels.
All inputs are finite; a program needn't handle non-finite values.
Results may differ from a plain program's by a relative error of at most 0.0001.
Values sent between devices are 32-bit elements; how exact they have to be, the bound alone decides.
No kernel may reach another device: no remote copies, remote signals or barrier semaphores. Data moves between devices by JAX's collectives and lax.ppermute only.
A program may use at most 64 MiB of HBM per device.

v0:
```python
import jax
import jax.numpy as jnp
from jax import lax
from jax.sharding import PartitionSpec as P

STEPS = 3


flow_velocity = [
    (0, 0, 0),
    (1, 0, 0),
    (-1, 0, 0),
    (0, 1, 0),
    (0, -1, 0),
    (0, 0, 1),
    (0, 0, -1),
    (1, 1, 0),
    (-1, -1, 0),
    (1, -1, 0),
    (-1, 1, 0),
    (1, 0, 1),
    (-1, 0, -1),
    (1, 0, -1),
    (-1, 0, 1),
    (0, 1, 1),
    (0, -1, -1),
    (0, 1, -1),
    (0, -1, 1),
]
flow_weight = [1.0 / 3.0] + [1.0 / 18.0] * 6 + [1.0 / 36.0] * 12
solute_velocity = flow_velocity[:7]
solute_weight = [0.25] + [0.125] * 6
all_velocity = flow_velocity + solute_velocity
flow_plus = 1.25
flow_minus = 1.0 / 1.125
solute_plus = 1.0 / 1.75
solute_minus = 1.0 / 0.7
inlet_density = 1.05
outlet_density = 0.95
inlet_solute = 1.0


def padded(block, sides, width):
    for axis, dim in sides:
        count = lax.axis_size(axis)
        forward = [(i, i + 1) for i in range(count - 1)]
        forward.append((count - 1, 0))
        backward = [(target, source) for source, target in forward]
        low = lax.ppermute(
            lax.slice_in_dim(block, block.shape[dim] - width, None, axis=dim), axis, forward
        )
        high = lax.ppermute(lax.slice_in_dim(block, 0, width, axis=dim), axis, backward)
        block = jnp.concatenate([low, block, high], axis=dim)
    return block


def opposite(component):
    if component == 0:
        return 0
    if component % 2 == 1:
        return component + 1
    return component - 1


def moments(flow):
    density = jnp.sum(flow, axis=0)
    components = []
    for axis_number in range(3):
        summed = jnp.zeros_like(density)
        for component, velocity in enumerate(flow_velocity):
            if velocity[axis_number] != 0:
                summed = summed + velocity[axis_number] * flow[component]
        components.append(summed)
    return (density, components)


def collide(flow, solute, voxel_kind):
    density, (mom_x, mom_y, mom_z) = moments(flow)
    concentration = jnp.sum(solute, axis=0)
    square = mom_x * mom_x + mom_y * mom_y + mom_z * mom_z
    is_fluid = voxel_kind == 0
    is_inlet = voxel_kind == 2
    is_outlet = voxel_kind == 3
    outgoing = []
    for component, velocity in enumerate(flow_velocity):
        weight = flow_weight[component]
        mirror = opposite(component)
        projection = velocity[0] * mom_x + velocity[1] * mom_y + velocity[2] * mom_z
        even_eq = weight * (density + 4.5 * projection * projection - 1.5 * square)
        odd_eq = weight * 3.0 * projection
        even_part = 0.5 * (flow[component] + flow[mirror])
        odd_part = 0.5 * (flow[component] - flow[mirror])
        relaxed = (
            flow[component] - flow_plus * (even_part - even_eq) - flow_minus * (odd_part - odd_eq)
        )
        result = jnp.where(is_fluid, relaxed, flow[mirror])
        result = jnp.where(is_inlet, weight * inlet_density, result)
        result = jnp.where(is_outlet, weight * outlet_density, result)
        outgoing.append(result)
    for component, velocity in enumerate(solute_velocity):
        weight = solute_weight[component]
        mirror = opposite(component)
        projection = velocity[0] * mom_x + velocity[1] * mom_y + velocity[2] * mom_z
        even_eq = weight * concentration
        odd_eq = weight * 4.0 * concentration * projection
        even_part = 0.5 * (solute[component] + solute[mirror])
        odd_part = 0.5 * (solute[component] - solute[mirror])
        relaxed = (
            solute[component]
            - solute_plus * (even_part - even_eq)
            - solute_minus * (odd_part - odd_eq)
        )
        result = jnp.where(is_fluid, relaxed, solute[mirror])
        result = jnp.where(is_inlet, weight * inlet_solute, result)
        result = jnp.where(is_outlet, jnp.zeros_like(result), result)
        outgoing.append(result)
    return jnp.stack(outgoing)


def depth_shift(section, along_z):
    if along_z == 1:
        return jnp.concatenate([jnp.zeros_like(section[:, :, :1]), section[:, :, :-1]], axis=2)
    if along_z == -1:
        return jnp.concatenate([section[:, :, 1:], jnp.zeros_like(section[:, :, :1])], axis=2)
    return section


def propagate(stacked):
    cells_x = stacked.shape[1]
    cells_y = stacked.shape[2]
    planes = []
    cross_x = [component for component, velocity in enumerate(all_velocity) if velocity[0] != 0]
    cross_y = [component for component, velocity in enumerate(all_velocity) if velocity[1] != 0]
    padded_x = padded(jnp.stack([stacked[component] for component in cross_x]), (("gx", 1),), 1)
    after_x = [stacked[component] for component in range(len(all_velocity))]
    for position, component in enumerate(cross_x):
        shift_x = all_velocity[component][0]
        after_x[component] = padded_x[position, 1 - shift_x : 1 - shift_x + cells_x, :, :]
    padded_y = padded(jnp.stack([after_x[component] for component in cross_y]), (("gy", 2),), 1)
    after_y = list(after_x)
    for position, component in enumerate(cross_y):
        shift_y = all_velocity[component][1]
        after_y[component] = padded_y[position, :, 1 - shift_y : 1 - shift_y + cells_y, :]
    for component, velocity in enumerate(all_velocity):
        planes.append(depth_shift(after_y[component], velocity[2]))
    return jnp.stack(planes)


def local(flow_populations, solute_populations, voxel_kind):
    flow = flow_populations
    solute = solute_populations
    for sweep in range(STEPS):
        outgoing = collide(flow, solute, voxel_kind)
        shifted = propagate(outgoing)
        flow = shifted[:19]
        solute = shifted[19:]
    density, components = moments(flow)
    return (density, jnp.stack(components), jnp.sum(solute, axis=0))


def solution(mesh):
    placed = (P(None, "gx", "gy", None), P(None, "gx", "gy", None), P("gx", "gy", None))
    return jax.shard_map(
        local,
        mesh=mesh,
        in_specs=placed,
        out_specs=(P("gx", "gy", None), P(None, "gx", "gy", None), P("gx", "gy", None)),
        check_vma=False,
    )
```

profile of v0, /device:TPU:0, one launch (start us, length us, event | category | flops | bytes accessed | tf_op | source)
XLA Modules:
  0.0 53.8 jit_solution(13548645552287623831)
XLA Ops:
  0.6 1.5 %reduce_sum.322 = f32[16,8,128]{2,1,0:T(8,128)S(1)} reduce(f32[19,16,8,128]{3,2,1,0:T(8,128)} %param.3, f32[]{:T(128)} %constant.2.clone.1), dimensions={0}, to_apply=%region_0.0 | reduce | flops 294912 | bytes 1310724 | tf_op jit(solution)/shard_map/reduce_sum | solution.py:66
  2.1 1.1 %reduce_sum.323 = f32[16,8,128]{2,1,0:T(8,128)S(1)} reduce(f32[7,16,8,128]{3,2,1,0:T(8,128)} %param.4, f32[]{:T(128)} %constant.2.clone.1), dimensions={0}, to_apply=%region_1.0 | reduce | flops 98304 | bytes 524292 | tf_op jit(solution)/shard_map/reduce_sum | solution.py:79
  4.3 0.6 %copy-done.1 = f32[7,16,8,128]{3,2,1,0:T(8,128)S(1)} copy-done((f32[7,16,8,128]{3,2,1,0:T(8,128)S(1)}, f32[7,16,8,128]{3,2,1,0:T(8,128)}, u32[]{:S(2)}) %copy-start.1) | copy-done | bytes 458776
  5.0 5.1 %collective-permute-start.1 = (f32[12,1,8,128]{3,2,1,0:T(8,128)S(1)}, f32[12,1,8,128]{3,2,1,0:T(8,128)S(1)}, u32[]{:S(2)}, u32[]{:S(2)}) collective-permute-start(f32[12,1,8,128]{3,2,1,0:T(8,128)S(1)} %get-tuple-element.147), channel_id=1, source_target_pairs={{8,0},{16,8},{24,16},{0,24},{9,1},{17,9},{25,17},{1,25},{10,2},{18... | collective-permute-start | bytes 147464 | tf_op jit(solution)/shard_map/ppermute | solution.py:52
  10.2 5.8 %collective-permute-done = f32[12,1,8,128]{3,2,1,0:T(8,128)S(1)} collective-permute-done((f32[12,1,8,128]{3,2,1,0:T(8,128)S(1)}, f32[12,1,8,128]{3,2,1,0:T(8,128)S(1)}, u32[]{:S(2)}, u32[]{:S(2)}) %collective-permute-start) | collective-permute-done | bytes 49184 | tf_op jit(solution)/shard_map/ppermute | solution.py:49
  16.7 0.5 collective-permute-start.3
  17.8 2.1 %collective-permute-done.3 = f32[12,16,1,128]{3,2,1,0:T(1,128)S(1)} collective-permute-done((f32[12,16,1,128]{3,2,1,0:T(1,128)S(1)}, f32[12,16,1,128]{3,2,1,0:T(1,128)S(1)}, u32[]{:S(2)}, u32[]{:S(2)}) %collective-permute-start.3) | collective-permute-done | bytes 98336 | tf_op jit(solution)/shard_map/ppermute | solution.py:52
  19.9 2.9 %collective-permute-done.2 = f32[12,16,1,128]{3,2,1,0:T(1,128)S(1)} collective-permute-done((f32[12,16,1,128]{3,2,1,0:T(1,128)S(1)}, f32[12,16,1,128]{3,2,1,0:T(1,128)S(1)}, u32[]{:S(2)}, u32[]{:S(2)}) %collective-permute-start.2) | collective-permute-done | bytes 98336 | tf_op jit(solution)/shard_map/ppermute | solution.py:49
  23.0 0.3 multiply_multiply_fusion.60
  24.9 2.0 %collective-permute-start.4 = (f32[12,1,8,128]{3,2,1,0:T(8,128)S(1)}, f32[12,1,8,128]{3,2,1,0:T(8,128)S(1)}, u32[]{:S(2)}, u32[]{:S(2)}) collective-permute-start(f32[12,1,8,128]{3,2,1,0:T(8,128)S(1)} %get-tuple-element.142), channel_id=1, source_target_pairs={{0,8},{8,16},{16,24},{24,0},{1,9},{9,17},{17,25},{25,1},{2,10},{10... | collective-permute-start | bytes 147464 | tf_op jit(solution)/shard_map/ppermute | solution.py:49
  27.2 3.7 %collective-permute-done.4 = f32[12,1,8,128]{3,2,1,0:T(8,128)S(1)} collective-permute-done((f32[12,1,8,128]{3,2,1,0:T(8,128)S(1)}, f32[12,1,8,128]{3,2,1,0:T(8,128)S(1)}, u32[]{:S(2)}, u32[]{:S(2)}) %collective-permute-start.4) | collective-permute-done | bytes 49184 | tf_op jit(solution)/shard_map/ppermute | solution.py:49
  31.8 0.5 collective-permute-start.6
  32.6 2.2 %collective-permute-done.7 = f32[12,16,1,128]{3,2,1,0:T(1,128)S(1)} collective-permute-done((f32[12,16,1,128]{3,2,1,0:T(1,128)S(1)}, f32[12,16,1,128]{3,2,1,0:T(1,128)S(1)}, u32[]{:S(2)}, u32[]{:S(2)}) %collective-permute-start.7) | collective-permute-done | bytes 98336 | tf_op jit(solution)/shard_map/ppermute | solution.py:52
  34.8 1.9 %collective-permute-done.6 = f32[12,16,1,128]{3,2,1,0:T(1,128)S(1)} collective-permute-done((f32[12,16,1,128]{3,2,1,0:T(1,128)S(1)}, f32[12,16,1,128]{3,2,1,0:T(1,128)S(1)}, u32[]{:S(2)}, u32[]{:S(2)}) %collective-permute-start.6) | collective-permute-done | bytes 98336 | tf_op jit(solution)/shard_map/ppermute | solution.py:49
  37.0 0.3 multiply_multiply_fusion.58
  39.1 3.7 %collective-permute-start.9 = (f32[12,1,8,128]{3,2,1,0:T(8,128)S(1)}, f32[12,1,8,128]{3,2,1,0:T(8,128)S(1)}, u32[]{:S(2)}, u32[]{:S(2)}) collective-permute-start(f32[12,1,8,128]{3,2,1,0:T(8,128)S(1)} %get-tuple-element.136), channel_id=1, source_target_pairs={{8,0},{16,8},{24,16},{0,24},{9,1},{17,9},{25,17},{1,25},{10,2},{18... | collective-permute-start | bytes 147464 | tf_op jit(solution)/shard_map/ppermute | solution.py:52
  42.8 1.9 %collective-permute-done.8 = f32[12,1,8,128]{3,2,1,0:T(8,128)S(1)} collective-permute-done((f32[12,1,8,128]{3,2,1,0:T(8,128)S(1)}, f32[12,1,8,128]{3,2,1,0:T(8,128)S(1)}, u32[]{:S(2)}, u32[]{:S(2)}) %collective-permute-start.8) | collective-permute-done | bytes 49184 | tf_op jit(solution)/shard_map/ppermute | solution.py:49
  45.5 0.3 collective-permute-start.11
  45.8 0.3 collective-permute-start.10
  46.4 2.2 %collective-permute-done.11 = f32[12,16,1,128]{3,2,1,0:T(1,128)S(1)} collective-permute-done((f32[12,16,1,128]{3,2,1,0:T(1,128)S(1)}, f32[12,16,1,128]{3,2,1,0:T(1,128)S(1)}, u32[]{:S(2)}, u32[]{:S(2)}) %collective-permute-start.11) | collective-permute-done | bytes 98336 | tf_op jit(solution)/shard_map/ppermute | solution.py:52
  48.7 2.0 %collective-permute-done.10 = f32[12,16,1,128]{3,2,1,0:T(1,128)S(1)} collective-permute-done((f32[12,16,1,128]{3,2,1,0:T(1,128)S(1)}, f32[12,16,1,128]{3,2,1,0:T(1,128)S(1)}, u32[]{:S(2)}, u32[]{:S(2)}) %collective-permute-start.10) | collective-permute-done | bytes 98336 | tf_op jit(solution)/shard_map/ppermute | solution.py:49
  50.9 0.8 %fusion.607 = (f32[16,8,128]{2,1,0:T(8,128)}, f32[16,8,128]{2,1,0:T(8,128)S(1)}, f32[16,8,128]{2,1,0:T(8,128)S(1)}) fusion(f32[12,16,1,128]{3,2,1,0:T(1,128)S(1)} %collective-permute-done.11, f32[12,16,8,128]{3,2,1,0:T(8,128)S(1)} %constant_dynamic-update-slice_fusion.60, f32[12,16,1,128]{3,2,1,0:T(1,128)S(1)} %collective-permute-done.10, ...), kind=kLoop, calls=%fused_computation.744 | loop fusion | flops 524288 | bytes 2505728 | tf_op jit(solution)/shard_map/reduce_sum | solution.py:158
  52.3 0.7 %pad_maximum_fusion = f32[3,16,8,128]{3,2,1,0:T(8,128)} fusion(f32[1,16,8,128]{3,2,1,0:T(8,128)S(1)} %add_bitcast_fusion, f32[1,16,8,128]{3,2,1,0:T(8,128)S(1)} %get-tuple-element.29, f32[1,16,8,128]{3,2,1,0:T(8,128)S(1)} %get-tuple-element.22), kind=kLoop, calls=%fused_computation | loop fusion | flops 98304 | bytes 393216 | tf_op jit(solution)/shard_map/stack | solution.py:158
  52.9 0.8 %add_add_fusion = f32[16,8,128]{2,1,0:T(8,128)} fusion(f32[16,8,128]{2,1,0:T(8,128)S(1)} %get-tuple-element.28, f32[16,8,128]{2,1,0:T(8,128)S(1)} %get-tuple-element.27, f32[16,8,128]{2,1,0:T(8,128)S(1)} %get-tuple-element.26, f32[16,8,128]{2,1,0:T(8,128)S(1)} %get-tuple-element.25, f32[16,8,128]{2,1,0:T(8,128)S(1)} %get-tuple-element.31, ...), kind=kLoop, calls=%fused_computation.1080 | loop fusion | flops 622592 | bytes 1616896 | tf_op jit(solution)/shard_map/reduce_sum | solution.py:66
  (117 shorter events, 9.4 us)
Async XLA Ops:
  0.6 2.6 %copy-start = (f32[19,16,8,128]{3,2,1,0:T(8,128)S(1)}, f32[19,16,8,128]{3,2,1,0:T(8,128)}, u32[]{:S(2)}) copy-start(f32[19,16,8,128]{3,2,1,0:T(8,128)} %param.3) | copy-start | bytes 3735556
  2.1 1.3 %copy-start.2 = (s32[16,8,128]{2,1,0:T(8,128)S(1)}, s32[16,8,128]{2,1,0:T(8,128)}, u32[]{:S(2)}) copy-start(s32[16,8,128]{2,1,0:T(8,128)} %param.5) | copy-start | bytes 196612
  3.9 1.0 %copy-start.1 = (f32[7,16,8,128]{3,2,1,0:T(8,128)S(1)}, f32[7,16,8,128]{3,2,1,0:T(8,128)}, u32[]{:S(2)}) copy-start(f32[7,16,8,128]{3,2,1,0:T(8,128)} %param.4) | copy-start | bytes 1376260
  5.0 11.0 %collective-permute-start.1 = (f32[12,1,8,128]{3,2,1,0:T(8,128)S(1)}, f32[12,1,8,128]{3,2,1,0:T(8,128)S(1)}, u32[]{:S(2)}, u32[]{:S(2)}) collective-permute-start(f32[12,1,8,128]{3,2,1,0:T(8,128)S(1)} %get-tuple-element.147), channel_id=1, source_target_pairs={{8,0},{16,8},{24,16},{0,24},{9,1},{17,9},{25,17},{1,25},{10,2},{18... | collective-permute-start | bytes 147464 | tf_op jit(solution)/shard_map/ppermute | solution.py:52
  10.1 5.9 %collective-permute-start = (f32[12,1,8,128]{3,2,1,0:T(8,128)S(1)}, f32[12,1,8,128]{3,2,1,0:T(8,128)S(1)}, u32[]{:S(2)}, u32[]{:S(2)}) collective-permute-start(f32[12,1,8,128]{3,2,1,0:T(8,128)S(1)} %get-tuple-element.148), channel_id=1, source_target_pairs={{0,8},{8,16},{16,24},{24,0},{1,9},{9,17},{17,25},{25,1},{2,10},{10... | collective-permute-start | bytes 147464 | tf_op jit(solution)/shard_map/ppermute | solution.py:49
  16.7 3.2 %collective-permute-start.3 = (f32[12,16,1,128]{3,2,1,0:T(1,128)S(1)}, f32[12,16,1,128]{3,2,1,0:T(1,128)S(1)}, u32[]{:S(2)}, u32[]{:S(2)}) collective-permute-start(f32[12,16,1,128]{3,2,1,0:T(1,128)S(1)} %get-tuple-element.145), channel_id=1, source_target_pairs={{1,0},{2,1},{3,2},{4,3},{5,4},{6,5},{7,6},{0,7},{9,8},{10,9},{11,1... | collective-permute-start | bytes 294920 | tf_op jit(solution)/shard_map/ppermute | solution.py:52
  17.2 5.6 %collective-permute-start.2 = (f32[12,16,1,128]{3,2,1,0:T(1,128)S(1)}, f32[12,16,1,128]{3,2,1,0:T(1,128)S(1)}, u32[]{:S(2)}, u32[]{:S(2)}) collective-permute-start(f32[12,16,1,128]{3,2,1,0:T(1,128)S(1)} %get-tuple-element.146), channel_id=1, source_target_pairs={{0,1},{1,2},{2,3},{3,4},{4,5},{5,6},{6,7},{7,0},{8,9},{9,10},{10,1... | collective-permute-start | bytes 294920 | tf_op jit(solution)/shard_map/ppermute | solution.py:49
  24.9 6.0 %collective-permute-start.5 = (f32[12,1,8,128]{3,2,1,0:T(8,128)S(1)}, f32[12,1,8,128]{3,2,1,0:T(8,128)S(1)}, u32[]{:S(2)}, u32[]{:S(2)}) collective-permute-start(f32[12,1,8,128]{3,2,1,0:T(8,128)S(1)} %get-tuple-element.141), channel_id=1, source_target_pairs={{8,0},{16,8},{24,16},{0,24},{9,1},{17,9},{25,17},{1,25},{10,2},{18... | collective-permute-start | bytes 147464 | tf_op jit(solution)/shard_map/ppermute | solution.py:52
  24.9 5.9 %collective-permute-start.4 = (f32[12,1,8,128]{3,2,1,0:T(8,128)S(1)}, f32[12,1,8,128]{3,2,1,0:T(8,128)S(1)}, u32[]{:S(2)}, u32[]{:S(2)}) collective-permute-start(f32[12,1,8,128]{3,2,1,0:T(8,128)S(1)} %get-tuple-element.142), channel_id=1, source_target_pairs={{0,8},{8,16},{16,24},{24,0},{1,9},{9,17},{17,25},{25,1},{2,10},{10... | collective-permute-start | bytes 147464 | tf_op jit(solution)/shard_map/ppermute | solution.py:49
  31.7 3.1 %collective-permute-start.7 = (f32[12,16,1,128]{3,2,1,0:T(1,128)S(1)}, f32[12,16,1,128]{3,2,1,0:T(1,128)S(1)}, u32[]{:S(2)}, u32[]{:S(2)}) collective-permute-start(f32[12,16,1,128]{3,2,1,0:T(1,128)S(1)} %get-tuple-element.139), channel_id=1, source_target_pairs={{1,0},{2,1},{3,2},{4,3},{5,4},{6,5},{7,6},{0,7},{9,8},{10,9},{11,1... | collective-permute-start | bytes 294920 | tf_op jit(solution)/shard_map/ppermute | solution.py:52
  31.8 5.0 %collective-permute-start.6 = (f32[12,16,1,128]{3,2,1,0:T(1,128)S(1)}, f32[12,16,1,128]{3,2,1,0:T(1,128)S(1)}, u32[]{:S(2)}, u32[]{:S(2)}) collective-permute-start(f32[12,16,1,128]{3,2,1,0:T(1,128)S(1)} %get-tuple-element.140), channel_id=1, source_target_pairs={{0,1},{1,2},{2,3},{3,4},{4,5},{5,6},{6,7},{7,0},{8,9},{9,10},{10,1... | collective-permute-start | bytes 294920 | tf_op jit(solution)/shard_map/ppermute | solution.py:49
  38.7 5.9 %collective-permute-start.8 = (f32[12,1,8,128]{3,2,1,0:T(8,128)S(1)}, f32[12,1,8,128]{3,2,1,0:T(8,128)S(1)}, u32[]{:S(2)}, u32[]{:S(2)}) collective-permute-start(f32[12,1,8,128]{3,2,1,0:T(8,128)S(1)} %get-tuple-element.135), channel_id=1, source_target_pairs={{0,8},{8,16},{16,24},{24,0},{1,9},{9,17},{17,25},{25,1},{2,10},{10... | collective-permute-start | bytes 147464 | tf_op jit(solution)/shard_map/ppermute | solution.py:49
  39.1 5.6 %collective-permute-start.9 = (f32[12,1,8,128]{3,2,1,0:T(8,128)S(1)}, f32[12,1,8,128]{3,2,1,0:T(8,128)S(1)}, u32[]{:S(2)}, u32[]{:S(2)}) collective-permute-start(f32[12,1,8,128]{3,2,1,0:T(8,128)S(1)} %get-tuple-element.136), channel_id=1, source_target_pairs={{8,0},{16,8},{24,16},{0,24},{9,1},{17,9},{25,17},{1,25},{10,2},{18... | collective-permute-start | bytes 147464 | tf_op jit(solution)/shard_map/ppermute | solution.py:52
  45.5 3.2 %collective-permute-start.11 = (f32[12,16,1,128]{3,2,1,0:T(1,128)S(1)}, f32[12,16,1,128]{3,2,1,0:T(1,128)S(1)}, u32[]{:S(2)}, u32[]{:S(2)}) collective-permute-start(f32[12,16,1,128]{3,2,1,0:T(1,128)S(1)} %get-tuple-element.133), channel_id=1, source_target_pairs={{1,0},{2,1},{3,2},{4,3},{5,4},{6,5},{7,6},{0,7},{9,8},{10,9},{11,1... | collective-permute-start | bytes 294920 | tf_op jit(solution)/shard_map/ppermute | solution.py:52
  45.8 4.9 %collective-permute-start.10 = (f32[12,16,1,128]{3,2,1,0:T(1,128)S(1)}, f32[12,16,1,128]{3,2,1,0:T(1,128)S(1)}, u32[]{:S(2)}, u32[]{:S(2)}) collective-permute-start(f32[12,16,1,128]{3,2,1,0:T(1,128)S(1)} %get-tuple-element.134), channel_id=1, source_target_pairs={{0,1},{1,2},{2,3},{3,4},{4,5},{5,6},{6,7},{7,0},{8,9},{9,10},{10,1... | collective-permute-start | bytes 294920 | tf_op jit(solution)/shard_map/ppermute | solution.py:49
where the time goes:
time: 54 us; the launch traced here: 53.8 us
  waiting for transfers between devices  24.8 us (46%)
  other arithmetic  13 us (24%)
  starting transfers between devices  12.8 us (24%)
  local copies, waits for them, and re-layouts  1.94 us (4%)
  between operations  1.17 us (2%)
    ppermute x6, waiting for transfers between devices, padded(): lax.ppermute(lax.slice_in_dim(block, block.shape[dim] - width, None, axis...  18.3 us
    ppermute x6, starting transfers between devices, padded(): lax.ppermute(lax.slice_in_dim(block, 0, width, axis=dim), axis, backward)  9.7 us
    ppermute x6, waiting for transfers between devices, padded(): lax.ppermute(lax.slice_in_dim(block, 0, width, axis=dim), axis, backward)  6.53 us
    unnamed x55, other arithmetic  4.5 us
    ppermute x6, starting transfers between devices, padded(): lax.ppermute(lax.slice_in_dim(block, block.shape[dim] - width, None, axis...  3.09 us
    reduce_sum x2, other arithmetic, moments(): density = jnp.sum(flow, axis=0)  2.26 us
    reduce_sum x1, other arithmetic, collide(): concentration = jnp.sum(solute, axis=0)  1.08 us
  transfers between devices with their start and end apart: 12, of which 9 were waited for; matrix products, arithmetic and copies ran while one was open for 3% of the time, Pallas kernels for 0%

commit v1 on v0

v1 whole, which is shorter than its diff:
```python
import functools
import math

import jax
import jax.numpy as jnp
from jax import lax
from jax.experimental import pallas as pl
from jax.experimental.pallas import tpu as pltpu
from jax.sharding import PartitionSpec as P

STEPS = 3
HALO = STEPS

flow_velocity = [
    (0, 0, 0),
    (1, 0, 0),
    (-1, 0, 0),
    (0, 1, 0),
    (0, -1, 0),
    (0, 0, 1),
    (0, 0, -1),
    (1, 1, 0),
    (-1, -1, 0),
    (1, -1, 0),
    (-1, 1, 0),
    (1, 0, 1),
    (-1, 0, -1),
    (1, 0, -1),
    (-1, 0, 1),
    (0, 1, 1),
    (0, -1, -1),
    (0, 1, -1),
    (0, -1, 1),
]
FLOW = len(flow_velocity)
all_velocity = flow_velocity + flow_velocity[:7]
COUNT = len(all_velocity)
KIND = COUNT
flow_plus = 1.25
flow_minus = 1.0 / 1.125
solute_plus = 1.0 / 1.75
solute_minus = 1.0 / 0.7
inlet_density = 1.05
outlet_density = 0.95
inlet_solute = 1.0


def mirrored(channel, sign_x, sign_y):
    if channel == KIND:
        return KIND
    cx, cy, cz = all_velocity[channel]
    wanted = (cx * sign_x, cy * sign_y, cz)
    if channel < FLOW:
        return flow_velocity.index(wanted)
    return FLOW + flow_velocity[:7].index(wanted)


face_x = [
    (c, d) for d in range(1, HALO + 1) for c in range(COUNT) if d - all_velocity[c][0] <= HALO - 1
] + [(KIND, d) for d in range(1, HALO)]
face_y = [
    (c, d) for d in range(1, HALO + 1) for c in range(COUNT) if d - all_velocity[c][1] <= HALO - 1
] + [(KIND, d) for d in range(1, HALO)]
corner = [
    (c, dx, dy)
    for dx in range(1, HALO + 1)
    for dy in range(1, HALO + 1)
    for c in range(COUNT)
    if dx - all_velocity[c][0] <= HALO - 1 and dy - all_velocity[c][1] <= HALO - 1
] + [(KIND, dx, dy) for dx in range(1, HALO) for dy in range(1, HALO)]
CORNER_ROWS = -(-len(corner) // 8) * 8


def collide(flow, solute, kind):
    pore = kind == 0.0
    solid = kind == 1.0
    inlet = kind == 2.0
    zero = jnp.zeros_like(kind)
    pairs = range(1, FLOW, 2)
    total = {i: flow[i] + flow[i + 1] for i in pairs}
    gap = {i: flow[i] - flow[i + 1] for i in pairs}
    density = (flow[0] + total[1] + total[3]) + (total[5] + total[7] + total[9])
    density = density + ((total[11] + total[13]) + (total[15] + total[17]))
    mom_x = (gap[1] + gap[7]) + (gap[9] + gap[11]) + gap[13]
    mom_y = (gap[3] + gap[7]) + (gap[15] - gap[9]) + gap[17]
    mom_z = (gap[5] + gap[11]) + (gap[15] - gap[13]) - gap[17]
    square = mom_x * mom_x + mom_y * mom_y + mom_z * mom_z
    wall = jnp.where(solid, 0.5, zero)
    even = jnp.where(pore, (1.0 - flow_plus) / 2.0, wall)
    odd = jnp.where(pore, (1.0 - flow_minus) / 2.0, -wall)
    border = jnp.where(inlet, inlet_density, jnp.where(solid, 0.0, outlet_density))
    base = jnp.where(pore, flow_plus * density - (1.5 * flow_plus) * square, border)
    base_18 = base * (1.0 / 18.0)
    base_36 = base * (1.0 / 36.0)
    scale = math.sqrt(4.5 * flow_plus / 36.0)
    held = jnp.where(pore, scale, zero)
    vel = (mom_x * held, mom_y * held, mom_z * held)
    along = 3.0 * flow_minus / (36.0 * scale)
    out = [None] * COUNT
    out[0] = (even + even) * flow[0] + base * (1.0 / 3.0)
    for i in pairs:
        cx, cy, cz = flow_velocity[i]
        parts = [(c, v) for c, v in zip((cx, cy, cz), vel) if c != 0]
        if len(parts) == 1:
            t = parts[0][1]
            a = even * total[i] + (base_18 + 2.0 * (t * t))
            b = odd * gap[i] + (2.0 * along) * t
        else:
            t = parts[0][1] + parts[1][1] if parts[1][0] > 0 else parts[0][1] - parts[1][1]
            a = even * total[i] + (base_36 + t * t)
            b = odd * gap[i] + along * t
        out[i] = a + b
        out[i + 1] = a - b
    total = {i: solute[i] + solute[i + 1] for i in (1, 3, 5)}
    gap = {i: solute[i] - solute[i + 1] for i in (1, 3, 5)}
    concentration = (solute[0] + total[1]) + (total[3] + total[5])
    even = jnp.where(pore, (1.0 - solute_plus) / 2.0, wall)
    odd = jnp.where(pore, (1.0 - solute_minus) / 2.0, -wall)
    border = jnp.where(inlet, inlet_solute, zero)
    base = jnp.where(pore, solute_plus * concentration, border) * 0.125
    drift = concentration * (0.5 * solute_minus / scale)
    out[FLOW] = (even + even) * solute[0] + (base + base)
    for i, t in zip((1, 3, 5), vel):
        a = even * total[i] + base
        b = odd * gap[i] + drift * t
        out[FLOW + i] = a + b
        out[FLOW + i + 1] = a - b
    return out


def depth_shift(section, along_z, lane):
    depth = section.shape[-1]
    if along_z == 1:
        return jnp.where(lane == 0, 0.0, pltpu.roll(section, 1, section.ndim - 1))
    if along_z == -1:
        return jnp.where(lane == depth - 1, 0.0, pltpu.roll(section, depth - 1, section.ndim - 1))
    return section


def store_outgoing(values, lane, store):
    for c in range(COUNT):
        store(c, depth_shift(values[c], all_velocity[c][2], lane))


def first_kernel(cells_x, cells_y, odd_ref, flow_ref, solute_ref, kind_ref, post_ref, kindf_ref,
                 xa_ref, xb_ref, ya_ref, yb_ref, cab_ref, cbb_ref):
    depth = kind_ref.shape[-1]
    lane = lax.broadcasted_iota(jnp.int32, (cells_y, depth), 1)

    def plane(x, carry):
        kind = kind_ref[x].astype(jnp.float32)
        rows = pl.ds(pl.multiple_of(x * cells_y, cells_y), cells_y)
        kindf_ref[rows, :] = kind
        values = collide(
            [flow_ref[c, x] for c in range(FLOW)],
            [solute_ref[c, x] for c in range(COUNT - FLOW)],
            kind,
        )

        def store(c, value):
            post_ref[c, rows, :] = value

        store_outgoing(values, lane, store)
        return carry

    lax.fori_loop(0, cells_x, plane, 0)

    def held(c, where):
        return kindf_ref[where, :] if c == KIND else post_ref[c, where, :]

    for odd_x in (0, 1):

        @pl.when(odd_ref[0] == odd_x)
        def _():
            for ref, sign in ((xa_ref, 1 - 2 * odd_x), (xb_ref, 2 * odd_x - 1)):
                for k, (c, d) in enumerate(face_x):
                    x = cells_x - d if sign > 0 else d - 1
                    ref[k] = held(mirrored(c, sign, 1), pl.ds(x * cells_y, cells_y))

    for odd_y in (0, 1):

        @pl.when(odd_ref[1] == odd_y)
        def _():
            for ref, sign in ((ya_ref, 1 - 2 * odd_y), (yb_ref, 2 * odd_y - 1)):
                for k, (c, d) in enumerate(face_y):
                    y = cells_y - d if sign > 0 else d - 1
                    ref[k] = held(mirrored(c, 1, sign), pl.ds(y, cells_x, stride=cells_y))

    for odd_x in (0, 1):
        for odd_y in (0, 1):

            @pl.when((odd_ref[0] == odd_x) & (odd_ref[1] == odd_y))
            def _():
                sign_y = 2 * odd_y - 1
                for ref, sign_x in ((cab_ref, 1 - 2 * odd_x), (cbb_ref, 2 * odd_x - 1)):
                    for k, (c, dx, dy) in enumerate(corner):
                        x = cells_x - dx if sign_x > 0 else dx - 1
                        y = cells_y - dy if sign_y > 0 else dy - 1
                        ref[pl.ds(k, 1), :] = held(
                            mirrored(c, sign_x, sign_y), pl.ds(x * cells_y + y, 1)
                        )


def forward_kernel(cells_y, odd_ref, xa_ref, xb_ref, out_ref):
    for odd_y in (0, 1):

        @pl.when(odd_ref[1] == odd_y)
        def _():
            sign_y = 1 - 2 * odd_y
            for side, ref in enumerate((xa_ref, xb_ref)):
                for k, (c, dx, dy) in enumerate(corner):
                    y = cells_y - dy if sign_y > 0 else dy - 1
                    out_ref[side, pl.ds(k, 1), :] = ref[
                        face_x.index((mirrored(c, 1, sign_y), dx)), pl.ds(y, 1), :
                    ]


def last_kernel(cells_x, cells_y, odd_ref, post_ref, kindf_ref, xa_ref, xb_ref, ya_ref, yb_ref,
                cab_ref, cbb_ref, cya_ref, density_ref, momentum_ref, concentration_ref,
                one_ref, two_ref, kinds_ref):
    depth = post_ref.shape[-1]
    pitch = cells_y + 2 * HALO

    def row(x, y):
        return (x + HALO) * pitch + y + HALO

    def put(c, where, value):
        if c == KIND:
            kinds_ref[where, :] = value
        else:
            one_ref[c, where, :] = value

    for x in range(cells_x):
        for c in range(COUNT):
            put(c, pl.ds(row(x, 0), cells_y), post_ref[c, pl.ds(x * cells_y, cells_y), :])
        put(KIND, pl.ds(row(x, 0), cells_y), kindf_ref[pl.ds(x * cells_y, cells_y), :])

    def beyond(cells, sign, d):
        return cells - 1 + d if sign > 0 else -d

    for odd_x in (0, 1):

        @pl.when(odd_ref[0] == odd_x)
        def _():
            for ref, sign in ((xa_ref, 1 - 2 * odd_x), (xb_ref, 2 * odd_x - 1)):
                for k, (c, d) in enumerate(face_x):
                    put(
                        mirrored(c, -sign, 1),
                        pl.ds(row(beyond(cells_x, sign, d), 0), cells_y),
                        ref[k],
                    )

    for odd_y in (0, 1):

        @pl.when(odd_ref[1] == odd_y)
        def _():
            for ref, sign in ((ya_ref, 1 - 2 * odd_y), (yb_ref, 2 * odd_y - 1)):
                for k, (c, d) in enumerate(face_y):
                    put(
                        mirrored(c, 1, -sign),
                        pl.ds(row(0, beyond(cells_y, sign, d)), cells_x, stride=pitch),
                        ref[k],
                    )

    for odd_x in (0, 1):
        for odd_y in (0, 1):

            @pl.when((odd_ref[0] == odd_x) & (odd_ref[1] == odd_y))
            def _():
                to_a, to_b = 1 - 2 * odd_x, 2 * odd_x - 1
                pair, far = 1 - 2 * odd_y, 2 * odd_y - 1
                for ref, sign_x, sign_y in (
                    (cab_ref, to_a, far),
                    (cbb_ref, to_b, far),
                    (cya_ref.at[0], to_a, pair),
                    (cya_ref.at[1], to_b, pair),
                ):
                    for k, (c, dx, dy) in enumerate(corner):
                        put(
                            mirrored(c, -sign_x, -sign_y),
                            pl.ds(row(beyond(cells_x, sign_x, dx), beyond(cells_y, sign_y, dy)), 1),
                            ref[pl.ds(k, 1), :],
                        )

    lane = lax.broadcasted_iota(jnp.int32, (8, depth), 1)

    def arriving(ref, c, start, size):
        cx, cy, _ = all_velocity[c]
        return ref[c, pl.ds(start - (cx * pitch + cy), size), :]

    def advance(source, target, width):
        first = row(-width, -width)
        chunks = -(-(row(cells_x - 1 + width, cells_y - 1 + width) + 1 - first) // 8)

        def chunk(k, carry):
            start = first + 8 * k
            values = [arriving(source, c, start, 8) for c in range(COUNT)]
            values = collide(values[:FLOW], values[FLOW:], kinds_ref[pl.ds(start, 8), :])

            def store(c, value):
                target[c, pl.ds(start, 8), :] = value

            store_outgoing(values, lane, store)
            return carry

        lax.fori_loop(0, chunks, chunk, 0)

    source, target = one_ref, two_ref
    for width in range(HALO - 1, 0, -1):
        advance(source, target, width)
        source, target = target, source

    def plane(x, carry):
        start = row(0, 0) + x * pitch
        values = [arriving(source, c, start, cells_y) for c in range(COUNT)]
        total = functools.reduce(jnp.add, values[:FLOW])
        density_ref[x] = total
        for axis in range(3):
            summed = None
            for c in range(FLOW):
                part = all_velocity[c][axis]
                if part == 0:
                    continue
                if summed is None:
                    summed = values[c] if part > 0 else -values[c]
                else:
                    summed = summed + values[c] if part > 0 else summed - values[c]
            momentum_ref[axis, x] = summed
        concentration_ref[x] = functools.reduce(jnp.add, values[FLOW:])
        return carry

    lax.fori_loop(0, cells_x, plane, 0)


def near(i, count):
    return i ^ 1


def across(i, count):
    return (i + 1) % count if i % 2 else (i - 1) % count


def swapped(block, count_x, count_y, move_x, move_y):
    pairs = []
    for i in range(count_x):
        for j in range(count_y):
            to_x = move_x(i, count_x) if move_x else i
            to_y = move_y(j, count_y) if move_y else j
            pairs.append((i * count_y + j, to_x * count_y + to_y))
    return lax.ppermute(block, ("gx", "gy"), pairs)


def solution(mesh):
    count_x, count_y = mesh.shape["gx"], mesh.shape["gy"]
    assert count_x % 2 == 0 and count_y % 2 == 0

    def local(flow, solute, kind):
        _, cells_x, cells_y, depth = flow.shape
        f32 = jnp.float32
        shape = lambda *dims: jax.ShapeDtypeStruct(dims, f32)
        smem = pl.BlockSpec(memory_space=pltpu.SMEM)
        vmem = pl.BlockSpec(memory_space=pltpu.VMEM)
        params = pltpu.CompilerParams(vmem_limit_bytes=40 * 1024 * 1024)
        odd = jnp.stack([lax.axis_index("gx") % 2, lax.axis_index("gy") % 2]).astype(jnp.int32)
        rows = cells_x * cells_y
        post, kindf, xa, xb, ya, yb, cab, cbb = pl.pallas_call(
            functools.partial(first_kernel, cells_x, cells_y),
            out_shape=[
                shape(COUNT, rows, depth),
                shape(rows, depth),
                shape(len(face_x), cells_y, depth),
                shape(len(face_x), cells_y, depth),
                shape(len(face_y), cells_x, depth),
                shape(len(face_y), cells_x, depth),
                shape(CORNER_ROWS, depth),
                shape(CORNER_ROWS, depth),
            ],
            in_specs=[smem, vmem, vmem, vmem],
            out_specs=[vmem] * 8,
            compiler_params=params,
        )(odd, flow, solute, kind)
        move = functools.partial(swapped, count_x=count_x, count_y=count_y)
        xb = move(xb, move_x=across, move_y=None)
        yb = move(yb, move_x=None, move_y=across)
        xa = move(xa, move_x=near, move_y=None)
        cbb = move(cbb, move_x=across, move_y=across)
        cab = move(cab, move_x=near, move_y=across)
        ya = move(ya, move_x=None, move_y=near)
        cya = pl.pallas_call(
            functools.partial(forward_kernel, cells_y),
            out_shape=shape(2, CORNER_ROWS, depth),
            in_specs=[smem, vmem, vmem],
            out_specs=vmem,
            compiler_params=params,
        )(odd, xa, xb)
        cya = move(cya, move_x=None, move_y=near)
        pitch = cells_y + 2 * HALO
        extended = -(-((cells_x + 2 * HALO) * pitch + 16) // 8) * 8
        return pl.pallas_call(
            functools.partial(last_kernel, cells_x, cells_y),
            out_shape=[
                shape(cells_x, cells_y, depth),
                shape(3, cells_x, cells_y, depth),
                shape(cells_x, cells_y, depth),
            ],
            in_specs=[smem] + [vmem] * 9,
            out_specs=[vmem] * 3,
            scratch_shapes=[
                pltpu.VMEM((COUNT, extended, depth), f32),
                pltpu.VMEM((COUNT, extended, depth), f32),
                pltpu.VMEM((extended, depth), f32),
            ],
            compiler_params=params,
        )(odd, post, kindf, xa, xb, ya, yb, cab, cbb, cya)

    placed = (P(None, "gx", "gy", None), P(None, "gx", "gy", None), P("gx", "gy", None))
    return jax.shard_map(
        lambda *args: tuple(local(*args)),
        mesh=mesh,
        in_specs=placed,
        out_specs=(P("gx", "gy", None), P(None, "gx", "gy", None), P("gx", "gy", None)),
        check_vma=False,
    )
```

time: 54 us -> 42.3 us (0.78)
  other arithmetic: 13 us -> 0.08 us
  Pallas kernels: 0 us -> 11.8 us
  waiting for transfers between devices: 24.8 us -> 13.3 us
  local copies, waits for them, and re-layouts: 1.94 us -> 3.15 us
    pallas_call x0 -> x3, Pallas kernels: none -> 11.8 us  [the longest x1 8.65 us: local(): pl.pallas_call(functools.partial(last_kernel, cells_x, cells_y), out_shap...]
    ppermute x12 -> x7, waiting for transfers between devices: 24.8 us -> 13.3 us  [swapped(): return lax.ppermute(block, ('gx', 'gy'), pairs)]
    unnamed x55 -> x0, other arithmetic: 4.5 us -> none
    reduce_sum x4 -> x0, other arithmetic: 4.1 us -> none  [the longest x2 2.26 us: moments(): density = jnp.sum(flow, axis=0)]
    unnamed x6, local copies, waits for them, and re-layouts: 0.59 us -> 3.15 us
    another operation x10 -> x1, other arithmetic: 1.43 us -> 0.08 us  [local(): jnp.stack([lax.axis_index('gx') % 2, lax.axis_index('gy') % 2])]
    slice x18 -> x0, local copies, waits for them, and re-layouts: 1.34 us -> none  [the longest x12 0.95 us: depth_shift(): section[:, :, 1:]]
    select_n x6 -> x0, other arithmetic: 1.21 us -> none  [the longest x3 0.61 us: collide(): result = jnp.where(is_outlet, jnp.zeros_like(result), result)]
  transfers between devices with their start and end apart: 12 -> 7, of which waited for: 9 -> 4; matrix products, arithmetic and copies ran while one was open for 3% -> 0% of each run, Pallas kernels for 0% -> 1%
where the time goes in v1:
time: 42.3 us; the launch traced here: 42 us
  waiting for transfers between devices  13.3 us (31%)
  starting transfers between devices  13 us (31%)
  Pallas kernels  11.8 us (28%)
  local copies, waits for them, and re-layouts  3.15 us (7%)
  between operations  0.69 us (2%)
    ppermute x7, waiting for transfers between devices, swapped(): return lax.ppermute(block, ('gx', 'gy'), pairs)  13.3 us
    ppermute x7, starting transfers between devices, swapped(): return lax.ppermute(block, ('gx', 'gy'), pairs)  13 us
    pallas_call x1, Pallas kernels, local(): pl.pallas_call(functools.partial(last_kernel, cells_x, cells_y), out_shap...  8.65 us
    unnamed x6, local copies, waits for them, and re-layouts  3.15 us
    pallas_call x1, Pallas kernels, local(): pl.pallas_call(functools.partial(first_kernel, cells_x, cells_y), out_sha...  2.55 us
  transfers between devices with their start and end apart: 7, of which 4 were waited for; matrix products, arithmetic and copies ran while one was open for 0% of the time, Pallas kernels for 1%

profile of v1, /device:TPU:0, one launch (start us, length us, event | category | flops | bytes accessed | tf_op | source)
XLA Modules:
  0.0 42.0 jit_solution(4088499906723134781)
XLA Ops:
  0.6 0.1 pad_add_fusion.odd_ref
  0.7 0.0 copy-start
  0.7 1.3 %copy-done = f32[19,16,8,128]{3,2,1,0:T(8,128)S(1)} copy-done((f32[19,16,8,128]{3,2,1,0:T(8,128)S(1)}, f32[19,16,8,128]{3,2,1,0:T(8,128)}, u32[]{:S(2)}) %copy-start) | copy-done | bytes 1245208
  2.0 0.0 copy-start.1
  2.0 1.0 %copy-done.1 = f32[7,16,8,128]{3,2,1,0:T(8,128)S(1)} copy-done((f32[7,16,8,128]{3,2,1,0:T(8,128)S(1)}, f32[7,16,8,128]{3,2,1,0:T(8,128)}, u32[]{:S(2)}) %copy-start.1) | copy-done | bytes 458776
  3.0 0.0 copy-start.2
  3.0 0.8 %copy-done.2 = s32[16,8,128]{2,1,0:T(8,128)S(1)} copy-done((s32[16,8,128]{2,1,0:T(8,128)S(1)}, s32[16,8,128]{2,1,0:T(8,128)}, u32[]{:S(2)}) %copy-start.2) | copy-done | bytes 65560
  3.9 2.6 %shard_map.58 = (f32[26,128,128]{2,1,0:T(8,128)S(1)}, f32[128,128]{1,0:T(8,128)S(1)}, f32[54,8,128]{2,1,0:T(8,128)S(1)}, f32[54,8,128]{2,1,0:T(8,128)S(1)}, f32[...) custom-call(s32[2]{0:T(128)S(1)} %pad_add_fusion.odd_ref, ...), custom_call_target="tpu_custom_call" | custom-call | tf_op jit(solution)/shard_map/pallas_call | solution.py:366
  6.4 0.5 %collective-permute-start.2 = (f32[54,16,128]{2,1,0:T(8,128)S(1)}, f32[54,16,128]{2,1,0:T(8,128)S(1)}, u32[]{:S(2)}, u32[]{:S(2)}) collective-permute-start(f32[54,16,128]{2,1,0:T(8,128)S(1)} %get-tuple-element.15), channel_id=1, source_target_pairs={{0,1},{1,0},{2,3},{3,2},{4,5},{5,4},{6,7},{7,6},{8,9},{9,8},{10,11... | collective-permute-start | bytes 1327112 | tf_op jit(solution)/shard_map/ppermute | solution.py:350
  7.0 3.6 %collective-permute-start.3 = (f32[54,16,128]{2,1,0:T(8,128)S(1)}, f32[54,16,128]{2,1,0:T(8,128)S(1)}, u32[]{:S(2)}, u32[]{:S(2)}) collective-permute-start(f32[54,16,128]{2,1,0:T(8,128)S(1)} %get-tuple-element.16), channel_id=1, source_target_pairs={{0,7},{1,2},{2,1},{3,4},{4,3},{5,6},{6,5},{7,0},{8,15},{9,10},{10,... | collective-permute-start | bytes 1327112 | tf_op jit(solution)/shard_map/ppermute | solution.py:350
  10.5 1.6 %collective-permute-start = (f32[54,8,128]{2,1,0:T(8,128)S(1)}, f32[54,8,128]{2,1,0:T(8,128)S(1)}, u32[]{:S(2)}, u32[]{:S(2)}) collective-permute-start(f32[54,8,128]{2,1,0:T(8,128)S(1)} %get-tuple-element.13), channel_id=1, source_target_pairs={{0,8},{1,9},{2,10},{3,11},{4,12},{5,13},{6,14},{7,15},{8,0},{9,1},... | collective-permute-start | bytes 663560 | tf_op jit(solution)/shard_map/ppermute | solution.py:350
  12.1 2.5 %collective-permute-start.1 = (f32[54,8,128]{2,1,0:T(8,128)S(1)}, f32[54,8,128]{2,1,0:T(8,128)S(1)}, u32[]{:S(2)}, u32[]{:S(2)}) collective-permute-start(f32[54,8,128]{2,1,0:T(8,128)S(1)} %get-tuple-element.14), channel_id=1, source_target_pairs={{0,24},{1,25},{2,26},{3,27},{4,28},{5,29},{6,30},{7,31},{8,16},{9,... | collective-permute-start | bytes 663560 | tf_op jit(solution)/shard_map/ppermute | solution.py:350
  14.6 3.4 %collective-permute-done.xa_ref = f32[54,8,128]{2,1,0:T(8,128)S(1)} collective-permute-done((f32[54,8,128]{2,1,0:T(8,128)S(1)}, f32[54,8,128]{2,1,0:T(8,128)S(1)}, u32[]{:S(2)}, u32[]{:S(2)}) %collective-permute-start) | collective-permute-done | bytes 221216 | tf_op jit(solution)/shard_map/ppermute | solution.py:350
  18.0 5.9 %collective-permute-done.1.xb_ref = f32[54,8,128]{2,1,0:T(8,128)S(1)} collective-permute-done((f32[54,8,128]{2,1,0:T(8,128)S(1)}, f32[54,8,128]{2,1,0:T(8,128)S(1)}, u32[]{:S(2)}, u32[]{:S(2)}) %collective-permute-start.1) | collective-permute-done | bytes 221216 | tf_op jit(solution)/shard_map/ppermute | solution.py:350
  23.8 0.6 %shard_map.59 = f32[2,112,128]{2,1,0:T(8,128)S(1)} custom-call(s32[2]{0:T(128)S(1)} %pad_add_fusion.odd_ref, f32[54,8,128]{2,1,0:T(8,128)S(1)} %collective-permute-done.xa_ref, f32[54,8,128]{2,1,0:T(8,128)S(1)} %collective-permute-done.1.xb_ref), custom_call_target="tpu_custom_call" | custom-call | tf_op jit(solution)/shard_map/pallas_call | solution.py:389
  24.5 0.1 collective-permute-start.6
  24.6 1.5 %collective-permute-start.4 = (f32[112,128]{1,0:T(8,128)S(1)}, f32[112,128]{1,0:T(8,128)S(1)}, u32[]{:S(2)}, u32[]{:S(2)}) collective-permute-start(f32[112,128]{1,0:T(8,128)S(1)} %get-tuple-element.17), channel_id=1, source_target_pairs={{0,15},{1,10},{2,9},{3,12},{4,11},{5,14},{6,13},{7,8},{8,7},{9,2},... | collective-permute-start | bytes 172040 | tf_op jit(solution)/shard_map/ppermute | solution.py:350
  26.1 3.3 %collective-permute-start.5 = (f32[112,128]{1,0:T(8,128)S(1)}, f32[112,128]{1,0:T(8,128)S(1)}, u32[]{:S(2)}, u32[]{:S(2)}) collective-permute-start(f32[112,128]{1,0:T(8,128)S(1)} %get-tuple-element.18), channel_id=1, source_target_pairs={{0,31},{1,26},{2,25},{3,28},{4,27},{5,30},{6,29},{7,24},{8,23},{9,... | collective-permute-start | bytes 172040 | tf_op jit(solution)/shard_map/ppermute | solution.py:350
  29.4 0.7 %collective-permute-done.4.cab_ref = f32[112,128]{1,0:T(8,128)S(1)} collective-permute-done((f32[112,128]{1,0:T(8,128)S(1)}, f32[112,128]{1,0:T(8,128)S(1)}, u32[]{:S(2)}, u32[]{:S(2)}) %collective-permute-start.4) | collective-permute-done | bytes 57376 | tf_op jit(solution)/shard_map/ppermute | solution.py:350
  30.0 3.4 %collective-permute-done.5.cbb_ref = f32[112,128]{1,0:T(8,128)S(1)} collective-permute-done((f32[112,128]{1,0:T(8,128)S(1)}, f32[112,128]{1,0:T(8,128)S(1)}, u32[]{:S(2)}, u32[]{:S(2)}) %collective-permute-start.5) | collective-permute-done | bytes 57376 | tf_op jit(solution)/shard_map/ppermute | solution.py:350
  33.4 0.0 collective-permute-done.6.cya_ref
  33.4 0.0 collective-permute-done.2.ya_ref
  33.4 0.0 collective-permute-done.3.yb_ref
  33.4 8.7 %shard_map.60 = (f32[16,8,128]{2,1,0:T(8,128)}, f32[3,16,8,128]{3,2,1,0:T(8,128)}, f32[16,8,128]{2,1,0:T(8,128)}) custom-call(s32[2]{0:T(128)S(1)} %pad_add_fusion.odd_ref, f32[26,128,128]{2,1,0:T(8,128)S(1)} %get-tuple-element.11.post_ref, f32[128,128]{1,0:T(8,128)S(1)} %get-tuple-element.12.kindf_ref, f32[54,8,128]{2,1,0:T(8,128)S(1)} %collective-permute-done.xa_ref, ...), custom_call_target="tpu_custom_call" | custom-call | tf_op jit(solution)/shard_map/pallas_call | solution.py:399
Async XLA Ops:
  0.7 1.3 %copy-start = (f32[19,16,8,128]{3,2,1,0:T(8,128)S(1)}, f32[19,16,8,128]{3,2,1,0:T(8,128)}, u32[]{:S(2)}) copy-start(f32[19,16,8,128]{3,2,1,0:T(8,128)} %flow_ref.1) | copy-start | bytes 3735556
  2.0 1.0 %copy-start.1 = (f32[7,16,8,128]{3,2,1,0:T(8,128)S(1)}, f32[7,16,8,128]{3,2,1,0:T(8,128)}, u32[]{:S(2)}) copy-start(f32[7,16,8,128]{3,2,1,0:T(8,128)} %solute_ref.1) | copy-start | bytes 1376260
  3.0 0.8 %copy-start.2 = (s32[16,8,128]{2,1,0:T(8,128)S(1)}, s32[16,8,128]{2,1,0:T(8,128)}, u32[]{:S(2)}) copy-start(s32[16,8,128]{2,1,0:T(8,128)} %kind_ref.1) | copy-start | bytes 196612
  6.4 26.9 %collective-permute-start.2 = (f32[54,16,128]{2,1,0:T(8,128)S(1)}, f32[54,16,128]{2,1,0:T(8,128)S(1)}, u32[]{:S(2)}, u32[]{:S(2)}) collective-permute-start(f32[54,16,128]{2,1,0:T(8,128)S(1)} %get-tuple-element.15), channel_id=1, source_target_pairs={{0,1},{1,0},{2,3},{3,2},{4,5},{5,4},{6,7},{7,6},{8,9},{9,8},{10,11... | collective-permute-start | bytes 1327112 | tf_op jit(solution)/shard_map/ppermute | solution.py:350
  7.0 26.4 %collective-permute-start.3 = (f32[54,16,128]{2,1,0:T(8,128)S(1)}, f32[54,16,128]{2,1,0:T(8,128)S(1)}, u32[]{:S(2)}, u32[]{:S(2)}) collective-permute-start(f32[54,16,128]{2,1,0:T(8,128)S(1)} %get-tuple-element.16), channel_id=1, source_target_pairs={{0,7},{1,2},{2,1},{3,4},{4,3},{5,6},{6,5},{7,0},{8,15},{9,10},{10,... | collective-permute-start | bytes 1327112 | tf_op jit(solution)/shard_map/ppermute | solution.py:350
  10.5 7.5 %collective-permute-start = (f32[54,8,128]{2,1,0:T(8,128)S(1)}, f32[54,8,128]{2,1,0:T(8,128)S(1)}, u32[]{:S(2)}, u32[]{:S(2)}) collective-permute-start(f32[54,8,128]{2,1,0:T(8,128)S(1)} %get-tuple-element.13), channel_id=1, source_target_pairs={{0,8},{1,9},{2,10},{3,11},{4,12},{5,13},{6,14},{7,15},{8,0},{9,1},... | collective-permute-start | bytes 663560 | tf_op jit(solution)/shard_map/ppermute | solution.py:350
  12.1 11.8 %collective-permute-start.1 = (f32[54,8,128]{2,1,0:T(8,128)S(1)}, f32[54,8,128]{2,1,0:T(8,128)S(1)}, u32[]{:S(2)}, u32[]{:S(2)}) collective-permute-start(f32[54,8,128]{2,1,0:T(8,128)S(1)} %get-tuple-element.14), channel_id=1, source_target_pairs={{0,24},{1,25},{2,26},{3,27},{4,28},{5,29},{6,30},{7,31},{8,16},{9,... | collective-permute-start | bytes 663560 | tf_op jit(solution)/shard_map/ppermute | solution.py:350
  24.5 8.9 %collective-permute-start.6 = (f32[2,112,128]{2,1,0:T(8,128)S(1)}, f32[2,112,128]{2,1,0:T(8,128)S(1)}, u32[]{:S(2)}, u32[]{:S(2)}) collective-permute-start(f32[2,112,128]{2,1,0:T(8,128)S(1)} %shard_map.59), channel_id=1, source_target_pairs={{0,1},{1,0},{2,3},{3,2},{4,5},{5,4},{6,7},{7,6},{8,9},{9,8},{10,11... | collective-permute-start | bytes 344072 | tf_op jit(solution)/shard_map/ppermute | solution.py:350
  24.6 5.5 %collective-permute-start.4 = (f32[112,128]{1,0:T(8,128)S(1)}, f32[112,128]{1,0:T(8,128)S(1)}, u32[]{:S(2)}, u32[]{:S(2)}) collective-permute-start(f32[112,128]{1,0:T(8,128)S(1)} %get-tuple-element.17), channel_id=1, source_target_pairs={{0,15},{1,10},{2,9},{3,12},{4,11},{5,14},{6,13},{7,8},{8,7},{9,2},... | collective-permute-start | bytes 172040 | tf_op jit(solution)/shard_map/ppermute | solution.py:350
  26.1 7.3 %collective-permute-start.5 = (f32[112,128]{1,0:T(8,128)S(1)}, f32[112,128]{1,0:T(8,128)S(1)}, u32[]{:S(2)}, u32[]{:S(2)}) collective-permute-start(f32[112,128]{1,0:T(8,128)S(1)} %get-tuple-element.18), channel_id=1, source_target_pairs={{0,31},{1,26},{2,25},{3,28},{4,27},{5,30},{6,29},{7,24},{8,23},{9,... | collective-permute-start | bytes 172040 | tf_op jit(solution)/shard_map/ppermute | solution.py:350

commit v2 on v1

v2 whole, which is shorter than its diff:
```python
import functools
import math

import jax
import jax.numpy as jnp
from jax import lax
from jax.experimental import pallas as pl
from jax.experimental.pallas import tpu as pltpu
from jax.sharding import PartitionSpec as P

STEPS = 3
HALO = STEPS

flow_velocity = [
    (0, 0, 0),
    (1, 0, 0),
    (-1, 0, 0),
    (0, 1, 0),
    (0, -1, 0),
    (0, 0, 1),
    (0, 0, -1),
    (1, 1, 0),
    (-1, -1, 0),
    (1, -1, 0),
    (-1, 1, 0),
    (1, 0, 1),
    (-1, 0, -1),
    (1, 0, -1),
    (-1, 0, 1),
    (0, 1, 1),
    (0, -1, -1),
    (0, 1, -1),
    (0, -1, 1),
]
FLOW = len(flow_velocity)
all_velocity = flow_velocity + flow_velocity[:7]
COUNT = len(all_velocity)
KIND = COUNT
flow_plus = 1.25
flow_minus = 1.0 / 1.125
solute_plus = 1.0 / 1.75
solute_minus = 1.0 / 0.7
inlet_density = 1.05
outlet_density = 0.95
inlet_solute = 1.0


def mirrored(channel, sign_x, sign_y):
    if channel == KIND:
        return KIND
    cx, cy, cz = all_velocity[channel]
    wanted = (cx * sign_x, cy * sign_y, cz)
    if channel < FLOW:
        return flow_velocity.index(wanted)
    return FLOW + flow_velocity[:7].index(wanted)


face_x = [
    (c, d) for d in range(1, HALO + 1) for c in range(COUNT) if d - all_velocity[c][0] <= HALO - 1
] + [(KIND, d) for d in range(1, HALO)]
face_y = [
    (c, d) for d in range(1, HALO + 1) for c in range(COUNT) if d - all_velocity[c][1] <= HALO - 1
] + [(KIND, d) for d in range(1, HALO)]
corner = [
    (c, dx, dy)
    for dx in range(1, HALO + 1)
    for dy in range(1, HALO + 1)
    for c in range(COUNT)
    if dx - all_velocity[c][0] <= HALO - 1 and dy - all_velocity[c][1] <= HALO - 1
] + [(KIND, dx, dy) for dx in range(1, HALO) for dy in range(1, HALO)]
CORNER_ROWS = -(-len(corner) // 8) * 8


def collide(flow, solute, kind):
    pore = kind == 0.0
    solid = kind == 1.0
    inlet = kind == 2.0
    zero = jnp.zeros_like(kind)
    pairs = range(1, FLOW, 2)
    total = {i: flow[i] + flow[i + 1] for i in pairs}
    gap = {i: flow[i] - flow[i + 1] for i in pairs}
    density = (flow[0] + total[1] + total[3]) + (total[5] + total[7] + total[9])
    density = density + ((total[11] + total[13]) + (total[15] + total[17]))
    mom_x = (gap[1] + gap[7]) + (gap[9] + gap[11]) + gap[13]
    mom_y = (gap[3] + gap[7]) + (gap[15] - gap[9]) + gap[17]
    mom_z = (gap[5] + gap[11]) + (gap[15] - gap[13]) - gap[17]
    square = mom_x * mom_x + mom_y * mom_y + mom_z * mom_z
    wall = jnp.where(solid, 0.5, zero)
    even = jnp.where(pore, (1.0 - flow_plus) / 2.0, wall)
    odd = jnp.where(pore, (1.0 - flow_minus) / 2.0, -wall)
    border = jnp.where(inlet, inlet_density, jnp.where(solid, 0.0, outlet_density))
    base = jnp.where(pore, flow_plus * density - (1.5 * flow_plus) * square, border)
    base_18 = base * (1.0 / 18.0)
    base_36 = base * (1.0 / 36.0)
    scale = math.sqrt(4.5 * flow_plus / 36.0)
    held = jnp.where(pore, scale, zero)
    vel = (mom_x * held, mom_y * held, mom_z * held)
    along = 3.0 * flow_minus / (36.0 * scale)
    out = [None] * COUNT
    out[0] = (even + even) * flow[0] + base * (1.0 / 3.0)
    for i in pairs:
        cx, cy, cz = flow_velocity[i]
        parts = [(c, v) for c, v in zip((cx, cy, cz), vel) if c != 0]
        if len(parts) == 1:
            t = parts[0][1]
            a = even * total[i] + (base_18 + 2.0 * (t * t))
            b = odd * gap[i] + (2.0 * along) * t
        else:
            t = parts[0][1] + parts[1][1] if parts[1][0] > 0 else parts[0][1] - parts[1][1]
            a = even * total[i] + (base_36 + t * t)
            b = odd * gap[i] + along * t
        out[i] = a + b
        out[i + 1] = a - b
    total = {i: solute[i] + solute[i + 1] for i in (1, 3, 5)}
    gap = {i: solute[i] - solute[i + 1] for i in (1, 3, 5)}
    concentration = (solute[0] + total[1]) + (total[3] + total[5])
    even = jnp.where(pore, (1.0 - solute_plus) / 2.0, wall)
    odd = jnp.where(pore, (1.0 - solute_minus) / 2.0, -wall)
    border = jnp.where(inlet, inlet_solute, zero)
    base = jnp.where(pore, solute_plus * concentration, border) * 0.125
    drift = concentration * (0.5 * solute_minus / scale)
    out[FLOW] = (even + even) * solute[0] + (base + base)
    for i, t in zip((1, 3, 5), vel):
        a = even * total[i] + base
        b = odd * gap[i] + drift * t
        out[FLOW + i] = a + b
        out[FLOW + i + 1] = a - b
    return out


def depth_shift(section, along_z, lane):
    depth = section.shape[-1]
    if along_z == 1:
        return jnp.where(lane == 0, 0.0, pltpu.roll(section, 1, section.ndim - 1))
    if along_z == -1:
        return jnp.where(lane == depth - 1, 0.0, pltpu.roll(section, depth - 1, section.ndim - 1))
    return section


def store_shifted(values, lane, store):
    for c in range(COUNT):
        store(c, depth_shift(values[c], all_velocity[c][2], lane))


class Extended:
    def __init__(self, cells_x, cells_y):
        self.cells_x, self.cells_y = cells_x, cells_y
        self.pitch = cells_y + 2 * HALO
        self.rows = -(-((cells_x + 2 * HALO) * self.pitch + 16) // 8) * 8

    def row(self, x, y):
        return (x + HALO) * self.pitch + y + HALO


def first_kernel(ext, group, odd_ref, flow_hbm, solute_hbm, kind_hbm, post_ref, kinds_ref,
                 up_ref, down_ref, ya_ref, yb_ref, cup_ref, cdown_ref,
                 flow_ref, solute_ref, kind_ref, sems):
    cells_x, cells_y = ext.cells_x, ext.cells_y
    depth = kind_ref.shape[-1]
    lane = lax.broadcasted_iota(jnp.int32, (cells_y, depth), 1)
    copies = []
    for g in range(cells_x // group):
        planes = pl.ds(g * group, group)
        copies.append([
            pltpu.make_async_copy(kind_hbm.at[planes], kind_ref.at[planes], sems.at[g, 0]),
            pltpu.make_async_copy(flow_hbm.at[:, planes], flow_ref.at[:, planes], sems.at[g, 1]),
            pltpu.make_async_copy(
                solute_hbm.at[:, planes], solute_ref.at[:, planes], sems.at[g, 2]
            ),
        ])
        for copy in copies[-1]:
            copy.start()

    for x in range(cells_x):
        if x % group == 0:
            for copy in copies[x // group]:
                copy.wait()
        kind = kind_ref[x].astype(jnp.float32)
        rows = pl.ds(ext.row(x, 0), cells_y)
        kinds_ref[rows, :] = kind
        values = collide(
            [flow_ref[c, x] for c in range(FLOW)],
            [solute_ref[c, x] for c in range(COUNT - FLOW)],
            kind,
        )

        def store(c, value):
            post_ref[c, rows, :] = value

        store_shifted(values, lane, store)

    def held(c, where):
        return kinds_ref[where, :] if c == KIND else post_ref[c, where, :]

    def at(cells, sign, d):
        return cells - d if sign > 0 else d - 1

    for ref, sign in ((up_ref, 1), (down_ref, -1)):
        for k, (c, d) in enumerate(face_x):
            ref[k] = held(mirrored(c, sign, 1), pl.ds(ext.row(at(cells_x, sign, d), 0), cells_y))

    for odd_y in (0, 1):

        @pl.when(odd_ref[0] == odd_y)
        def _():
            for ref, sign in ((ya_ref, 1 - 2 * odd_y), (yb_ref, 2 * odd_y - 1)):
                for k, (c, d) in enumerate(face_y):
                    where = pl.ds(ext.row(0, at(cells_y, sign, d)), cells_x, stride=ext.pitch)
                    ref[k] = held(mirrored(c, 1, sign), where)
            sign_y = 2 * odd_y - 1
            for ref, sign_x in ((cup_ref, 1), (cdown_ref, -1)):
                for k, (c, dx, dy) in enumerate(corner):
                    row = ext.row(at(cells_x, sign_x, dx), at(cells_y, sign_y, dy))
                    ref[pl.ds(k, 1), :] = held(mirrored(c, sign_x, sign_y), pl.ds(row, 1))


def forward_kernel(cells_y, odd_ref, up_ref, down_ref, out_ref):
    for odd_y in (0, 1):

        @pl.when(odd_ref[0] == odd_y)
        def _():
            sign_y = 1 - 2 * odd_y
            for side, ref in enumerate((up_ref, down_ref)):
                for k, (c, dx, dy) in enumerate(corner):
                    y = cells_y - dy if sign_y > 0 else dy - 1
                    out_ref[side, pl.ds(k, 1), :] = ref[
                        face_x.index((mirrored(c, 1, sign_y), dx)), pl.ds(y, 1), :
                    ]


def beyond(cells, sign, d):
    return cells - 1 + d if sign > 0 else -d


def last_kernel(ext, odd_ref, _, __, up_ref, down_ref, ya_ref, yb_ref, cup_ref, cdown_ref,
                cpair_ref, density_ref, momentum_ref, concentration_ref, one_ref, kinds_ref,
                two_ref):
    cells_x, cells_y, pitch, row = ext.cells_x, ext.cells_y, ext.pitch, ext.row
    depth = one_ref.shape[-1]

    def put(c, where, value):
        if c == KIND:
            kinds_ref[where, :] = value
        else:
            one_ref[c, where, :] = value

    for ref, sign in ((up_ref, -1), (down_ref, 1)):
        for k, (c, d) in enumerate(face_x):
            put(mirrored(c, -sign, 1), pl.ds(row(beyond(cells_x, sign, d), 0), cells_y), ref[k])

    for odd_y in (0, 1):

        @pl.when(odd_ref[0] == odd_y)
        def _():
            for ref, sign in ((ya_ref, 1 - 2 * odd_y), (yb_ref, 2 * odd_y - 1)):
                for k, (c, d) in enumerate(face_y):
                    put(
                        mirrored(c, 1, -sign),
                        pl.ds(row(0, beyond(cells_y, sign, d)), cells_x, stride=pitch),
                        ref[k],
                    )
            pair, far = 1 - 2 * odd_y, 2 * odd_y - 1
            for ref, sign_x, sign_y in (
                (cup_ref, -1, far),
                (cdown_ref, 1, far),
                (cpair_ref.at[0], -1, pair),
                (cpair_ref.at[1], 1, pair),
            ):
                for k, (c, dx, dy) in enumerate(corner):
                    put(
                        mirrored(c, -sign_x, -sign_y),
                        pl.ds(row(beyond(cells_x, sign_x, dx), beyond(cells_y, sign_y, dy)), 1),
                        ref[pl.ds(k, 1), :],
                    )

    lane = lax.broadcasted_iota(jnp.int32, (8, depth), 1)

    def arriving(ref, c, start, size):
        cx, cy, _ = all_velocity[c]
        return ref[c, pl.ds(start - (cx * pitch + cy), size), :]

    def advance(source, target, width):
        first = row(-width, -width)
        for start in range(first, row(cells_x - 1 + width, cells_y - 1 + width) + 1, 8):
            values = [arriving(source, c, start, 8) for c in range(COUNT)]
            values = collide(values[:FLOW], values[FLOW:], kinds_ref[pl.ds(start, 8), :])

            def store(c, value):
                target[c, pl.ds(start, 8), :] = value

            if width > 1:
                store_shifted(values, lane, store)
            else:
                for c in range(COUNT):
                    store(c, values[c])

    source, target = one_ref, two_ref
    for width in range(HALO - 1, 0, -1):
        advance(source, target, width)
        source, target = target, source

    def summed(values, weights):
        total = None
        for along_z in (0, 1, -1):
            part = None
            for c, weight in weights.items():
                if weight == 0 or all_velocity[c][2] != along_z:
                    continue
                if part is None:
                    part = values[c] if weight > 0 else -values[c]
                else:
                    part = part + values[c] if weight > 0 else part - values[c]
            if part is not None:
                part = depth_shift(part, along_z, lane)
                total = part if total is None else total + part
        return total

    flow = range(FLOW)
    for x in range(cells_x):
        values = [arriving(source, c, row(x, 0), cells_y) for c in range(COUNT)]
        density_ref[x] = summed(values, {c: 1 for c in flow})
        for axis in range(3):
            momentum_ref[axis, x] = summed(values, {c: flow_velocity[c][axis] for c in flow})
        concentration_ref[x] = summed(values, {c: 1 for c in range(FLOW, COUNT)})


def higher(i, count):
    return (i + 1) % count


def lower(i, count):
    return (i - 1) % count


def near(i, count):
    return i ^ 1


def across(i, count):
    return (i + 1) % count if i % 2 else (i - 1) % count


def swapped(block, count_x, count_y, move_x, move_y):
    pairs = []
    for i in range(count_x):
        for j in range(count_y):
            to_x = move_x(i, count_x) if move_x else i
            to_y = move_y(j, count_y) if move_y else j
            pairs.append((i * count_y + j, to_x * count_y + to_y))
    return lax.ppermute(block, ("gx", "gy"), pairs)


def solution(mesh):
    count_x, count_y = mesh.shape["gx"], mesh.shape["gy"]
    assert count_y % 2 == 0

    def local(flow, solute, kind):
        _, cells_x, cells_y, depth = flow.shape
        f32 = jnp.float32
        shape = lambda *dims: jax.ShapeDtypeStruct(dims, f32)
        smem = pl.BlockSpec(memory_space=pltpu.SMEM)
        vmem = pl.BlockSpec(memory_space=pltpu.VMEM)
        hbm = pl.BlockSpec(memory_space=pltpu.HBM)
        params = pltpu.CompilerParams(vmem_limit_bytes=40 * 1024 * 1024)
        odd = jnp.reshape(lax.axis_index("gy") % 2, (1,)).astype(jnp.int32)
        ext = Extended(cells_x, cells_y)
        group = math.gcd(cells_x, 4)
        flow, solute, kind = (
            pltpu.with_memory_space_constraint(a, pltpu.HBM) for a in (flow, solute, kind)
        )
        post, kinds, up, down, ya, yb, cup, cdown = pl.pallas_call(
            functools.partial(first_kernel, ext, group),
            out_shape=[
                shape(COUNT, ext.rows, depth),
                shape(ext.rows, depth),
                shape(len(face_x), cells_y, depth),
                shape(len(face_x), cells_y, depth),
                shape(len(face_y), cells_x, depth),
                shape(len(face_y), cells_x, depth),
                shape(CORNER_ROWS, depth),
                shape(CORNER_ROWS, depth),
            ],
            in_specs=[smem, hbm, hbm, hbm],
            out_specs=[vmem] * 8,
            scratch_shapes=[
                pltpu.VMEM(flow.shape, f32),
                pltpu.VMEM(solute.shape, f32),
                pltpu.VMEM(kind.shape, kind.dtype),
                pltpu.SemaphoreType.DMA((cells_x // group, 3)),
            ],
            compiler_params=params,
        )(odd, flow, solute, kind)
        move = functools.partial(swapped, count_x=count_x, count_y=count_y)
        up = move(up, move_x=higher, move_y=None)
        down = move(down, move_x=lower, move_y=None)
        yb = move(yb, move_x=None, move_y=across)
        cup = move(cup, move_x=higher, move_y=across)
        cdown = move(cdown, move_x=lower, move_y=across)
        ya, up, down, yb, cup, cdown = lax.optimization_barrier((ya, up, down, yb, cup, cdown))
        ya = move(ya, move_x=None, move_y=near)
        cpair = pl.pallas_call(
            functools.partial(forward_kernel, cells_y),
            out_shape=shape(2, CORNER_ROWS, depth),
            in_specs=[smem, vmem, vmem],
            out_specs=vmem,
            compiler_params=params,
        )(odd, up, down)
        cpair = move(cpair, move_x=None, move_y=near)
        density, momentum, concentration, _, _ = pl.pallas_call(
            functools.partial(last_kernel, ext),
            out_shape=[
                shape(cells_x, cells_y, depth),
                shape(3, cells_x, cells_y, depth),
                shape(cells_x, cells_y, depth),
                shape(COUNT, ext.rows, depth),
                shape(ext.rows, depth),
            ],
            in_specs=[smem] + [vmem] * 9,
            out_specs=[vmem] * 5,
            scratch_shapes=[pltpu.VMEM((COUNT, ext.rows, depth), f32)],
            input_output_aliases={1: 3, 2: 4},
            compiler_params=params,
        )(odd, post, kinds, up, down, ya, yb, cup, cdown, cpair)
        return density, momentum, concentration

    placed = (P(None, "gx", "gy", None), P(None, "gx", "gy", None), P("gx", "gy", None))
    return jax.shard_map(
        local,
        mesh=mesh,
        in_specs=placed,
        out_specs=(P("gx", "gy", None), P(None, "gx", "gy", None), P("gx", "gy", None)),
        check_vma=False,
    )
```

time: 42.3 us -> 27.3 us (0.65)
  Pallas kernels: 11.8 us -> 5.4 us
  waiting for transfers between devices: 13.3 us -> 7.72 us
  local copies, waits for them, and re-layouts: 3.15 us -> 0 us
    pallas_call x2, Pallas kernels: 11.2 us -> 5.32 us  [the longest x1 3.32 us: local(): pl.pallas_call(functools.partial(last_kernel, ext), out_shape=[shape(cell...]
    ppermute x7, waiting for transfers between devices: 13.3 us -> 7.72 us  [swapped(): return lax.ppermute(block, ('gx', 'gy'), pairs)]
    unnamed x6 -> x0, local copies, waits for them, and re-layouts: 3.15 us -> none
    pallas_call x1, Pallas kernels: 0.63 us -> 0.08 us  [local(): pl.pallas_call(functools.partial(forward_kernel, cells_y), out_shape=shap...]
  transfers between devices with their start and end apart: 7 -> 7, of which waited for: 4 -> 2; matrix products, arithmetic and copies ran while one was open for 0% -> 0% of each run, Pallas kernels for 1% -> 0%
where the time goes in v2:
time: 27.3 us; the launch traced here: 27 us
  starting transfers between devices  13.2 us (48%)
  waiting for transfers between devices  7.72 us (28%)
  Pallas kernels  5.4 us (20%)
  between operations  0.67 us (2%)
    ppermute x7, starting transfers between devices, swapped(): return lax.ppermute(block, ('gx', 'gy'), pairs)  13.2 us
    ppermute x7, waiting for transfers between devices, swapped(): return lax.ppermute(block, ('gx', 'gy'), pairs)  7.72 us
    pallas_call x1, Pallas kernels, local(): pl.pallas_call(functools.partial(last_kernel, ext), out_shape=[shape(cell...  3.32 us
    pallas_call x1, Pallas kernels, local(): pl.pallas_call(functools.partial(first_kernel, ext, group), out_shape=[sh...  2 us
  transfers between devices with their start and end apart: 7, of which 2 were waited for; matrix products, arithmetic and copies ran while one was open for 0% of the time, Pallas kernels for 0%

profile of v2, /device:TPU:0, one launch (start us, length us, event | category | flops | bytes accessed | tf_op | source)
XLA Modules:
  0.0 27.0 jit_solution(6543066545749629412)
XLA Ops:
  0.6 2.0 %shard_map.58 = (f32[26,328,128]{2,1,0:T(8,128)S(1)}, f32[328,128]{1,0:T(8,128)S(1)}, f32[54,8,128]{2,1,0:T(8,128)S(1)}, f32[54,8,128]{2,1,0:T(8,128)S(1)}, f32[...) custom-call(s32[1]{0:T(128)} %bitcast.odd_ref, ...), custom_call_target="tpu_custom_call" | custom-call | tf_op jit(solution)/shard_map/pallas_call | solution.py:371
  2.6 3.4 %collective-permute-start.2 = (f32[54,16,128]{2,1,0:T(8,128)S(1)}, f32[54,16,128]{2,1,0:T(8,128)S(1)}, u32[]{:S(2)}, u32[]{:S(2)}) collective-permute-start(f32[54,16,128]{2,1,0:T(8,128)S(1)} %get-tuple-element.25), channel_id=1, source_target_pairs={{0,7},{1,2},{2,1},{3,4},{4,3},{5,6},{6,5},{7,0},{8,15},{9,10},{10,... | collective-permute-start | bytes 1327112 | tf_op jit(solution)/shard_map/ppermute | solution.py:350
  6.1 1.6 %collective-permute-start = (f32[54,8,128]{2,1,0:T(8,128)S(1)}, f32[54,8,128]{2,1,0:T(8,128)S(1)}, u32[]{:S(2)}, u32[]{:S(2)}) collective-permute-start(f32[54,8,128]{2,1,0:T(8,128)S(1)} %get-tuple-element.23), channel_id=1, source_target_pairs={{0,8},{1,9},{2,10},{3,11},{4,12},{5,13},{6,14},{7,15},{8,16},{9,17... | collective-permute-start | bytes 663560 | tf_op jit(solution)/shard_map/ppermute | solution.py:350
  7.7 2.2 %collective-permute-start.1 = (f32[54,8,128]{2,1,0:T(8,128)S(1)}, f32[54,8,128]{2,1,0:T(8,128)S(1)}, u32[]{:S(2)}, u32[]{:S(2)}) collective-permute-start(f32[54,8,128]{2,1,0:T(8,128)S(1)} %get-tuple-element.24), channel_id=1, source_target_pairs={{0,24},{1,25},{2,26},{3,27},{4,28},{5,29},{6,30},{7,31},{8,0},{9,1... | collective-permute-start | bytes 663560 | tf_op jit(solution)/shard_map/ppermute | solution.py:350
  9.9 0.0 collective-permute-start.3
  9.9 5.3 %collective-permute-start.4 = (f32[112,128]{1,0:T(8,128)S(1)}, f32[112,128]{1,0:T(8,128)S(1)}, u32[]{:S(2)}, u32[]{:S(2)}) collective-permute-start(f32[112,128]{1,0:T(8,128)S(1)} %get-tuple-element.27), channel_id=1, source_target_pairs={{0,31},{1,26},{2,25},{3,28},{4,27},{5,30},{6,29},{7,24},{8,7},{9,2... | collective-permute-start | bytes 172040 | tf_op jit(solution)/shard_map/ppermute | solution.py:350
  15.2 6.4 %collective-permute-done.3.cup_ref = f32[112,128]{1,0:T(8,128)S(1)} collective-permute-done((f32[112,128]{1,0:T(8,128)S(1)}, f32[112,128]{1,0:T(8,128)S(1)}, u32[]{:S(2)}, u32[]{:S(2)}) %collective-permute-start.3) | collective-permute-done | bytes 57376 | tf_op jit(solution)/shard_map/ppermute | solution.py:350
  21.6 0.0 collective-permute-done.4.cdown_ref
  21.7 0.0 collective-permute-done.up_ref
  21.7 0.0 collective-permute-done.1.down_ref
  21.7 0.0 collective-permute-done.2.yb_ref
  21.7 0.2 collective-permute-start.5
  21.9 0.1 shard_map.59
  21.9 0.5 %collective-permute-start.6 = (f32[2,112,128]{2,1,0:T(8,128)S(1)}, f32[2,112,128]{2,1,0:T(8,128)S(1)}, u32[]{:S(2)}, u32[]{:S(2)}) collective-permute-start(f32[2,112,128]{2,1,0:T(8,128)S(1)} %shard_map.59), channel_id=1, source_target_pairs={{0,1},{1,0},{2,3},{3,2},{4,5},{5,4},{6,7},{7,6},{8,9},{9,8},{10,11... | collective-permute-start | bytes 344072 | tf_op jit(solution)/shard_map/ppermute | solution.py:350
  22.4 1.3 %collective-permute-done.6.cpair_ref = f32[2,112,128]{2,1,0:T(8,128)S(1)} collective-permute-done((f32[2,112,128]{2,1,0:T(8,128)S(1)}, f32[2,112,128]{2,1,0:T(8,128)S(1)}, u32[]{:S(2)}, u32[]{:S(2)}) %collective-permute-start.6) | collective-permute-done | bytes 114720 | tf_op jit(solution)/shard_map/ppermute | solution.py:350
  23.7 0.0 collective-permute-done.5.ya_ref
  23.7 3.3 %shard_map.60 = (f32[16,8,128]{2,1,0:T(8,128)}, f32[3,16,8,128]{3,2,1,0:T(8,128)}, f32[16,8,128]{2,1,0:T(8,128)}, f32[26,328,128]{2,1,0:T(8,128)S(1)}, f32[328,128]{1,0:T(8,128)S(1)}) custom-call(s32[1]{0:T(128)} %bitcast.odd_ref, f32[26,328,128]{2,1,0:T(8,128)S(1)} %get-tuple-element.20._, ...), custom_call_target="tpu_custom_call", output_to_operand_aliasing={{3}: (1, {}), {4}: (2, {})} | custom-call | tf_op jit(solution)/shard_map/pallas_call | solution.py:409
Async XLA Ops:
  2.6 19.0 %collective-permute-start.2 = (f32[54,16,128]{2,1,0:T(8,128)S(1)}, f32[54,16,128]{2,1,0:T(8,128)S(1)}, u32[]{:S(2)}, u32[]{:S(2)}) collective-permute-start(f32[54,16,128]{2,1,0:T(8,128)S(1)} %get-tuple-element.25), channel_id=1, source_target_pairs={{0,7},{1,2},{2,1},{3,4},{4,3},{5,6},{6,5},{7,0},{8,15},{9,10},{10,... | collective-permute-start | bytes 1327112 | tf_op jit(solution)/shard_map/ppermute | solution.py:350
  6.1 15.6 %collective-permute-start = (f32[54,8,128]{2,1,0:T(8,128)S(1)}, f32[54,8,128]{2,1,0:T(8,128)S(1)}, u32[]{:S(2)}, u32[]{:S(2)}) collective-permute-start(f32[54,8,128]{2,1,0:T(8,128)S(1)} %get-tuple-element.23), channel_id=1, source_target_pairs={{0,8},{1,9},{2,10},{3,11},{4,12},{5,13},{6,14},{7,15},{8,16},{9,17... | collective-permute-start | bytes 663560 | tf_op jit(solution)/shard_map/ppermute | solution.py:350
  7.7 14.0 %collective-permute-start.1 = (f32[54,8,128]{2,1,0:T(8,128)S(1)}, f32[54,8,128]{2,1,0:T(8,128)S(1)}, u32[]{:S(2)}, u32[]{:S(2)}) collective-permute-start(f32[54,8,128]{2,1,0:T(8,128)S(1)} %get-tuple-element.24), channel_id=1, source_target_pairs={{0,24},{1,25},{2,26},{3,27},{4,28},{5,29},{6,30},{7,31},{8,0},{9,1... | collective-permute-start | bytes 663560 | tf_op jit(solution)/shard_map/ppermute | solution.py:350
  9.9 11.7 %collective-permute-start.3 = (f32[112,128]{1,0:T(8,128)S(1)}, f32[112,128]{1,0:T(8,128)S(1)}, u32[]{:S(2)}, u32[]{:S(2)}) collective-permute-start(f32[112,128]{1,0:T(8,128)S(1)} %get-tuple-element.26), channel_id=1, source_target_pairs={{0,15},{1,10},{2,9},{3,12},{4,11},{5,14},{6,13},{7,8},{8,23},{9,18... | collective-permute-start | bytes 172040 | tf_op jit(solution)/shard_map/ppermute | solution.py:350
  9.9 11.7 %collective-permute-start.4 = (f32[112,128]{1,0:T(8,128)S(1)}, f32[112,128]{1,0:T(8,128)S(1)}, u32[]{:S(2)}, u32[]{:S(2)}) collective-permute-start(f32[112,128]{1,0:T(8,128)S(1)} %get-tuple-element.27), channel_id=1, source_target_pairs={{0,31},{1,26},{2,25},{3,28},{4,27},{5,30},{6,29},{7,24},{8,7},{9,2... | collective-permute-start | bytes 172040 | tf_op jit(solution)/shard_map/ppermute | solution.py:350
  21.7 2.0 %collective-permute-start.5 = (f32[54,16,128]{2,1,0:T(8,128)S(1)}, f32[54,16,128]{2,1,0:T(8,128)S(1)}, u32[]{:S(2)}, u32[]{:S(2)}) collective-permute-start(f32[54,16,128]{2,1,0:T(8,128)S(1)} %get-tuple-element.30), channel_id=1, source_target_pairs={{0,1},{1,0},{2,3},{3,2},{4,5},{5,4},{6,7},{7,6},{8,9},{9,8},{10,11... | collective-permute-start | bytes 1327112 | tf_op jit(solution)/shard_map/ppermute | solution.py:350
  21.9 1.8 %collective-permute-start.6 = (f32[2,112,128]{2,1,0:T(8,128)S(1)}, f32[2,112,128]{2,1,0:T(8,128)S(1)}, u32[]{:S(2)}, u32[]{:S(2)}) collective-permute-start(f32[2,112,128]{2,1,0:T(8,128)S(1)} %shard_map.59), channel_id=1, source_target_pairs={{0,1},{1,0},{2,3},{3,2},{4,5},{5,4},{6,7},{7,6},{8,9},{9,8},{10,11... | collective-permute-start | bytes 344072 | tf_op jit(solution)/shard_map/ppermute | solution.py:350

commit v3 on v2

--- a/solution.py
+++ b/solution.py
@@ -36,6 +36,7 @@
 all_velocity = flow_velocity + flow_velocity[:7]
 COUNT = len(all_velocity)
 KIND = COUNT
+SUMS = {0: range(COUNT + 1, COUNT + 5), 1: range(COUNT + 5, COUNT + 9)}
 flow_plus = 1.25
 flow_minus = 1.0 / 1.125
 solute_plus = 1.0 / 1.75
@@ -46,8 +47,8 @@
 
 
 def mirrored(channel, sign_x, sign_y):
-    if channel == KIND:
-        return KIND
+    if channel >= KIND:
+        return channel
     cx, cy, cz = all_velocity[channel]
     wanted = (cx * sign_x, cy * sign_y, cz)
     if channel < FLOW:
@@ -55,20 +56,35 @@
     return FLOW + flow_velocity[:7].index(wanted)
 
 
-face_x = [
-    (c, d) for d in range(1, HALO + 1) for c in range(COUNT) if d - all_velocity[c][0] <= HALO - 1
-] + [(KIND, d) for d in range(1, HALO)]
-face_y = [
-    (c, d) for d in range(1, HALO + 1) for c in range(COUNT) if d - all_velocity[c][1] <= HALO - 1
-] + [(KIND, d) for d in range(1, HALO)]
-corner = [
-    (c, dx, dy)
-    for dx in range(1, HALO + 1)
-    for dy in range(1, HALO + 1)
-    for c in range(COUNT)
-    if dx - all_velocity[c][0] <= HALO - 1 and dy - all_velocity[c][1] <= HALO - 1
-] + [(KIND, dx, dy) for dx in range(1, HALO) for dy in range(1, HALO)]
-CORNER_ROWS = -(-len(corner) // 8) * 8
+def moving(axis, toward):
+    return [c for c in range(COUNT) if all_velocity[c][axis] == toward]
+
+
+def needed(axis):
+    outer = HALO - 1
+    return (
+        [(c, d) for d in range(1, outer) for c in range(COUNT)]
+        + [(c, d) for d in (outer, HALO) for c in moving(axis, 1)]
+        + [(c, outer) for c in SUMS[axis]]
+        + [(KIND, d) for d in range(1, HALO)]
+    )
+
+
+face_x = needed(0)
+face_y = needed(1)
+ends_x = [c for c in moving(0, 0) if all_velocity[c][1] == 1]
+ends_y = [c for c in moving(1, 0) if all_velocity[c][0] == 1]
+
+
+def reach(channel):
+    return HALO - 1 + (all_velocity[channel][1] if channel < COUNT else 0)
+
+
+corner_start = [sum(reach(c) for c, _ in face_x[:k]) for k in range(len(face_x) + 1)]
+ENDS_START = corner_start[-1]
+CORNER_ROWS = -(-(ENDS_START + len(ends_x)) // 8) * 8
+FACE_X_SUMS = face_x.index((SUMS[0][0], HALO - 1))
+FACE_Y_SUMS = face_y.index((SUMS[1][0], HALO - 1))
 
 
 def collide(flow, solute, kind):
@@ -148,13 +164,19 @@
         self.pitch = cells_y + 2 * HALO
         self.rows = -(-((cells_x + 2 * HALO) * self.pitch + 16) // 8) * 8
 
+        self.face_y_rows = len(face_y) * cells_x + 2 * len(ends_y)
+        self.inner_rows = cells_y - 2 * (HALO - 1)
+
     def row(self, x, y):
         return (x + HALO) * self.pitch + y + HALO
 
+    def inner(self, channel):
+        return HALO - 1 - (all_velocity[channel][1] if channel < COUNT else 0)
+
 
 def first_kernel(ext, group, odd_ref, flow_hbm, solute_hbm, kind_hbm, post_ref, kinds_ref,
                  up_ref, down_ref, ya_ref, yb_ref, cup_ref, cdown_ref,
-                 flow_ref, solute_ref, kind_ref, sems):
+                 flow_ref, solute_ref, kind_ref, sums_ref, sems):
     cells_x, cells_y = ext.cells_x, ext.cells_y
     depth = kind_ref.shape[-1]
     lane = lax.broadcasted_iota(jnp.int32, (cells_y, depth), 1)
@@ -189,89 +211,224 @@
 
         store_shifted(values, lane, store)
 
-    def held(c, where):
-        return kinds_ref[where, :] if c == KIND else post_ref[c, where, :]
+    def sums(axis, where):
+        across = 1 - axis
+        cells = (cells_x, cells_y)[across]
+        place = lax.broadcasted_iota(jnp.int32, (cells, depth), 0)
+        parts = {}
+        for move in (0, 1, -1):
+            total = along = solute = None
+            for c in moving(axis, 0):
+                if all_velocity[c][across] != move:
+                    continue
+                value = post_ref[c, where(-move), :]
+                if c >= FLOW:
+                    solute = value if solute is None else solute + value
+                    continue
+                total = value if total is None else total + value
+                cz = all_velocity[c][2]
+                if cz != 0:
+                    signed = value if cz > 0 else -value
+                    along = signed if along is None else along + signed
+            parts[move] = [total, along, solute]
+            if move != 0:
+                inside = place != (0 if move > 0 else cells - 1)
+                parts[move] = [jnp.where(inside, p, 0.0) for p in parts[move]]
+        total, along, solute = (parts[0][n] + parts[1][n] + parts[-1][n] for n in range(3))
+        for c, value in zip(
+            SUMS[axis], (total - along, parts[1][0] - parts[-1][0], along, solute)
+        ):
+            sums_ref[c - SUMS[0][0], where(0), :] = value
 
     def at(cells, sign, d):
         return cells - d if sign > 0 else d - 1
 
+    def line_x(x):
+        return lambda y: pl.ds(ext.row(x, y), cells_y)
+
+    def line_y(y):
+        return lambda x: pl.ds(ext.row(x, y), cells_x, stride=ext.pitch)
+
+    zero = jnp.zeros((8, depth), jnp.float32)
+    zeros = jnp.zeros((cells_x, depth), jnp.float32)
+    for sign in (1, -1):
+        sums(0, line_x(at(cells_x, sign, HALO - 1)))
+        sums(1, line_y(at(cells_y, sign, HALO - 1)))
+        for c in moving(0, 0):
+            first = ext.row(beyond(cells_x, sign, HALO - 1), -HALO)
+            for start in [*range(0, ext.pitch - 8, 8), ext.pitch - 8]:
+                post_ref[c, pl.ds(first + start, 8), :] = zero
+        for c in moving(1, 0):
+            post_ref[c, line_y(beyond(cells_y, sign, HALO - 1))(0), :] = zeros
+
+    def held(c, where):
+        if c > KIND:
+            return sums_ref[c - SUMS[0][0], where, :]
+        return kinds_ref[where, :] if c == KIND else post_ref[c, where, :]
+
+    for odd_y in (0, 1):
+
+        @pl.when(odd_ref[0] == odd_y)
+        def _():
+            pair = 1 - 2 * odd_y
+            for ref, sign_x in ((cup_ref, 1), (cdown_ref, -1)):
+                for side, sign_y in enumerate((pair, -pair)):
+                    for k, (c, d) in enumerate(face_x):
+                        y = cells_y - reach(c) if sign_y > 0 else 0
+                        where = pl.ds(ext.row(at(cells_x, sign_x, d), y), reach(c))
+                        ref[side, pl.ds(corner_start[k], reach(c)), :] = held(
+                            mirrored(c, sign_x, sign_y), where
+                        )
+                    for k, c in enumerate(ends_x):
+                        row = ext.row(at(cells_x, sign_x, HALO - 1), at(cells_y, sign_y, 1))
+                        ref[side, pl.ds(ENDS_START + k, 1), :] = held(
+                            mirrored(c, 1, sign_y), pl.ds(row, 1)
+                        )
+            for ref, sign in ((ya_ref, pair), (yb_ref, -pair)):
+                for k, (c, d) in enumerate(face_y):
+                    ref[pl.ds(k * cells_x, cells_x), :] = held(
+                        mirrored(c, 1, sign), line_y(at(cells_y, sign, d))(0)
+                    )
+                for side, sign_x in enumerate((1, -1)):
+                    for k, c in enumerate(ends_y):
+                        row = ext.row(at(cells_x, sign_x, 1), at(cells_y, sign, HALO - 1))
+                        to = len(face_y) * cells_x + side * len(ends_y) + k
+                        ref[pl.ds(to, 1), :] = held(mirrored(c, sign_x, 1), pl.ds(row, 1))
+
     for ref, sign in ((up_ref, 1), (down_ref, -1)):
         for k, (c, d) in enumerate(face_x):
-            ref[k] = held(mirrored(c, sign, 1), pl.ds(ext.row(at(cells_x, sign, d), 0), cells_y))
-
-    for odd_y in (0, 1):
-
-        @pl.when(odd_ref[0] == odd_y)
-        def _():
-            for ref, sign in ((ya_ref, 1 - 2 * odd_y), (yb_ref, 2 * odd_y - 1)):
-                for k, (c, d) in enumerate(face_y):
-                    where = pl.ds(ext.row(0, at(cells_y, sign, d)), cells_x, stride=ext.pitch)
-                    ref[k] = held(mirrored(c, 1, sign), where)
-            sign_y = 2 * odd_y - 1
-            for ref, sign_x in ((cup_ref, 1), (cdown_ref, -1)):
-                for k, (c, dx, dy) in enumerate(corner):
-                    row = ext.row(at(cells_x, sign_x, dx), at(cells_y, sign_y, dy))
-                    ref[pl.ds(k, 1), :] = held(mirrored(c, sign_x, sign_y), pl.ds(row, 1))
-
-
-def forward_kernel(cells_y, odd_ref, up_ref, down_ref, out_ref):
-    for odd_y in (0, 1):
-
-        @pl.when(odd_ref[0] == odd_y)
-        def _():
-            sign_y = 1 - 2 * odd_y
-            for side, ref in enumerate((up_ref, down_ref)):
-                for k, (c, dx, dy) in enumerate(corner):
-                    y = cells_y - dy if sign_y > 0 else dy - 1
-                    out_ref[side, pl.ds(k, 1), :] = ref[
-                        face_x.index((mirrored(c, 1, sign_y), dx)), pl.ds(y, 1), :
-                    ]
+            where = pl.ds(ext.row(at(cells_x, sign, d), ext.inner(c)), ext.inner_rows)
+            ref[pl.ds(k * ext.inner_rows, ext.inner_rows), :] = held(mirrored(c, sign, 1), where)
+
+
+def forward_kernel(cup_ref, cdown_ref, pair_ref, far_ref):
+    for side, ref in enumerate((pair_ref, far_ref)):
+        ref[0] = cup_ref[side]
+        ref[1] = cdown_ref[side]
 
 
 def beyond(cells, sign, d):
     return cells - 1 + d if sign > 0 else -d
 
 
-def last_kernel(ext, odd_ref, _, __, up_ref, down_ref, ya_ref, yb_ref, cup_ref, cdown_ref,
-                cpair_ref, density_ref, momentum_ref, concentration_ref, one_ref, kinds_ref,
-                two_ref):
-    cells_x, cells_y, pitch, row = ext.cells_x, ext.cells_y, ext.pitch, ext.row
-    depth = one_ref.shape[-1]
-
+def putter(one_ref, kinds_ref):
     def put(c, where, value):
         if c == KIND:
             kinds_ref[where, :] = value
         else:
             one_ref[c, where, :] = value
 
-    for ref, sign in ((up_ref, -1), (down_ref, 1)):
-        for k, (c, d) in enumerate(face_x):
-            put(mirrored(c, -sign, 1), pl.ds(row(beyond(cells_x, sign, d), 0), cells_y), ref[k])
-
+    return put
+
+
+def put_sums(ext, put, x, y, count, values, carry):
+    total, across, along, solute = values
+    rows = pl.ds(ext.row(x, y), count)
+    moved = across if carry > 0 else -across
+    put(0, rows, total - moved)
+    put(all_velocity.index((0, carry, 0)), pl.ds(ext.row(x, y - carry), count), moved)
+    put(all_velocity.index((0, 0, 1)), rows, along)
+    put(FLOW, rows, solute)
+
+
+def put_corner(ext, put, ref, sign_x, sign_y, origin):
+    for k, (c, d) in enumerate(face_x):
+        x = beyond(ext.cells_x, sign_x, d)
+        y = origin + (ext.cells_y - reach(c) if sign_y > 0 else 0)
+        if c <= KIND:
+            put(
+                mirrored(c, -sign_x, sign_y),
+                pl.ds(ext.row(x, y), reach(c)),
+                ref[pl.ds(corner_start[k], reach(c)), :],
+            )
+        elif k == FACE_X_SUMS:
+            for n in range(reach(c)):
+                values = [ref[pl.ds(corner_start[k + i] + n, 1), :] for i in range(4)]
+                carry = 1 if y + n < 0 or y + n == ext.cells_y - 1 else -1
+                put_sums(ext, put, x, y + n, 1, values, carry)
+    x = beyond(ext.cells_x, sign_x, HALO - 1)
+    y = origin + (ext.cells_y - 1 if sign_y > 0 else 0)
+    for k, c in enumerate(ends_x):
+        put(mirrored(c, 1, sign_y), pl.ds(ext.row(x, y), 1), ref[pl.ds(ENDS_START + k, 1), :])
+
+
+def put_inner(ext, put, ref, sign_x):
+    for k, (c, d) in enumerate(face_x):
+        x, y = beyond(ext.cells_x, sign_x, d), ext.inner(c)
+        rows = [pl.ds((k + i) * ext.inner_rows, ext.inner_rows) for i in range(4)]
+        if c <= KIND:
+            put(
+                mirrored(c, -sign_x, 1),
+                pl.ds(ext.row(x, y), ext.inner_rows),
+                ref[rows[0], :],
+            )
+        elif k == FACE_X_SUMS:
+            put_sums(ext, put, x, y, ext.inner_rows, [ref[r, :] for r in rows], -1)
+
+
+def put_face_y(ext, put, ref, sign_y):
+    cells = ext.cells_x
+
+    def line(x, y, count=cells):
+        return pl.ds(ext.row(x, y), count, stride=ext.pitch)
+
+    for k, (c, d) in enumerate(face_y):
+        if c <= KIND:
+            put(
+                mirrored(c, 1, -sign_y),
+                line(0, beyond(ext.cells_y, sign_y, d)),
+                ref[pl.ds(k * cells, cells), :],
+            )
+    y = beyond(ext.cells_y, sign_y, HALO - 1)
+    total, across, along, solute = (
+        ref[pl.ds((FACE_Y_SUMS + i) * cells, cells), :] for i in range(4)
+    )
+    last = lax.broadcasted_iota(jnp.int32, across.shape, 0) == cells - 1
+    back = all_velocity.index((-1, 0, 0))
+    forth = all_velocity.index((1, 0, 0))
+    put(0, line(0, y), total - jnp.where(last, across, -across))
+    put(back, line(1, y, cells - 1), -across[: cells - 1])
+    put(forth, pl.ds(ext.row(cells - 2, y), 1), across[cells - 1 :])
+    put(all_velocity.index((0, 0, 1)), line(0, y), along)
+    put(FLOW, line(0, y), solute)
+    for side, sign_x in enumerate((1, -1)):
+        x = cells - 1 if sign_x > 0 else 0
+        for k, c in enumerate(ends_y):
+            start = len(face_y) * cells + side * len(ends_y) + k
+            put(mirrored(c, sign_x, 1), pl.ds(ext.row(x, y), 1), ref[pl.ds(start, 1), :])
+
+
+def insert_kernel(ext, odd_ref, _, __, up_ref, down_ref, cup_ref, cdown_ref, ya_ref,
+                  one_ref, kinds_ref):
+    put = putter(one_ref, kinds_ref)
+    put_inner(ext, put, up_ref, -1)
+    put_inner(ext, put, down_ref, 1)
     for odd_y in (0, 1):
 
         @pl.when(odd_ref[0] == odd_y)
         def _():
-            for ref, sign in ((ya_ref, 1 - 2 * odd_y), (yb_ref, 2 * odd_y - 1)):
-                for k, (c, d) in enumerate(face_y):
-                    put(
-                        mirrored(c, 1, -sign),
-                        pl.ds(row(0, beyond(cells_y, sign, d)), cells_x, stride=pitch),
-                        ref[k],
-                    )
-            pair, far = 1 - 2 * odd_y, 2 * odd_y - 1
-            for ref, sign_x, sign_y in (
-                (cup_ref, -1, far),
-                (cdown_ref, 1, far),
-                (cpair_ref.at[0], -1, pair),
-                (cpair_ref.at[1], 1, pair),
-            ):
-                for k, (c, dx, dy) in enumerate(corner):
-                    put(
-                        mirrored(c, -sign_x, -sign_y),
-                        pl.ds(row(beyond(cells_x, sign_x, dx), beyond(cells_y, sign_y, dy)), 1),
-                        ref[pl.ds(k, 1), :],
-                    )
+            pair = 1 - 2 * odd_y
+            for ref, sign_x in ((cup_ref, -1), (cdown_ref, 1)):
+                for side, sign_y in enumerate((pair, -pair)):
+                    put_corner(ext, put, ref.at[side], sign_x, sign_y, 0)
+            put_face_y(ext, put, ya_ref.at[1 - odd_y], pair)
+
+
+def last_kernel(ext, odd_ref, _, __, yb_ref, pair_ref, far_ref, density_ref, momentum_ref,
+                concentration_ref, one_ref, kinds_ref, two_ref):
+    cells_x, cells_y, pitch, row = ext.cells_x, ext.cells_y, ext.pitch, ext.row
+    depth = one_ref.shape[-1]
+    put = putter(one_ref, kinds_ref)
+
+    for odd_y in (0, 1):
+
+        @pl.when(odd_ref[0] == odd_y)
+        def _():
+            pair = 1 - 2 * odd_y
+            put_face_y(ext, put, yb_ref, -pair)
+            for ref, sign_y in ((pair_ref, pair), (far_ref, -pair)):
+                for side, sign_x in enumerate((-1, 1)):
+                    put_corner(ext, put, ref.at[side], sign_x, -sign_y, sign_y * cells_y)
 
     lane = lax.broadcasted_iota(jnp.int32, (8, depth), 1)
 
@@ -373,12 +530,12 @@
             out_shape=[
                 shape(COUNT, ext.rows, depth),
                 shape(ext.rows, depth),
-                shape(len(face_x), cells_y, depth),
-                shape(len(face_x), cells_y, depth),
-                shape(len(face_y), cells_x, depth),
-                shape(len(face_y), cells_x, depth),
-                shape(CORNER_ROWS, depth),
-                shape(CORNER_ROWS, depth),
+                shape(len(face_x) * ext.inner_rows, depth),
+                shape(len(face_x) * ext.inner_rows, depth),
+                shape(ext.face_y_rows, depth),
+                shape(ext.face_y_rows, depth),
+                shape(2, CORNER_ROWS, depth),
+                shape(2, CORNER_ROWS, depth),
             ],
             in_specs=[smem, hbm, hbm, hbm],
             out_specs=[vmem] * 8,
@@ -386,26 +543,35 @@
                 pltpu.VMEM(flow.shape, f32),
                 pltpu.VMEM(solute.shape, f32),
                 pltpu.VMEM(kind.shape, kind.dtype),
+                pltpu.VMEM((8, ext.rows, depth), f32),
                 pltpu.SemaphoreType.DMA((cells_x // group, 3)),
             ],
             compiler_params=params,
         )(odd, flow, solute, kind)
         move = functools.partial(swapped, count_x=count_x, count_y=count_y)
+        cup = move(cup, move_x=higher, move_y=None)
+        cdown = move(cdown, move_x=lower, move_y=None)
+        yb = move(yb, move_x=None, move_y=across)
         up = move(up, move_x=higher, move_y=None)
         down = move(down, move_x=lower, move_y=None)
-        yb = move(yb, move_x=None, move_y=across)
-        cup = move(cup, move_x=higher, move_y=across)
-        cdown = move(cdown, move_x=lower, move_y=across)
-        ya, up, down, yb, cup, cdown = lax.optimization_barrier((ya, up, down, yb, cup, cdown))
-        ya = move(ya, move_x=None, move_y=near)
-        cpair = pl.pallas_call(
-            functools.partial(forward_kernel, cells_y),
-            out_shape=shape(2, CORNER_ROWS, depth),
-            in_specs=[smem, vmem, vmem],
-            out_specs=vmem,
+        pair, far = pl.pallas_call(
+            forward_kernel,
+            out_shape=[shape(2, CORNER_ROWS, depth)] * 2,
+            in_specs=[vmem, vmem],
+            out_specs=[vmem, vmem],
             compiler_params=params,
-        )(odd, up, down)
-        cpair = move(cpair, move_x=None, move_y=near)
+        )(cup, cdown)
+        far = move(far, move_x=None, move_y=across)
+        pair = move(pair, move_x=None, move_y=near)
+        ya = lax.all_gather(ya, "gy", axis_index_groups=[[j, j + 1] for j in range(0, count_y, 2)])
+        post, kinds = pl.pallas_call(
+            functools.partial(insert_kernel, ext),
+            out_shape=[shape(COUNT, ext.rows, depth), shape(ext.rows, depth)],
+            in_specs=[smem] + [vmem] * 7,
+            out_specs=[vmem] * 2,
+            input_output_aliases={1: 0, 2: 1},
+            compiler_params=params,
+        )(odd, post, kinds, up, down, cup, cdown, ya)
         density, momentum, concentration, _, _ = pl.pallas_call(
             functools.partial(last_kernel, ext),
             out_shape=[
@@ -415,12 +581,12 @@
                 shape(COUNT, ext.rows, depth),
                 shape(ext.rows, depth),
             ],
-            in_specs=[smem] + [vmem] * 9,
+            in_specs=[smem] + [vmem] * 5,
             out_specs=[vmem] * 5,
             scratch_shapes=[pltpu.VMEM((COUNT, ext.rows, depth), f32)],
             input_output_aliases={1: 3, 2: 4},
             compiler_params=params,
-        )(odd, post, kinds, up, down, ya, yb, cup, cdown, cpair)
+        )(odd, post, kinds, yb, pair, far)
         return density, momentum, concentration
 
     placed = (P(None, "gx", "gy", None), P(None, "gx", "gy", None), P("gx", "gy", None))

time: 27.3 us -> 24.8 us (0.908)
  waiting for transfers between devices: 7.72 us -> 3.99 us
  blocking collectives: 0 us -> 2.31 us
  starting transfers between devices: 13.2 us -> 12.1 us
    ppermute x7, waiting for transfers between devices: 7.72 us -> 3.99 us  [swapped(): return lax.ppermute(block, ('gx', 'gy'), pairs)]
    all_gather x0 -> x1, blocking collectives: none -> 2.31 us  [local(): lax.all_gather(ya, 'gy', axis_index_groups=[[j, j + 1] for j in range(0,...]
    ppermute x7, starting transfers between devices: 13.2 us -> 12.1 us  [swapped(): return lax.ppermute(block, ('gx', 'gy'), pairs)]
  transfers between devices with their start and end apart: 7 -> 7, of which waited for: 2 -> 2; matrix products, arithmetic and copies ran while one was open for 0% -> 0% of each run, Pallas kernels for 0% -> 1%
where the time goes in v3:
time: 24.8 us; the launch traced here: 24.5 us
  starting transfers between devices  12.1 us (49%)
  Pallas kernels  5.46 us (22%)
  waiting for transfers between devices  3.99 us (16%)
  blocking collectives  2.31 us (9%)
  between operations  0.68 us (3%)
    ppermute x7, starting transfers between devices, swapped(): return lax.ppermute(block, ('gx', 'gy'), pairs)  12.1 us
    ppermute x7, waiting for transfers between devices, swapped(): return lax.ppermute(block, ('gx', 'gy'), pairs)  3.99 us
    pallas_call x1, Pallas kernels, local(): pl.pallas_call(functools.partial(last_kernel, ext), out_shape=[shape(cell...  3.25 us
    all_gather x1, blocking collectives, local(): lax.all_gather(ya, 'gy', axis_index_groups=[[j, j + 1] for j in range(0,...  2.31 us
    pallas_call x1, Pallas kernels, local(): pl.pallas_call(functools.partial(first_kernel, ext, group), out_shape=[sh...  2.06 us
  transfers between devices with their start and end apart: 7, of which 2 were waited for; matrix products, arithmetic and copies ran while one was open for 0% of the time, Pallas kernels for 1%

profile of v3, /device:TPU:0, one launch (start us, length us, event | category | flops | bytes accessed | tf_op | source)
XLA Modules:
  0.0 24.5 jit_solution(16754692954823504898)
XLA Ops:
  0.6 2.1 %shard_map.58 = (f32[26,328,128]{2,1,0:T(8,128)S(1)}, f32[328,128]{1,0:T(8,128)S(1)}, f32[176,128]{1,0:T(8,128)S(1)}, f32[176,128]{1,0:T(8,128)S(1)}, f32[712,12...) custom-call(s32[1]{0:T(128)} %bitcast.odd_ref, ...), custom_call_target="tpu_custom_call" | custom-call | tf_op jit(solution)/shard_map/pallas_call | solution.py:528
  2.7 3.4 %collective-permute-start.4 = (f32[712,128]{1,0:T(8,128)S(1)}, f32[712,128]{1,0:T(8,128)S(1)}, u32[]{:S(2)}, u32[]{:S(2)}) collective-permute-start(f32[712,128]{1,0:T(8,128)S(1)} %get-tuple-element.27), channel_id=1, source_target_pairs={{0,7},{1,2},{2,1},{3,4},{4,3},{5,6},{6,5},{7,0},{8,15},{9,10},{10,... | collective-permute-start | bytes 1093640 | tf_op jit(solution)/shard_map/ppermute | solution.py:507
  6.1 1.6 %collective-permute-start.2 = (f32[2,96,128]{2,1,0:T(8,128)S(1)}, f32[2,96,128]{2,1,0:T(8,128)S(1)}, u32[]{:S(2)}, u32[]{:S(2)}) collective-permute-start(f32[2,96,128]{2,1,0:T(8,128)S(1)} %get-tuple-element.22), channel_id=1, source_target_pairs={{0,8},{1,9},{2,10},{3,11},{4,12},{5,13},{6,14},{7,15},{8,16},{9,17... | collective-permute-start | bytes 294920 | tf_op jit(solution)/shard_map/ppermute | solution.py:507
  7.7 2.2 %collective-permute-start.3 = (f32[2,96,128]{2,1,0:T(8,128)S(1)}, f32[2,96,128]{2,1,0:T(8,128)S(1)}, u32[]{:S(2)}, u32[]{:S(2)}) collective-permute-start(f32[2,96,128]{2,1,0:T(8,128)S(1)} %get-tuple-element.23), channel_id=1, source_target_pairs={{0,24},{1,25},{2,26},{3,27},{4,28},{5,29},{6,30},{7,31},{8,0},{9,1... | collective-permute-start | bytes 294920 | tf_op jit(solution)/shard_map/ppermute | solution.py:507
  9.9 0.0 collective-permute-start
  9.9 3.8 %collective-permute-start.1 = (f32[176,128]{1,0:T(8,128)S(1)}, f32[176,128]{1,0:T(8,128)S(1)}, u32[]{:S(2)}, u32[]{:S(2)}) collective-permute-start(f32[176,128]{1,0:T(8,128)S(1)} %get-tuple-element.21), channel_id=1, source_target_pairs={{0,24},{1,25},{2,26},{3,27},{4,28},{5,29},{6,30},{7,31},{8,0},{9,1... | collective-permute-start | bytes 270344 | tf_op jit(solution)/shard_map/ppermute | solution.py:507
  13.8 0.0 collective-permute-done.2.cup_ref
  13.8 1.7 %collective-permute-done.3.cdown_ref = f32[2,96,128]{2,1,0:T(8,128)S(1)} collective-permute-done((f32[2,96,128]{2,1,0:T(8,128)S(1)}, f32[2,96,128]{2,1,0:T(8,128)S(1)}, u32[]{:S(2)}, u32[]{:S(2)}) %collective-permute-start.3) | collective-permute-done | bytes 98336 | tf_op jit(solution)/shard_map/ppermute | solution.py:507
  15.5 0.1 collective-permute-start.5
  15.5 0.9 %collective-permute-start.6 = (f32[2,96,128]{2,1,0:T(8,128)S(1)}, f32[2,96,128]{2,1,0:T(8,128)S(1)}, u32[]{:S(2)}, u32[]{:S(2)}) collective-permute-start(f32[2,96,128]{2,1,0:T(8,128)S(1)} %get-tuple-element.29), channel_id=1, source_target_pairs={{0,7},{1,2},{2,1},{3,4},{4,3},{5,6},{6,5},{7,0},{8,15},{9,10},{10,... | collective-permute-start | bytes 294920 | tf_op jit(solution)/shard_map/ppermute | solution.py:507
  16.5 2.3 %all-gather = f32[1424,128]{1,0:T(8,128)S(1)} all-gather(f32[712,128]{1,0:T(8,128)S(1)} %get-tuple-element.24), channel_id=2, replica_groups={{0,1},{2,3},{4,5},{6,7},{8,9},{10,11},{12,13},{14,15},{16,17},{18,19},{..., dimensions={0}, use_global_device_ids=true | all-gather | bytes 1093632 | tf_op jit(solution)/shard_map/all_gather | solution.py:566
  18.8 0.0 collective-permute-done.up_ref
  18.8 0.0 collective-permute-done.1.down_ref
  18.8 0.1 shard_map.59
  18.9 0.0 collective-permute-done.5.pair_ref
  19.0 2.3 %collective-permute-done.6.far_ref = f32[2,96,128]{2,1,0:T(8,128)S(1)} collective-permute-done((f32[2,96,128]{2,1,0:T(8,128)S(1)}, f32[2,96,128]{2,1,0:T(8,128)S(1)}, u32[]{:S(2)}, u32[]{:S(2)}) %collective-permute-start.6) | collective-permute-done | bytes 98336 | tf_op jit(solution)/shard_map/ppermute | solution.py:507
  21.3 0.0 collective-permute-done.4.yb_ref
  21.3 3.3 %shard_map.61 = (f32[16,8,128]{2,1,0:T(8,128)}, f32[3,16,8,128]{3,2,1,0:T(8,128)}, f32[16,8,128]{2,1,0:T(8,128)}, f32[26,328,128]{2,1,0:T(8,128)S(1)}, f32[328,128]{1,0:T(8,128)S(1)}) custom-call(s32[1]{0:T(128)} %bitcast.odd_ref, f32[26,328,128]{2,1,0:T(8,128)S(1)} %get-tuple-element.25._, ...), custom_call_target="tpu_custom_call", output_to_operand_aliasing={{3}: (1, {}), {4}: (2, {})} | custom-call | tf_op jit(solution)/shard_map/pallas_call | solution.py:575
  (1 shorter events, 0.0 us)
Async XLA Ops:
  2.7 18.6 %collective-permute-start.4 = (f32[712,128]{1,0:T(8,128)S(1)}, f32[712,128]{1,0:T(8,128)S(1)}, u32[]{:S(2)}, u32[]{:S(2)}) collective-permute-start(f32[712,128]{1,0:T(8,128)S(1)} %get-tuple-element.27), channel_id=1, source_target_pairs={{0,7},{1,2},{2,1},{3,4},{4,3},{5,6},{6,5},{7,0},{8,15},{9,10},{10,... | collective-permute-start | bytes 1093640 | tf_op jit(solution)/shard_map/ppermute | solution.py:507
  6.1 7.7 %collective-permute-start.2 = (f32[2,96,128]{2,1,0:T(8,128)S(1)}, f32[2,96,128]{2,1,0:T(8,128)S(1)}, u32[]{:S(2)}, u32[]{:S(2)}) collective-permute-start(f32[2,96,128]{2,1,0:T(8,128)S(1)} %get-tuple-element.22), channel_id=1, source_target_pairs={{0,8},{1,9},{2,10},{3,11},{4,12},{5,13},{6,14},{7,15},{8,16},{9,17... | collective-permute-start | bytes 294920 | tf_op jit(solution)/shard_map/ppermute | solution.py:507
  7.7 7.8 %collective-permute-start.3 = (f32[2,96,128]{2,1,0:T(8,128)S(1)}, f32[2,96,128]{2,1,0:T(8,128)S(1)}, u32[]{:S(2)}, u32[]{:S(2)}) collective-permute-start(f32[2,96,128]{2,1,0:T(8,128)S(1)} %get-tuple-element.23), channel_id=1, source_target_pairs={{0,24},{1,25},{2,26},{3,27},{4,28},{5,29},{6,30},{7,31},{8,0},{9,1... | collective-permute-start | bytes 294920 | tf_op jit(solution)/shard_map/ppermute | solution.py:507
  9.9 8.9 %collective-permute-start = (f32[176,128]{1,0:T(8,128)S(1)}, f32[176,128]{1,0:T(8,128)S(1)}, u32[]{:S(2)}, u32[]{:S(2)}) collective-permute-start(f32[176,128]{1,0:T(8,128)S(1)} %get-tuple-element.20), channel_id=1, source_target_pairs={{0,8},{1,9},{2,10},{3,11},{4,12},{5,13},{6,14},{7,15},{8,16},{9,17... | collective-permute-start | bytes 270344 | tf_op jit(solution)/shard_map/ppermute | solution.py:507
  9.9 8.9 %collective-permute-start.1 = (f32[176,128]{1,0:T(8,128)S(1)}, f32[176,128]{1,0:T(8,128)S(1)}, u32[]{:S(2)}, u32[]{:S(2)}) collective-permute-start(f32[176,128]{1,0:T(8,128)S(1)} %get-tuple-element.21), channel_id=1, source_target_pairs={{0,24},{1,25},{2,26},{3,27},{4,28},{5,29},{6,30},{7,31},{8,0},{9,1... | collective-permute-start | bytes 270344 | tf_op jit(solution)/shard_map/ppermute | solution.py:507
  15.5 3.5 %collective-permute-start.5 = (f32[2,96,128]{2,1,0:T(8,128)S(1)}, f32[2,96,128]{2,1,0:T(8,128)S(1)}, u32[]{:S(2)}, u32[]{:S(2)}) collective-permute-start(f32[2,96,128]{2,1,0:T(8,128)S(1)} %get-tuple-element.28), channel_id=1, source_target_pairs={{0,1},{1,0},{2,3},{3,2},{4,5},{5,4},{6,7},{7,6},{8,9},{9,8},{10,11... | collective-permute-start | bytes 294920 | tf_op jit(solution)/shard_map/ppermute | solution.py:507
  15.5 5.7 %collective-permute-start.6 = (f32[2,96,128]{2,1,0:T(8,128)S(1)}, f32[2,96,128]{2,1,0:T(8,128)S(1)}, u32[]{:S(2)}, u32[]{:S(2)}) collective-permute-start(f32[2,96,128]{2,1,0:T(8,128)S(1)} %get-tuple-element.29), channel_id=1, source_target_pairs={{0,7},{1,2},{2,1},{3,4},{4,3},{5,6},{6,5},{7,0},{8,15},{9,10},{10,... | collective-permute-start | bytes 294920 | tf_op jit(solution)/shard_map/ppermute | solution.py:507

commit v4 on v3

--- a/solution.py
+++ b/solution.py
@@ -414,49 +414,32 @@
             put_face_y(ext, put, ya_ref.at[1 - odd_y], pair)
 
 
-def last_kernel(ext, odd_ref, _, __, yb_ref, pair_ref, far_ref, density_ref, momentum_ref,
-                concentration_ref, one_ref, kinds_ref, two_ref):
-    cells_x, cells_y, pitch, row = ext.cells_x, ext.cells_y, ext.pitch, ext.row
-    depth = one_ref.shape[-1]
-    put = putter(one_ref, kinds_ref)
-
-    for odd_y in (0, 1):
-
-        @pl.when(odd_ref[0] == odd_y)
-        def _():
-            pair = 1 - 2 * odd_y
-            put_face_y(ext, put, yb_ref, -pair)
-            for ref, sign_y in ((pair_ref, pair), (far_ref, -pair)):
-                for side, sign_x in enumerate((-1, 1)):
-                    put_corner(ext, put, ref.at[side], sign_x, -sign_y, sign_y * cells_y)
-
-    lane = lax.broadcasted_iota(jnp.int32, (8, depth), 1)
-
-    def arriving(ref, c, start, size):
-        cx, cy, _ = all_velocity[c]
-        return ref[c, pl.ds(start - (cx * pitch + cy), size), :]
-
-    def advance(source, target, width):
-        first = row(-width, -width)
-        for start in range(first, row(cells_x - 1 + width, cells_y - 1 + width) + 1, 8):
-            values = [arriving(source, c, start, 8) for c in range(COUNT)]
-            values = collide(values[:FLOW], values[FLOW:], kinds_ref[pl.ds(start, 8), :])
-
-            def store(c, value):
-                target[c, pl.ds(start, 8), :] = value
-
-            if width > 1:
-                store_shifted(values, lane, store)
-            else:
-                for c in range(COUNT):
-                    store(c, values[c])
-
-    source, target = one_ref, two_ref
-    for width in range(HALO - 1, 0, -1):
-        advance(source, target, width)
-        source, target = target, source
-
-    def summed(values, weights):
+def arriving(ext, ref, c, start, count):
+    cx, cy, _ = all_velocity[c]
+    return ref[c, pl.ds(start - (cx * ext.pitch + cy), count), :]
+
+
+def advance(ext, source, target, kinds_ref, first, shifted):
+    rows = pl.ds(first, 8)
+    values = [arriving(ext, source, c, first, 8) for c in range(COUNT)]
+    values = collide(values[:FLOW], values[FLOW:], kinds_ref[rows, :])
+    lane = lax.broadcasted_iota(jnp.int32, values[0].shape, 1)
+
+    def store(c, value):
+        target[c, rows, :] = value
+
+    if shifted:
+        store_shifted(values, lane, store)
+    else:
+        for c in range(COUNT):
+            store(c, values[c])
+
+
+def finish(ext, source, x, density_ref, momentum_ref, concentration_ref):
+    values = [arriving(ext, source, c, ext.row(x, 0), ext.cells_y) for c in range(COUNT)]
+    lane = lax.broadcasted_iota(jnp.int32, values[0].shape, 1)
+
+    def summed(weights):
         total = None
         for along_z in (0, 1, -1):
             part = None
@@ -472,13 +455,58 @@
                 total = part if total is None else total + part
         return total
 
-    flow = range(FLOW)
-    for x in range(cells_x):
-        values = [arriving(source, c, row(x, 0), cells_y) for c in range(COUNT)]
-        density_ref[x] = summed(values, {c: 1 for c in flow})
+    density_ref[x] = summed({c: 1 for c in range(FLOW)})
+    for axis in range(3):
+        momentum_ref[axis, x] = summed({c: flow_velocity[c][axis] for c in range(FLOW)})
+    concentration_ref[x] = summed({c: 1 for c in range(FLOW, COUNT)})
+
+
+def middle_kernel(ext, odd_ref, _, __, yb_ref, pair_ref, one_ref, kinds_ref, two_ref, three_ref,
+                  density_ref, momentum_ref, concentration_ref):
+    put = putter(one_ref, kinds_ref)
+    for odd_y in (0, 1):
+
+        @pl.when(odd_ref[0] == odd_y)
+        def _():
+            pair = 1 - 2 * odd_y
+            put_face_y(ext, put, yb_ref, -pair)
+            for side, sign_x in enumerate((-1, 1)):
+                put_corner(ext, put, pair_ref.at[side], sign_x, -pair, pair * ext.cells_y)
+
+    for source, target, width in ((one_ref, two_ref, 2), (two_ref, three_ref, 1)):
+        end = ext.row(ext.cells_x - 1 + width, ext.cells_y - 1 + width)
+        for first in range(ext.row(-width, -width), end + 1, 8):
+            advance(ext, source, target, kinds_ref, first, width > 1)
+    for x in range(ext.cells_x):
+        finish(ext, three_ref, x, density_ref, momentum_ref, concentration_ref)
+
+
+def last_kernel(ext, odd_ref, _, __, ___, ____, far_ref, early_density_ref, early_momentum_ref,
+                early_concentration_ref, density_ref, momentum_ref, concentration_ref,
+                one_ref, kinds_ref, two_ref, three_ref):
+    cells_x, cells_y = ext.cells_x, ext.cells_y
+    put = putter(one_ref, kinds_ref)
+    for x in range(HALO, cells_x - HALO):
+        density_ref[x] = early_density_ref[x]
         for axis in range(3):
-            momentum_ref[axis, x] = summed(values, {c: flow_velocity[c][axis] for c in flow})
-        concentration_ref[x] = summed(values, {c: 1 for c in range(FLOW, COUNT)})
+            momentum_ref[axis, x] = early_momentum_ref[axis, x]
+        concentration_ref[x] = early_concentration_ref[x]
+    for odd_y in (0, 1):
+
+        @pl.when(odd_ref[0] == odd_y)
+        def _():
+            far = 2 * odd_y - 1
+            for side, sign_x in enumerate((-1, 1)):
+                put_corner(ext, put, far_ref.at[side], sign_x, -far, far * cells_y)
+            for source, target, width in ((one_ref, two_ref, 2), (two_ref, three_ref, 1)):
+                y = cells_y + width - 8 if far > 0 else -width
+                for k in range(HALO):
+                    for x in (k - width, cells_x - 1 + width - k):
+                        advance(ext, source, target, kinds_ref, ext.row(x, y), width > 1)
+
+    for k in range(HALO):
+        for x in (k, cells_x - 1 - k):
+            finish(ext, three_ref, x, density_ref, momentum_ref, concentration_ref)
 
 
 def higher(i, count):
@@ -518,7 +546,7 @@
         smem = pl.BlockSpec(memory_space=pltpu.SMEM)
         vmem = pl.BlockSpec(memory_space=pltpu.VMEM)
         hbm = pl.BlockSpec(memory_space=pltpu.HBM)
-        params = pltpu.CompilerParams(vmem_limit_bytes=40 * 1024 * 1024)
+        params = pltpu.CompilerParams(vmem_limit_bytes=16 * 1024 * 1024)
         odd = jnp.reshape(lax.axis_index("gy") % 2, (1,)).astype(jnp.int32)
         ext = Extended(cells_x, cells_y)
         group = math.gcd(cells_x, 4)
@@ -572,21 +600,28 @@
             input_output_aliases={1: 0, 2: 1},
             compiler_params=params,
         )(odd, post, kinds, up, down, cup, cdown, ya)
-        density, momentum, concentration, _, _ = pl.pallas_call(
+        moments = [
+            shape(cells_x, cells_y, depth),
+            shape(3, cells_x, cells_y, depth),
+            shape(cells_x, cells_y, depth),
+        ]
+        one = shape(COUNT, ext.rows, depth)
+        post, kinds, two, three, *early = pl.pallas_call(
+            functools.partial(middle_kernel, ext),
+            out_shape=[one, shape(ext.rows, depth), one, one] + moments,
+            in_specs=[smem] + [vmem] * 4,
+            out_specs=[vmem] * 7,
+            input_output_aliases={1: 0, 2: 1},
+            compiler_params=params,
+        )(odd, post, kinds, yb, pair)
+        density, momentum, concentration, *_ = pl.pallas_call(
             functools.partial(last_kernel, ext),
-            out_shape=[
-                shape(cells_x, cells_y, depth),
-                shape(3, cells_x, cells_y, depth),
-                shape(cells_x, cells_y, depth),
-                shape(COUNT, ext.rows, depth),
-                shape(ext.rows, depth),
-            ],
-            in_specs=[smem] + [vmem] * 5,
-            out_specs=[vmem] * 5,
-            scratch_shapes=[pltpu.VMEM((COUNT, ext.rows, depth), f32)],
-            input_output_aliases={1: 3, 2: 4},
+            out_shape=moments + [one, shape(ext.rows, depth), one, one],
+            in_specs=[smem] + [vmem] * 8,
+            out_specs=[vmem] * 7,
+            input_output_aliases={1: 3, 2: 4, 3: 5, 4: 6},
             compiler_params=params,
-        )(odd, post, kinds, yb, pair, far)
+        )(odd, post, kinds, two, three, far, *early)
         return density, momentum, concentration
 
     placed = (P(None, "gx", "gy", None), P(None, "gx", "gy", None), P("gx", "gy", None))

time: 24.8 us -> 23 us (0.927)
  waiting for transfers between devices: 3.99 us -> 1.7 us
  Pallas kernels: 5.46 us -> 6.01 us
    ppermute x7, waiting for transfers between devices: 3.99 us -> 1.7 us  [swapped(): return lax.ppermute(block, ('gx', 'gy'), pairs)]
    pallas_call x1 -> x2, Pallas kernels: 3.25 us -> 3.8 us  [the longest x1 2.54 us: local(): pl.pallas_call(functools.partial(middle_kernel, ext), out_shape=[one, sha...]
  transfers between devices with their start and end apart: 7 -> 7, of which waited for: 2 -> 1; matrix products, arithmetic and copies ran while one was open for 0% -> 0% of each run, Pallas kernels for 1% -> 12%
where the time goes in v4:
time: 23 us; the launch traced here: 22.8 us
  starting transfers between devices  12.1 us (53%)
  Pallas kernels  6.01 us (26%)
  blocking collectives  2.31 us (10%)
  waiting for transfers between devices  1.7 us (7%)
  between operations  0.7 us (3%)
    ppermute x7, starting transfers between devices, swapped(): return lax.ppermute(block, ('gx', 'gy'), pairs)  12.1 us
    pallas_call x1, Pallas kernels, local(): pl.pallas_call(functools.partial(middle_kernel, ext), out_shape=[one, sha...  2.54 us
    all_gather x1, blocking collectives, local(): lax.all_gather(ya, 'gy', axis_index_groups=[[j, j + 1] for j in range(0,...  2.31 us
    pallas_call x1, Pallas kernels, local(): pl.pallas_call(functools.partial(first_kernel, ext, group), out_shape=[sh...  2.06 us
    ppermute x7, waiting for transfers between devices, swapped(): return lax.ppermute(block, ('gx', 'gy'), pairs)  1.7 us
    pallas_call x1, Pallas kernels, local(): pl.pallas_call(functools.partial(last_kernel, ext), out_shape=moments + [...  1.26 us
  transfers between devices with their start and end apart: 7, of which 1 were waited for; matrix products, arithmetic and copies ran while one was open for 0% of the time, Pallas kernels for 12%

profile of v4, /device:TPU:0, one launch (start us, length us, event | category | flops | bytes accessed | tf_op | source)
XLA Modules:
  0.0 22.8 jit_solution(2346517301237748648)
XLA Ops:
  0.6 2.1 %shard_map.58 = (f32[26,328,128]{2,1,0:T(8,128)S(1)}, f32[328,128]{1,0:T(8,128)S(1)}, f32[176,128]{1,0:T(8,128)S(1)}, f32[176,128]{1,0:T(8,128)S(1)}, f32[712,12...) custom-call(s32[1]{0:T(128)} %bitcast.odd_ref, ...), custom_call_target="tpu_custom_call" | custom-call | tf_op jit(solution)/shard_map/pallas_call | solution.py:556
  2.7 3.4 %collective-permute-start.4 = (f32[712,128]{1,0:T(8,128)S(1)}, f32[712,128]{1,0:T(8,128)S(1)}, u32[]{:S(2)}, u32[]{:S(2)}) collective-permute-start(f32[712,128]{1,0:T(8,128)S(1)} %get-tuple-element.34), channel_id=1, source_target_pairs={{0,7},{1,2},{2,1},{3,4},{4,3},{5,6},{6,5},{7,0},{8,15},{9,10},{10,... | collective-permute-start | bytes 1093640 | tf_op jit(solution)/shard_map/ppermute | solution.py:535
  6.1 1.6 %collective-permute-start.2 = (f32[2,96,128]{2,1,0:T(8,128)S(1)}, f32[2,96,128]{2,1,0:T(8,128)S(1)}, u32[]{:S(2)}, u32[]{:S(2)}) collective-permute-start(f32[2,96,128]{2,1,0:T(8,128)S(1)} %get-tuple-element.29), channel_id=1, source_target_pairs={{0,8},{1,9},{2,10},{3,11},{4,12},{5,13},{6,14},{7,15},{8,16},{9,17... | collective-permute-start | bytes 294920 | tf_op jit(solution)/shard_map/ppermute | solution.py:535
  7.7 2.2 %collective-permute-start.3 = (f32[2,96,128]{2,1,0:T(8,128)S(1)}, f32[2,96,128]{2,1,0:T(8,128)S(1)}, u32[]{:S(2)}, u32[]{:S(2)}) collective-permute-start(f32[2,96,128]{2,1,0:T(8,128)S(1)} %get-tuple-element.30), channel_id=1, source_target_pairs={{0,24},{1,25},{2,26},{3,27},{4,28},{5,29},{6,30},{7,31},{8,0},{9,1... | collective-permute-start | bytes 294920 | tf_op jit(solution)/shard_map/ppermute | solution.py:535
  9.9 0.0 collective-permute-start
  9.9 3.8 %collective-permute-start.1 = (f32[176,128]{1,0:T(8,128)S(1)}, f32[176,128]{1,0:T(8,128)S(1)}, u32[]{:S(2)}, u32[]{:S(2)}) collective-permute-start(f32[176,128]{1,0:T(8,128)S(1)} %get-tuple-element.28), channel_id=1, source_target_pairs={{0,24},{1,25},{2,26},{3,27},{4,28},{5,29},{6,30},{7,31},{8,0},{9,1... | collective-permute-start | bytes 270344 | tf_op jit(solution)/shard_map/ppermute | solution.py:535
  13.8 0.0 collective-permute-done.2.cup_ref
  13.8 1.7 %collective-permute-done.3.cdown_ref = f32[2,96,128]{2,1,0:T(8,128)S(1)} collective-permute-done((f32[2,96,128]{2,1,0:T(8,128)S(1)}, f32[2,96,128]{2,1,0:T(8,128)S(1)}, u32[]{:S(2)}, u32[]{:S(2)}) %collective-permute-start.3) | collective-permute-done | bytes 98336 | tf_op jit(solution)/shard_map/ppermute | solution.py:535
  15.5 0.1 collective-permute-start.5
  15.5 0.9 %collective-permute-start.6 = (f32[2,96,128]{2,1,0:T(8,128)S(1)}, f32[2,96,128]{2,1,0:T(8,128)S(1)}, u32[]{:S(2)}, u32[]{:S(2)}) collective-permute-start(f32[2,96,128]{2,1,0:T(8,128)S(1)} %get-tuple-element.40), channel_id=1, source_target_pairs={{0,7},{1,2},{2,1},{3,4},{4,3},{5,6},{6,5},{7,0},{8,15},{9,10},{10,... | collective-permute-start | bytes 294920 | tf_op jit(solution)/shard_map/ppermute | solution.py:535
  16.5 2.3 %all-gather = f32[1424,128]{1,0:T(8,128)S(1)} all-gather(f32[712,128]{1,0:T(8,128)S(1)} %get-tuple-element.31), channel_id=2, replica_groups={{0,1},{2,3},{4,5},{6,7},{8,9},{10,11},{12,13},{14,15},{16,17},{18,19},{..., dimensions={0}, use_global_device_ids=true | all-gather | bytes 1093632 | tf_op jit(solution)/shard_map/all_gather | solution.py:594
  18.8 0.0 collective-permute-done.up_ref
  18.8 0.0 collective-permute-done.1.down_ref
  18.8 0.1 shard_map.59
  19.0 0.0 collective-permute-done.5.pair_ref
  19.0 0.0 collective-permute-done.4.yb_ref
  19.0 2.5 %shard_map.61 = (f32[26,328,128]{2,1,0:T(8,128)S(1)}, f32[328,128]{1,0:T(8,128)S(1)}, f32[26,328,128]{2,1,0:T(8,128)S(1)}, f32[26,328,128]{2,1,0:T(8,128)S(1)}, ...) custom-call(s32[1]{0:T(128)} %bitcast.odd_ref, ...), custom_call_target="tpu_custom_call", output_to_operand_aliasing={{0}: (1, {}), {1}: (2, {})} | custom-call | tf_op jit(solution)/shard_map/pallas_call | solution.py:609
  21.5 0.0 collective-permute-done.6.far_ref
  21.5 1.3 %shard_map.62 = (f32[16,8,128]{2,1,0:T(8,128)}, f32[3,16,8,128]{3,2,1,0:T(8,128)}, f32[16,8,128]{2,1,0:T(8,128)}, f32[26,328,128]{2,1,0:T(8,128)S(1)}, f32[328,1...) custom-call(s32[1]{0:T(128)} %bitcast.odd_ref, ...), custom_call_target="tpu_custom_call", output_to_operand_aliasing={{3}: (1, {}), {4}: (2, {}), {5}: (3, {}), {6}: (4, {})} | custom-call | tf_op jit(solution)/shard_map/pallas_call | solution.py:617
  (1 shorter events, 0.0 us)
Async XLA Ops:
  2.7 16.3 %collective-permute-start.4 = (f32[712,128]{1,0:T(8,128)S(1)}, f32[712,128]{1,0:T(8,128)S(1)}, u32[]{:S(2)}, u32[]{:S(2)}) collective-permute-start(f32[712,128]{1,0:T(8,128)S(1)} %get-tuple-element.34), channel_id=1, source_target_pairs={{0,7},{1,2},{2,1},{3,4},{4,3},{5,6},{6,5},{7,0},{8,15},{9,10},{10,... | collective-permute-start | bytes 1093640 | tf_op jit(solution)/shard_map/ppermute | solution.py:535
  6.1 7.7 %collective-permute-start.2 = (f32[2,96,128]{2,1,0:T(8,128)S(1)}, f32[2,96,128]{2,1,0:T(8,128)S(1)}, u32[]{:S(2)}, u32[]{:S(2)}) collective-permute-start(f32[2,96,128]{2,1,0:T(8,128)S(1)} %get-tuple-element.29), channel_id=1, source_target_pairs={{0,8},{1,9},{2,10},{3,11},{4,12},{5,13},{6,14},{7,15},{8,16},{9,17... | collective-permute-start | bytes 294920 | tf_op jit(solution)/shard_map/ppermute | solution.py:535
  7.7 7.8 %collective-permute-start.3 = (f32[2,96,128]{2,1,0:T(8,128)S(1)}, f32[2,96,128]{2,1,0:T(8,128)S(1)}, u32[]{:S(2)}, u32[]{:S(2)}) collective-permute-start(f32[2,96,128]{2,1,0:T(8,128)S(1)} %get-tuple-element.30), channel_id=1, source_target_pairs={{0,24},{1,25},{2,26},{3,27},{4,28},{5,29},{6,30},{7,31},{8,0},{9,1... | collective-permute-start | bytes 294920 | tf_op jit(solution)/shard_map/ppermute | solution.py:535
  9.9 8.9 %collective-permute-start = (f32[176,128]{1,0:T(8,128)S(1)}, f32[176,128]{1,0:T(8,128)S(1)}, u32[]{:S(2)}, u32[]{:S(2)}) collective-permute-start(f32[176,128]{1,0:T(8,128)S(1)} %get-tuple-element.27), channel_id=1, source_target_pairs={{0,8},{1,9},{2,10},{3,11},{4,12},{5,13},{6,14},{7,15},{8,16},{9,17... | collective-permute-start | bytes 270344 | tf_op jit(solution)/shard_map/ppermute | solution.py:535
  9.9 8.9 %collective-permute-start.1 = (f32[176,128]{1,0:T(8,128)S(1)}, f32[176,128]{1,0:T(8,128)S(1)}, u32[]{:S(2)}, u32[]{:S(2)}) collective-permute-start(f32[176,128]{1,0:T(8,128)S(1)} %get-tuple-element.28), channel_id=1, source_target_pairs={{0,24},{1,25},{2,26},{3,27},{4,28},{5,29},{6,30},{7,31},{8,0},{9,1... | collective-permute-start | bytes 270344 | tf_op jit(solution)/shard_map/ppermute | solution.py:535
  15.5 3.5 %collective-permute-start.5 = (f32[2,96,128]{2,1,0:T(8,128)S(1)}, f32[2,96,128]{2,1,0:T(8,128)S(1)}, u32[]{:S(2)}, u32[]{:S(2)}) collective-permute-start(f32[2,96,128]{2,1,0:T(8,128)S(1)} %get-tuple-element.35), channel_id=1, source_target_pairs={{0,1},{1,0},{2,3},{3,2},{4,5},{5,4},{6,7},{7,6},{8,9},{9,8},{10,11... | collective-permute-start | bytes 294920 | tf_op jit(solution)/shard_map/ppermute | solution.py:535
  15.5 6.0 %collective-permute-start.6 = (f32[2,96,128]{2,1,0:T(8,128)S(1)}, f32[2,96,128]{2,1,0:T(8,128)S(1)}, u32[]{:S(2)}, u32[]{:S(2)}) collective-permute-start(f32[2,96,128]{2,1,0:T(8,128)S(1)} %get-tuple-element.40), channel_id=1, source_target_pairs={{0,7},{1,2},{2,1},{3,4},{4,3},{5,6},{6,5},{7,0},{8,15},{9,10},{10,... | collective-permute-start | bytes 294920 | tf_op jit(solution)/shard_map/ppermute | solution.py:535

commit v5 on v4

--- a/solution.py
+++ b/solution.py
@@ -301,10 +301,11 @@
             ref[pl.ds(k * ext.inner_rows, ext.inner_rows), :] = held(mirrored(c, sign, 1), where)
 
 
-def forward_kernel(cup_ref, cdown_ref, pair_ref, far_ref):
-    for side, ref in enumerate((pair_ref, far_ref)):
-        ref[0] = cup_ref[side]
-        ref[1] = cdown_ref[side]
+def forward_kernel(cup_ref, cdown_ref, _, ya_ref, far_ref):
+    first = ya_ref.shape[0] - 2 * CORNER_ROWS
+    for side, ref in enumerate((cup_ref, cdown_ref)):
+        ya_ref[pl.ds(first + side * CORNER_ROWS, CORNER_ROWS), :] = ref[0]
+        far_ref[side] = ref[1]
 
 
 def beyond(cells, sign, d):
@@ -398,22 +399,6 @@
             put(mirrored(c, sign_x, 1), pl.ds(ext.row(x, y), 1), ref[pl.ds(start, 1), :])
 
 
-def insert_kernel(ext, odd_ref, _, __, up_ref, down_ref, cup_ref, cdown_ref, ya_ref,
-                  one_ref, kinds_ref):
-    put = putter(one_ref, kinds_ref)
-    put_inner(ext, put, up_ref, -1)
-    put_inner(ext, put, down_ref, 1)
-    for odd_y in (0, 1):
-
-        @pl.when(odd_ref[0] == odd_y)
-        def _():
-            pair = 1 - 2 * odd_y
-            for ref, sign_x in ((cup_ref, -1), (cdown_ref, 1)):
-                for side, sign_y in enumerate((pair, -pair)):
-                    put_corner(ext, put, ref.at[side], sign_x, sign_y, 0)
-            put_face_y(ext, put, ya_ref.at[1 - odd_y], pair)
-
-
 def arriving(ext, ref, c, start, count):
     cx, cy, _ = all_velocity[c]
     return ref[c, pl.ds(start - (cx * ext.pitch + cy), count), :]
@@ -461,17 +446,26 @@
     concentration_ref[x] = summed({c: 1 for c in range(FLOW, COUNT)})
 
 
-def middle_kernel(ext, odd_ref, _, __, yb_ref, pair_ref, one_ref, kinds_ref, two_ref, three_ref,
+def middle_kernel(ext, odd_ref, _, __, up_ref, down_ref, cup_ref, cdown_ref, yb_ref, ya_ref,
+                  one_ref, kinds_ref, two_ref, three_ref,
                   density_ref, momentum_ref, concentration_ref):
     put = putter(one_ref, kinds_ref)
+    put_inner(ext, put, up_ref, -1)
+    put_inner(ext, put, down_ref, 1)
     for odd_y in (0, 1):
 
         @pl.when(odd_ref[0] == odd_y)
         def _():
             pair = 1 - 2 * odd_y
+            partner = ya_ref.at[1 - odd_y]
             put_face_y(ext, put, yb_ref, -pair)
-            for side, sign_x in enumerate((-1, 1)):
-                put_corner(ext, put, pair_ref.at[side], sign_x, -pair, pair * ext.cells_y)
+            put_face_y(ext, put, partner, pair)
+            for side, (ref, sign_x) in enumerate(((cup_ref, -1), (cdown_ref, 1))):
+                put_corner(ext, put, ref.at[0], sign_x, pair, 0)
+                put_corner(ext, put, ref.at[1], sign_x, -pair, 0)
+                first = partner.shape[0] - (2 - side) * CORNER_ROWS
+                corners = partner.at[pl.ds(first, CORNER_ROWS)]
+                put_corner(ext, put, corners, sign_x, -pair, pair * ext.cells_y)
 
     for source, target, width in ((one_ref, two_ref, 2), (two_ref, three_ref, 1)):
         end = ext.row(ext.cells_x - 1 + width, ext.cells_y - 1 + width)
@@ -515,10 +509,6 @@
 
 def lower(i, count):
     return (i - 1) % count
-
-
-def near(i, count):
-    return i ^ 1
 
 
 def across(i, count):
@@ -560,7 +550,7 @@
                 shape(ext.rows, depth),
                 shape(len(face_x) * ext.inner_rows, depth),
                 shape(len(face_x) * ext.inner_rows, depth),
-                shape(ext.face_y_rows, depth),
+                shape(ext.face_y_rows + 2 * CORNER_ROWS, depth),
                 shape(ext.face_y_rows, depth),
                 shape(2, CORNER_ROWS, depth),
                 shape(2, CORNER_ROWS, depth),
@@ -582,24 +572,16 @@
         yb = move(yb, move_x=None, move_y=across)
         up = move(up, move_x=higher, move_y=None)
         down = move(down, move_x=lower, move_y=None)
-        pair, far = pl.pallas_call(
+        ya, far = pl.pallas_call(
             forward_kernel,
-            out_shape=[shape(2, CORNER_ROWS, depth)] * 2,
-            in_specs=[vmem, vmem],
-            out_specs=[vmem, vmem],
+            out_shape=[shape(*ya.shape), shape(2, CORNER_ROWS, depth)],
+            in_specs=[vmem] * 3,
+            out_specs=[vmem] * 2,
+            input_output_aliases={2: 0},
             compiler_params=params,
-        )(cup, cdown)
+        )(cup, cdown, ya)
         far = move(far, move_x=None, move_y=across)
-        pair = move(pair, move_x=None, move_y=near)
         ya = lax.all_gather(ya, "gy", axis_index_groups=[[j, j + 1] for j in range(0, count_y, 2)])
-        post, kinds = pl.pallas_call(
-            functools.partial(insert_kernel, ext),
-            out_shape=[shape(COUNT, ext.rows, depth), shape(ext.rows, depth)],
-            in_specs=[smem] + [vmem] * 7,
-            out_specs=[vmem] * 2,
-            input_output_aliases={1: 0, 2: 1},
-            compiler_params=params,
-        )(odd, post, kinds, up, down, cup, cdown, ya)
         moments = [
             shape(cells_x, cells_y, depth),
             shape(3, cells_x, cells_y, depth),
@@ -609,11 +591,11 @@
         post, kinds, two, three, *early = pl.pallas_call(
             functools.partial(middle_kernel, ext),
             out_shape=[one, shape(ext.rows, depth), one, one] + moments,
-            in_specs=[smem] + [vmem] * 4,
+            in_specs=[smem] + [vmem] * 8,
             out_specs=[vmem] * 7,
             input_output_aliases={1: 0, 2: 1},
             compiler_params=params,
-        )(odd, post, kinds, yb, pair)
+        )(odd, post, kinds, up, down, cup, cdown, yb, ya)
         density, momentum, concentration, *_ = pl.pallas_call(
             functools.partial(last_kernel, ext),
             out_shape=moments + [one, shape(ext.rows, depth), one, one],

time: 23 us -> 22.2 us (0.965)
  starting transfers between devices: 12.1 us -> 11.1 us
    ppermute x7 -> x6, starting transfers between devices: 12.1 us -> 11.1 us  [swapped(): return lax.ppermute(block, ('gx', 'gy'), pairs)]
    ppermute x7 -> x6, waiting for transfers between devices: 1.7 us -> 1.7 us  [swapped(): return lax.ppermute(block, ('gx', 'gy'), pairs)]
  transfers between devices with their start and end apart: 7 -> 6, of which waited for: 1 -> 1; matrix products, arithmetic and copies ran while one was open for 0% -> 0% of each run, Pallas kernels for 12% -> 12%
where the time goes in v5:
time: 22.2 us; the launch traced here: 22 us
  starting transfers between devices  11.1 us (50%)
  Pallas kernels  5.99 us (27%)
  blocking collectives  2.47 us (11%)
  waiting for transfers between devices  1.7 us (8%)
  between operations  0.69 us (3%)
    ppermute x6, starting transfers between devices, swapped(): return lax.ppermute(block, ('gx', 'gy'), pairs)  11.1 us
    pallas_call x1, Pallas kernels, local(): pl.pallas_call(functools.partial(middle_kernel, ext), out_shape=[one, sha...  2.66 us
    all_gather x1, blocking collectives, local(): lax.all_gather(ya, 'gy', axis_index_groups=[[j, j + 1] for j in range(0,...  2.47 us
    pallas_call x1, Pallas kernels, local(): pl.pallas_call(functools.partial(first_kernel, ext, group), out_shape=[sh...  2.06 us
    ppermute x6, waiting for transfers between devices, swapped(): return lax.ppermute(block, ('gx', 'gy'), pairs)  1.7 us
    pallas_call x1, Pallas kernels, local(): pl.pallas_call(functools.partial(last_kernel, ext), out_shape=moments + [...  1.26 us
  transfers between devices with their start and end apart: 6, of which 1 were waited for; matrix products, arithmetic and copies ran while one was open for 0% of the time, Pallas kernels for 12%

profile of v5, /device:TPU:0, one launch (start us, length us, event | category | flops | bytes accessed | tf_op | source)
XLA Modules:
  0.0 22.0 jit_solution(14848729009932477933)
XLA Ops:
  0.6 2.1 %shard_map.58 = (f32[26,328,128]{2,1,0:T(8,128)S(1)}, f32[328,128]{1,0:T(8,128)S(1)}, f32[176,128]{1,0:T(8,128)S(1)}, f32[176,128]{1,0:T(8,128)S(1)}, f32[904,12...) custom-call(s32[1]{0:T(128)} %bitcast.odd_ref, ...), custom_call_target="tpu_custom_call" | custom-call | tf_op jit(solution)/shard_map/pallas_call | solution.py:546
  2.7 3.4 %collective-permute-start.4 = (f32[712,128]{1,0:T(8,128)S(1)}, f32[712,128]{1,0:T(8,128)S(1)}, u32[]{:S(2)}, u32[]{:S(2)}) collective-permute-start(f32[712,128]{1,0:T(8,128)S(1)} %get-tuple-element.29), channel_id=1, source_target_pairs={{0,7},{1,2},{2,1},{3,4},{4,3},{5,6},{6,5},{7,0},{8,15},{9,10},{10,... | collective-permute-start | bytes 1093640 | tf_op jit(solution)/shard_map/ppermute | solution.py:525
  6.1 1.6 %collective-permute-start.2 = (f32[2,96,128]{2,1,0:T(8,128)S(1)}, f32[2,96,128]{2,1,0:T(8,128)S(1)}, u32[]{:S(2)}, u32[]{:S(2)}) collective-permute-start(f32[2,96,128]{2,1,0:T(8,128)S(1)} %get-tuple-element.27), channel_id=1, source_target_pairs={{0,8},{1,9},{2,10},{3,11},{4,12},{5,13},{6,14},{7,15},{8,16},{9,17... | collective-permute-start | bytes 294920 | tf_op jit(solution)/shard_map/ppermute | solution.py:525
  7.7 2.2 %collective-permute-start.3 = (f32[2,96,128]{2,1,0:T(8,128)S(1)}, f32[2,96,128]{2,1,0:T(8,128)S(1)}, u32[]{:S(2)}, u32[]{:S(2)}) collective-permute-start(f32[2,96,128]{2,1,0:T(8,128)S(1)} %get-tuple-element.28), channel_id=1, source_target_pairs={{0,24},{1,25},{2,26},{3,27},{4,28},{5,29},{6,30},{7,31},{8,0},{9,1... | collective-permute-start | bytes 294920 | tf_op jit(solution)/shard_map/ppermute | solution.py:525
  9.9 0.0 collective-permute-start
  9.9 3.8 %collective-permute-start.1 = (f32[176,128]{1,0:T(8,128)S(1)}, f32[176,128]{1,0:T(8,128)S(1)}, u32[]{:S(2)}, u32[]{:S(2)}) collective-permute-start(f32[176,128]{1,0:T(8,128)S(1)} %get-tuple-element.26), channel_id=1, source_target_pairs={{0,24},{1,25},{2,26},{3,27},{4,28},{5,29},{6,30},{7,31},{8,0},{9,1... | collective-permute-start | bytes 270344 | tf_op jit(solution)/shard_map/ppermute | solution.py:525
  13.8 0.0 collective-permute-done.2.cup_ref
  13.8 1.7 %collective-permute-done.3.cdown_ref = f32[2,96,128]{2,1,0:T(8,128)S(1)} collective-permute-done((f32[2,96,128]{2,1,0:T(8,128)S(1)}, f32[2,96,128]{2,1,0:T(8,128)S(1)}, u32[]{:S(2)}, u32[]{:S(2)}) %collective-permute-start.3) | collective-permute-done | bytes 98336 | tf_op jit(solution)/shard_map/ppermute | solution.py:525
  15.5 0.1 collective-permute-start.5
  15.5 2.5 %all-gather = f32[1808,128]{1,0:T(8,128)S(1)} all-gather(f32[904,128]{1,0:T(8,128)S(1)} %get-tuple-element.31), channel_id=2, replica_groups={{0,1},{2,3},{4,5},{6,7},{8,9},{10,11},{12,13},{14,15},{16,17},{18,19},{..., dimensions={0}, use_global_device_ids=true | all-gather | bytes 1388544 | tf_op jit(solution)/shard_map/all_gather | solution.py:584
  18.0 0.0 collective-permute-done.up_ref
  18.0 0.0 collective-permute-done.1.down_ref
  18.0 0.0 collective-permute-done.4.yb_ref
  18.0 2.7 %shard_map.60 = (f32[26,328,128]{2,1,0:T(8,128)S(1)}, f32[328,128]{1,0:T(8,128)S(1)}, f32[26,328,128]{2,1,0:T(8,128)S(1)}, f32[26,328,128]{2,1,0:T(8,128)S(1)}, ...) custom-call(s32[1]{0:T(128)} %bitcast.odd_ref, ...), custom_call_target="tpu_custom_call", output_to_operand_aliasing={{0}: (1, {}), {1}: (2, {})} | custom-call | tf_op jit(solution)/shard_map/pallas_call | solution.py:591
  20.7 0.0 collective-permute-done.5.far_ref
  20.7 1.3 %shard_map.61 = (f32[16,8,128]{2,1,0:T(8,128)}, f32[3,16,8,128]{3,2,1,0:T(8,128)}, f32[16,8,128]{2,1,0:T(8,128)}, f32[26,328,128]{2,1,0:T(8,128)S(1)}, f32[328,1...) custom-call(s32[1]{0:T(128)} %bitcast.odd_ref, ...), custom_call_target="tpu_custom_call", output_to_operand_aliasing={{3}: (1, {}), {4}: (2, {}), {5}: (3, {}), {6}: (4, {})} | custom-call | tf_op jit(solution)/shard_map/pallas_call | solution.py:599
  (1 shorter events, 0.0 us)
Async XLA Ops:
  2.7 15.3 %collective-permute-start.4 = (f32[712,128]{1,0:T(8,128)S(1)}, f32[712,128]{1,0:T(8,128)S(1)}, u32[]{:S(2)}, u32[]{:S(2)}) collective-permute-start(f32[712,128]{1,0:T(8,128)S(1)} %get-tuple-element.29), channel_id=1, source_target_pairs={{0,7},{1,2},{2,1},{3,4},{4,3},{5,6},{6,5},{7,0},{8,15},{9,10},{10,... | collective-permute-start | bytes 1093640 | tf_op jit(solution)/shard_map/ppermute | solution.py:525
  6.1 7.7 %collective-permute-start.2 = (f32[2,96,128]{2,1,0:T(8,128)S(1)}, f32[2,96,128]{2,1,0:T(8,128)S(1)}, u32[]{:S(2)}, u32[]{:S(2)}) collective-permute-start(f32[2,96,128]{2,1,0:T(8,128)S(1)} %get-tuple-element.27), channel_id=1, source_target_pairs={{0,8},{1,9},{2,10},{3,11},{4,12},{5,13},{6,14},{7,15},{8,16},{9,17... | collective-permute-start | bytes 294920 | tf_op jit(solution)/shard_map/ppermute | solution.py:525
  7.7 7.8 %collective-permute-start.3 = (f32[2,96,128]{2,1,0:T(8,128)S(1)}, f32[2,96,128]{2,1,0:T(8,128)S(1)}, u32[]{:S(2)}, u32[]{:S(2)}) collective-permute-start(f32[2,96,128]{2,1,0:T(8,128)S(1)} %get-tuple-element.28), channel_id=1, source_target_pairs={{0,24},{1,25},{2,26},{3,27},{4,28},{5,29},{6,30},{7,31},{8,0},{9,1... | collective-permute-start | bytes 294920 | tf_op jit(solution)/shard_map/ppermute | solution.py:525
  9.9 8.1 %collective-permute-start = (f32[176,128]{1,0:T(8,128)S(1)}, f32[176,128]{1,0:T(8,128)S(1)}, u32[]{:S(2)}, u32[]{:S(2)}) collective-permute-start(f32[176,128]{1,0:T(8,128)S(1)} %get-tuple-element.25), channel_id=1, source_target_pairs={{0,8},{1,9},{2,10},{3,11},{4,12},{5,13},{6,14},{7,15},{8,16},{9,17... | collective-permute-start | bytes 270344 | tf_op jit(solution)/shard_map/ppermute | solution.py:525
  9.9 8.1 %collective-permute-start.1 = (f32[176,128]{1,0:T(8,128)S(1)}, f32[176,128]{1,0:T(8,128)S(1)}, u32[]{:S(2)}, u32[]{:S(2)}) collective-permute-start(f32[176,128]{1,0:T(8,128)S(1)} %get-tuple-element.26), channel_id=1, source_target_pairs={{0,24},{1,25},{2,26},{3,27},{4,28},{5,29},{6,30},{7,31},{8,0},{9,1... | collective-permute-start | bytes 270344 | tf_op jit(solution)/shard_map/ppermute | solution.py:525
  15.5 5.2 %collective-permute-start.5 = (f32[2,96,128]{2,1,0:T(8,128)S(1)}, f32[2,96,128]{2,1,0:T(8,128)S(1)}, u32[]{:S(2)}, u32[]{:S(2)}) collective-permute-start(f32[2,96,128]{2,1,0:T(8,128)S(1)} %get-tuple-element.36), channel_id=1, source_target_pairs={{0,7},{1,2},{2,1},{3,4},{4,3},{5,6},{6,5},{7,0},{8,15},{9,10},{10,... | collective-permute-start | bytes 294920 | tf_op jit(solution)/shard_map/ppermute | solution.py:525

commit v6 on v5

--- a/solution.py
+++ b/solution.py
@@ -159,16 +159,25 @@
 
 
 class Extended:
-    def __init__(self, cells_x, cells_y):
-        self.cells_x, self.cells_y = cells_x, cells_y
-        self.pitch = cells_y + 2 * HALO
-        self.rows = -(-((cells_x + 2 * HALO) * self.pitch + 16) // 8) * 8
-
+    def __init__(self, cells_x, cells_y, halo=HALO):
+        self.cells_x, self.cells_y, self.halo = cells_x, cells_y, halo
+        self.pitch = cells_y + 2 * halo
+        self.rows = -(-((cells_x + 2 * halo) * self.pitch + 16) // 8) * 8
         self.face_y_rows = len(face_y) * cells_x + 2 * len(ends_y)
         self.inner_rows = cells_y - 2 * (HALO - 1)
 
     def row(self, x, y):
-        return (x + HALO) * self.pitch + y + HALO
+        return (x + self.halo) * self.pitch + y + self.halo
+
+    def runs(self, first, count):
+        found = []
+        for k in range(count):
+            x, y = divmod(first + k, self.pitch)
+            if found and y > 0:
+                found[-1][1] += 1
+            else:
+                found.append([k, 1, x - self.halo, y - self.halo])
+        return found
 
     def inner(self, channel):
         return HALO - 1 - (all_velocity[channel][1] if channel < COUNT else 0)
@@ -301,7 +310,7 @@
             ref[pl.ds(k * ext.inner_rows, ext.inner_rows), :] = held(mirrored(c, sign, 1), where)
 
 
-def forward_kernel(cup_ref, cdown_ref, _, ya_ref, far_ref):
+def forward_kernel(cup_ref, cdown_ref, _, __, ya_ref, far_ref):
     first = ya_ref.shape[0] - 2 * CORNER_ROWS
     for side, ref in enumerate((cup_ref, cdown_ref)):
         ya_ref[pl.ds(first + side * CORNER_ROWS, CORNER_ROWS), :] = ref[0]
@@ -404,20 +413,30 @@
     return ref[c, pl.ds(start - (cx * ext.pitch + cy), count), :]
 
 
-def advance(ext, source, target, kinds_ref, first, shifted):
-    rows = pl.ds(first, 8)
+def advance(ext, source, first, kind):
     values = [arriving(ext, source, c, first, 8) for c in range(COUNT)]
-    values = collide(values[:FLOW], values[FLOW:], kinds_ref[rows, :])
+    return collide(values[:FLOW], values[FLOW:], kind)
+
+
+def second_step(ext, near, one_ref, two_ref, kinds_ref, first):
+    values = advance(ext, one_ref, first, kinds_ref[pl.ds(first, 8), :])
     lane = lax.broadcasted_iota(jnp.int32, values[0].shape, 1)
+    pieces = []
+    for offset, count, x, y in ext.runs(first, 8):
+        low, high = max(y, -near.halo), min(y + count, ext.cells_y + near.halo)
+        if low < high and -near.halo <= x < ext.cells_x + near.halo:
+            pieces.append((offset + low - y, high - low, near.row(x, low)))
 
     def store(c, value):
-        target[c, rows, :] = value
-
-    if shifted:
-        store_shifted(values, lane, store)
-    else:
-        for c in range(COUNT):
-            store(c, values[c])
+        for offset, count, row in pieces:
+            two_ref[c, pl.ds(row, count), :] = value[offset : offset + count]
+
+    store_shifted(values, lane, store)
+
+
+def third_step(near, two_ref, three_ref, kind, first):
+    for c, value in enumerate(advance(near, two_ref, first, kind)):
+        three_ref[c, pl.ds(first, 8), :] = value
 
 
 def finish(ext, source, x, density_ref, momentum_ref, concentration_ref):
@@ -446,9 +465,18 @@
     concentration_ref[x] = summed({c: 1 for c in range(FLOW, COUNT)})
 
 
-def middle_kernel(ext, odd_ref, _, __, up_ref, down_ref, cup_ref, cdown_ref, yb_ref, ya_ref,
-                  one_ref, kinds_ref, two_ref, three_ref,
-                  density_ref, momentum_ref, concentration_ref):
+def interior_kernel(ext, near, post_ref, kinds_ref, two_ref, three_ref, token_ref):
+    for x in range(1, ext.cells_x - 1):
+        second_step(ext, near, post_ref, two_ref, kinds_ref, ext.row(x, 0))
+    for x in range(2, ext.cells_x - 2):
+        kind = kinds_ref[pl.ds(ext.row(x, 0), ext.cells_y), :]
+        third_step(near, two_ref, three_ref, kind, near.row(x, 0))
+    token_ref[...] = jnp.zeros_like(token_ref)
+
+
+def middle_kernel(ext, near, odd_ref, _, __, ___, ____, up_ref, down_ref, cup_ref, cdown_ref,
+                  yb_ref, ya_ref, one_ref, kinds_ref, two_ref, three_ref,
+                  density_ref, momentum_ref, concentration_ref, near_kinds_ref):
     put = putter(one_ref, kinds_ref)
     put_inner(ext, put, up_ref, -1)
     put_inner(ext, put, down_ref, 1)
@@ -467,15 +495,32 @@
                 corners = partner.at[pl.ds(first, CORNER_ROWS)]
                 put_corner(ext, put, corners, sign_x, -pair, pair * ext.cells_y)
 
-    for source, target, width in ((one_ref, two_ref, 2), (two_ref, three_ref, 1)):
-        end = ext.row(ext.cells_x - 1 + width, ext.cells_y - 1 + width)
-        for first in range(ext.row(-width, -width), end + 1, 8):
-            advance(ext, source, target, kinds_ref, first, width > 1)
+    last_x, last_y = ext.cells_x - 1, ext.cells_y - 1
+    for space, depth in ((ext, 1), (near, 2)):
+        halo = 3 - depth
+        runs = [
+            (space.row(-halo, -halo), space.row(depth, depth - 1)),
+            (space.row(last_x - depth, last_y - depth + 1), space.row(last_x + halo, last_y + halo)),
+        ] + [
+            (space.row(x, last_y - depth + 1), space.row(x + 1, depth - 1))
+            for x in range(depth, last_x - depth)
+        ]
+        if space is near:
+            for x in range(-halo, ext.cells_x + halo):
+                for y in (-halo, last_y + halo - 7):
+                    near_kinds_ref[pl.ds(near.row(x, y), 8), :] = kinds_ref[pl.ds(ext.row(x, y), 8), :]
+        for start, end in runs:
+            for first in range(start, end + 1, 8):
+                if space is ext:
+                    second_step(ext, near, one_ref, two_ref, kinds_ref, first)
+                else:
+                    kind = near_kinds_ref[pl.ds(first, 8), :]
+                    third_step(near, two_ref, three_ref, kind, first)
     for x in range(ext.cells_x):
-        finish(ext, three_ref, x, density_ref, momentum_ref, concentration_ref)
-
-
-def last_kernel(ext, odd_ref, _, __, ___, ____, far_ref, early_density_ref, early_momentum_ref,
+        finish(near, three_ref, x, density_ref, momentum_ref, concentration_ref)
+
+
+def last_kernel(ext, near, odd_ref, _, __, ___, ____, far_ref, early_density_ref, early_momentum_ref,
                 early_concentration_ref, density_ref, momentum_ref, concentration_ref,
                 one_ref, kinds_ref, two_ref, three_ref):
     cells_x, cells_y = ext.cells_x, ext.cells_y
@@ -492,15 +537,19 @@
             far = 2 * odd_y - 1
             for side, sign_x in enumerate((-1, 1)):
                 put_corner(ext, put, far_ref.at[side], sign_x, -far, far * cells_y)
-            for source, target, width in ((one_ref, two_ref, 2), (two_ref, three_ref, 1)):
+            for width in (2, 1):
                 y = cells_y + width - 8 if far > 0 else -width
                 for k in range(HALO):
                     for x in (k - width, cells_x - 1 + width - k):
-                        advance(ext, source, target, kinds_ref, ext.row(x, y), width > 1)
+                        if width == 2:
+                            second_step(ext, near, one_ref, two_ref, kinds_ref, ext.row(x, y))
+                        else:
+                            kind = kinds_ref[pl.ds(ext.row(x, y), 8), :]
+                            third_step(near, two_ref, three_ref, kind, near.row(x, y))
 
     for k in range(HALO):
         for x in (k, cells_x - 1 - k):
-            finish(ext, three_ref, x, density_ref, momentum_ref, concentration_ref)
+            finish(near, three_ref, x, density_ref, momentum_ref, concentration_ref)
 
 
 def higher(i, count):
@@ -572,14 +621,24 @@
         yb = move(yb, move_x=None, move_y=across)
         up = move(up, move_x=higher, move_y=None)
         down = move(down, move_x=lower, move_y=None)
+        near = Extended(cells_x, cells_y, HALO - 1)
+        one = shape(COUNT, ext.rows, depth)
+        two_shape = shape(COUNT, near.rows, depth)
+        two, three, token = pl.pallas_call(
+            functools.partial(interior_kernel, ext, near),
+            out_shape=[two_shape, two_shape, shape(8, depth)],
+            in_specs=[vmem] * 2,
+            out_specs=[vmem] * 3,
+            compiler_params=params,
+        )(post, kinds)
         ya, far = pl.pallas_call(
             forward_kernel,
             out_shape=[shape(*ya.shape), shape(2, CORNER_ROWS, depth)],
-            in_specs=[vmem] * 3,
+            in_specs=[vmem] * 4,
             out_specs=[vmem] * 2,
-            input_output_aliases={2: 0},
+            input_output_aliases={3: 0},
             compiler_params=params,
-        )(cup, cdown, ya)
+        )(cup, cdown, token, ya)
         far = move(far, move_x=None, move_y=across)
         ya = lax.all_gather(ya, "gy", axis_index_groups=[[j, j + 1] for j in range(0, count_y, 2)])
         moments = [
@@ -587,18 +646,18 @@
             shape(3, cells_x, cells_y, depth),
             shape(cells_x, cells_y, depth),
         ]
-        one = shape(COUNT, ext.rows, depth)
         post, kinds, two, three, *early = pl.pallas_call(
-            functools.partial(middle_kernel, ext),
-            out_shape=[one, shape(ext.rows, depth), one, one] + moments,
-            in_specs=[smem] + [vmem] * 8,
+            functools.partial(middle_kernel, ext, near),
+            out_shape=[one, shape(ext.rows, depth), two_shape, two_shape] + moments,
+            in_specs=[smem] + [vmem] * 10,
             out_specs=[vmem] * 7,
-            input_output_aliases={1: 0, 2: 1},
+            scratch_shapes=[pltpu.VMEM((near.rows, depth), f32)],
+            input_output_aliases={1: 0, 2: 1, 3: 2, 4: 3},
             compiler_params=params,
-        )(odd, post, kinds, up, down, cup, cdown, yb, ya)
+        )(odd, post, kinds, two, three, up, down, cup, cdown, yb, ya)
         density, momentum, concentration, *_ = pl.pallas_call(
-            functools.partial(last_kernel, ext),
-            out_shape=moments + [one, shape(ext.rows, depth), one, one],
+            functools.partial(last_kernel, ext, near),
+            out_shape=moments + [one, shape(ext.rows, depth), two_shape, two_shape],
             in_specs=[smem] + [vmem] * 8,
             out_specs=[vmem] * 7,
             input_output_aliases={1: 3, 2: 4, 3: 5, 4: 6},

time: 22.2 us -> 22 us (level)
  waiting for transfers between devices: 1.7 us -> 1.24 us
  Pallas kernels: 5.99 us -> 6.24 us
    ppermute x6, waiting for transfers between devices: 1.7 us -> 1.24 us  [swapped(): return lax.ppermute(block, ('gx', 'gy'), pairs)]
    pallas_call x2 -> x3, Pallas kernels: 3.92 us -> 4.17 us  [the longest x1 2.03 us: local(): pl.pallas_call(functools.partial(middle_kernel, ext, near), out_shape=[on...]
  transfers between devices with their start and end apart: 6 -> 6, of which waited for: 1 -> 2; matrix products, arithmetic and copies ran while one was open for 0% -> 0% of each run, Pallas kernels for 12% -> 13%
where the time goes in v6:
time: 22 us; the launch traced here: 21.8 us
  starting transfers between devices  11.1 us (50%)
  Pallas kernels  6.24 us (28%)
  blocking collectives  2.47 us (11%)
  waiting for transfers between devices  1.24 us (6%)
  between operations  0.69 us (3%)
    ppermute x6, starting transfers between devices, swapped(): return lax.ppermute(block, ('gx', 'gy'), pairs)  11.1 us
    all_gather x1, blocking collectives, local(): lax.all_gather(ya, 'gy', axis_index_groups=[[j, j + 1] for j in range(0,...  2.47 us
    pallas_call x1, Pallas kernels, local(): pl.pallas_call(functools.partial(first_kernel, ext, group), out_shape=[sh...  2.06 us
    pallas_call x1, Pallas kernels, local(): pl.pallas_call(functools.partial(middle_kernel, ext, near), out_shape=[on...  2.03 us
    pallas_call x1, Pallas kernels, local(): pl.pallas_call(functools.partial(last_kernel, ext, near), out_shape=momen...  1.3 us
    ppermute x6, waiting for transfers between devices, swapped(): return lax.ppermute(block, ('gx', 'gy'), pairs)  1.24 us
    pallas_call x1, Pallas kernels, local(): pl.pallas_call(functools.partial(interior_kernel, ext, near), out_shape=[...  0.85 us
  transfers between devices with their start and end apart: 6, of which 2 were waited for; matrix products, arithmetic and copies ran while one was open for 0% of the time, Pallas kernels for 13%

profile of v6, /device:TPU:0, one launch (start us, length us, event | category | flops | bytes accessed | tf_op | source)
XLA Modules:
  0.0 21.8 jit_solution(2326379653712843934)
XLA Ops:
  0.6 2.1 %shard_map.58 = (f32[26,328,128]{2,1,0:T(8,128)S(1)}, f32[328,128]{1,0:T(8,128)S(1)}, f32[176,128]{1,0:T(8,128)S(1)}, f32[176,128]{1,0:T(8,128)S(1)}, f32[904,12...) custom-call(s32[1]{0:T(128)} %bitcast.odd_ref, ...), custom_call_target="tpu_custom_call" | custom-call | tf_op jit(solution)/shard_map/pallas_call | solution.py:595
  2.7 3.4 %collective-permute-start.4 = (f32[712,128]{1,0:T(8,128)S(1)}, f32[712,128]{1,0:T(8,128)S(1)}, u32[]{:S(2)}, u32[]{:S(2)}) collective-permute-start(f32[712,128]{1,0:T(8,128)S(1)} %get-tuple-element.34), channel_id=1, source_target_pairs={{0,7},{1,2},{2,1},{3,4},{4,3},{5,6},{6,5},{7,0},{8,15},{9,10},{10,... | collective-permute-start | bytes 1093640 | tf_op jit(solution)/shard_map/ppermute | solution.py:574
  6.1 1.6 %collective-permute-start.2 = (f32[2,96,128]{2,1,0:T(8,128)S(1)}, f32[2,96,128]{2,1,0:T(8,128)S(1)}, u32[]{:S(2)}, u32[]{:S(2)}) collective-permute-start(f32[2,96,128]{2,1,0:T(8,128)S(1)} %get-tuple-element.32), channel_id=1, source_target_pairs={{0,8},{1,9},{2,10},{3,11},{4,12},{5,13},{6,14},{7,15},{8,16},{9,17... | collective-permute-start | bytes 294920 | tf_op jit(solution)/shard_map/ppermute | solution.py:574
  7.7 2.2 %collective-permute-start.3 = (f32[2,96,128]{2,1,0:T(8,128)S(1)}, f32[2,96,128]{2,1,0:T(8,128)S(1)}, u32[]{:S(2)}, u32[]{:S(2)}) collective-permute-start(f32[2,96,128]{2,1,0:T(8,128)S(1)} %get-tuple-element.33), channel_id=1, source_target_pairs={{0,24},{1,25},{2,26},{3,27},{4,28},{5,29},{6,30},{7,31},{8,0},{9,1... | collective-permute-start | bytes 294920 | tf_op jit(solution)/shard_map/ppermute | solution.py:574
  9.9 0.0 collective-permute-start
  9.9 3.8 %collective-permute-start.1 = (f32[176,128]{1,0:T(8,128)S(1)}, f32[176,128]{1,0:T(8,128)S(1)}, u32[]{:S(2)}, u32[]{:S(2)}) collective-permute-start(f32[176,128]{1,0:T(8,128)S(1)} %get-tuple-element.31), channel_id=1, source_target_pairs={{0,24},{1,25},{2,26},{3,27},{4,28},{5,29},{6,30},{7,31},{8,0},{9,1... | collective-permute-start | bytes 270344 | tf_op jit(solution)/shard_map/ppermute | solution.py:574
  13.8 0.8 %shard_map.59 = (f32[26,256,128]{2,1,0:T(8,128)S(1)}, f32[26,256,128]{2,1,0:T(8,128)S(1)}, f32[8,128]{1,0:T(8,128)S(1)}) custom-call(f32[26,328,128]{2,1,0:T(8,128)S(1)} %get-tuple-element.26.post_ref._, f32[328,128]{1,0:T(8,128)S(1)} %get-tuple-element.27.kinds_ref.__), custom_call_target="tpu_custom_call" | custom-call | tf_op jit(solution)/shard_map/pallas_call | solution.py:627
  14.6 0.0 collective-permute-done.2.cup_ref
  14.6 0.8 %collective-permute-done.3.cdown_ref = f32[2,96,128]{2,1,0:T(8,128)S(1)} collective-permute-done((f32[2,96,128]{2,1,0:T(8,128)S(1)}, f32[2,96,128]{2,1,0:T(8,128)S(1)}, u32[]{:S(2)}, u32[]{:S(2)}) %collective-permute-start.3) | collective-permute-done | bytes 98336 | tf_op jit(solution)/shard_map/ppermute | solution.py:574
  15.5 0.1 collective-permute-start.5
  15.5 2.5 %all-gather = f32[1808,128]{1,0:T(8,128)S(1)} all-gather(f32[904,128]{1,0:T(8,128)S(1)} %get-tuple-element.37), channel_id=2, replica_groups={{0,1},{2,3},{4,5},{6,7},{8,9},{10,11},{12,13},{14,15},{16,17},{18,19},{..., dimensions={0}, use_global_device_ids=true | all-gather | bytes 1388544 | tf_op jit(solution)/shard_map/all_gather | solution.py:643
  18.0 0.0 collective-permute-done.up_ref
  18.0 0.0 collective-permute-done.1.down_ref
  18.0 0.0 collective-permute-done.4.yb_ref
  18.0 2.0 %shard_map.61 = (f32[26,328,128]{2,1,0:T(8,128)S(1)}, f32[328,128]{1,0:T(8,128)S(1)}, f32[26,256,128]{2,1,0:T(8,128)S(1)}, f32[26,256,128]{2,1,0:T(8,128)S(1)}, ...) custom-call(s32[1]{0:T(128)} %bitcast.odd_ref, ...), custom_call_target="tpu_custom_call", output_to_operand_aliasing={{0}: (1, {}), {1}: (2, {}), {2}: (3, {}), {3}: (4, {})} | custom-call | tf_op jit(solution)/shard_map/pallas_call | solution.py:649
  20.1 0.4 %collective-permute-done.5.far_ref = f32[2,96,128]{2,1,0:T(8,128)S(1)} collective-permute-done((f32[2,96,128]{2,1,0:T(8,128)S(1)}, f32[2,96,128]{2,1,0:T(8,128)S(1)}, u32[]{:S(2)}, u32[]{:S(2)}) %collective-permute-start.5) | collective-permute-done | bytes 98336 | tf_op jit(solution)/shard_map/ppermute | solution.py:574
  20.5 1.3 %shard_map.62 = (f32[16,8,128]{2,1,0:T(8,128)}, f32[3,16,8,128]{3,2,1,0:T(8,128)}, f32[16,8,128]{2,1,0:T(8,128)}, f32[26,328,128]{2,1,0:T(8,128)S(1)}, f32[328,1...) custom-call(s32[1]{0:T(128)} %bitcast.odd_ref, ...), custom_call_target="tpu_custom_call", output_to_operand_aliasing={{3}: (1, {}), {4}: (2, {}), {5}: (3, {}), {6}: (4, {})} | custom-call | tf_op jit(solution)/shard_map/pallas_call | solution.py:658
  (1 shorter events, 0.0 us)
Async XLA Ops:
  2.7 15.3 %collective-permute-start.4 = (f32[712,128]{1,0:T(8,128)S(1)}, f32[712,128]{1,0:T(8,128)S(1)}, u32[]{:S(2)}, u32[]{:S(2)}) collective-permute-start(f32[712,128]{1,0:T(8,128)S(1)} %get-tuple-element.34), channel_id=1, source_target_pairs={{0,7},{1,2},{2,1},{3,4},{4,3},{5,6},{6,5},{7,0},{8,15},{9,10},{10,... | collective-permute-start | bytes 1093640 | tf_op jit(solution)/shard_map/ppermute | solution.py:574
  6.1 8.5 %collective-permute-start.2 = (f32[2,96,128]{2,1,0:T(8,128)S(1)}, f32[2,96,128]{2,1,0:T(8,128)S(1)}, u32[]{:S(2)}, u32[]{:S(2)}) collective-permute-start(f32[2,96,128]{2,1,0:T(8,128)S(1)} %get-tuple-element.32), channel_id=1, source_target_pairs={{0,8},{1,9},{2,10},{3,11},{4,12},{5,13},{6,14},{7,15},{8,16},{9,17... | collective-permute-start | bytes 294920 | tf_op jit(solution)/shard_map/ppermute | solution.py:574
  7.7 7.8 %collective-permute-start.3 = (f32[2,96,128]{2,1,0:T(8,128)S(1)}, f32[2,96,128]{2,1,0:T(8,128)S(1)}, u32[]{:S(2)}, u32[]{:S(2)}) collective-permute-start(f32[2,96,128]{2,1,0:T(8,128)S(1)} %get-tuple-element.33), channel_id=1, source_target_pairs={{0,24},{1,25},{2,26},{3,27},{4,28},{5,29},{6,30},{7,31},{8,0},{9,1... | collective-permute-start | bytes 294920 | tf_op jit(solution)/shard_map/ppermute | solution.py:574
  9.9 8.1 %collective-permute-start = (f32[176,128]{1,0:T(8,128)S(1)}, f32[176,128]{1,0:T(8,128)S(1)}, u32[]{:S(2)}, u32[]{:S(2)}) collective-permute-start(f32[176,128]{1,0:T(8,128)S(1)} %get-tuple-element.30), channel_id=1, source_target_pairs={{0,8},{1,9},{2,10},{3,11},{4,12},{5,13},{6,14},{7,15},{8,16},{9,17... | collective-permute-start | bytes 270344 | tf_op jit(solution)/shard_map/ppermute | solution.py:574
  9.9 8.1 %collective-permute-start.1 = (f32[176,128]{1,0:T(8,128)S(1)}, f32[176,128]{1,0:T(8,128)S(1)}, u32[]{:S(2)}, u32[]{:S(2)}) collective-permute-start(f32[176,128]{1,0:T(8,128)S(1)} %get-tuple-element.31), channel_id=1, source_target_pairs={{0,24},{1,25},{2,26},{3,27},{4,28},{5,29},{6,30},{7,31},{8,0},{9,1... | collective-permute-start | bytes 270344 | tf_op jit(solution)/shard_map/ppermute | solution.py:574
  15.5 5.0 %collective-permute-start.5 = (f32[2,96,128]{2,1,0:T(8,128)S(1)}, f32[2,96,128]{2,1,0:T(8,128)S(1)}, u32[]{:S(2)}, u32[]{:S(2)}) collective-permute-start(f32[2,96,128]{2,1,0:T(8,128)S(1)} %get-tuple-element.42), channel_id=1, source_target_pairs={{0,7},{1,2},{2,1},{3,4},{4,3},{5,6},{6,5},{7,0},{8,15},{9,10},{10,... | collective-permute-start | bytes 294920 | tf_op jit(solution)/shard_map/ppermute | solution.py:574

commit v7 on v6

--- a/solution.py
+++ b/solution.py
@@ -183,29 +183,98 @@
         return HALO - 1 - (all_velocity[channel][1] if channel < COUNT else 0)
 
 
-def first_kernel(ext, group, odd_ref, flow_hbm, solute_hbm, kind_hbm, post_ref, kinds_ref,
-                 up_ref, down_ref, ya_ref, yb_ref, cup_ref, cdown_ref,
+def inside(cells, sign, d):
+    return cells - d if sign > 0 else d - 1
+
+
+def beyond(cells, sign, d):
+    return cells - 1 + d if sign > 0 else -d
+
+
+def line_x(ext, x):
+    return lambda y: pl.ds(ext.row(x, y), ext.cells_y)
+
+
+def line_y(ext, y):
+    return lambda x: pl.ds(ext.row(x, y), ext.cells_x, stride=ext.pitch)
+
+
+def reader(post_ref, kinds_ref, sums_ref):
+    def held(c, where):
+        if c > KIND:
+            return sums_ref[c - SUMS[0][0], where, :]
+        return kinds_ref[where, :] if c == KIND else post_ref[c, where, :]
+
+    return held
+
+
+def put_line_sums(axis, cells, where, post_ref, sums_ref):
+    across = 1 - axis
+    place = lax.broadcasted_iota(jnp.int32, (cells, post_ref.shape[-1]), 0)
+    parts = {}
+    for move in (0, 1, -1):
+        total = along = solute = None
+        for c in moving(axis, 0):
+            if all_velocity[c][across] != move:
+                continue
+            value = post_ref[c, where(-move), :]
+            if c >= FLOW:
+                solute = value if solute is None else solute + value
+                continue
+            total = value if total is None else total + value
+            cz = all_velocity[c][2]
+            if cz != 0:
+                signed = value if cz > 0 else -value
+                along = signed if along is None else along + signed
+        parts[move] = [total, along, solute]
+        if move != 0:
+            inside = place != (0 if move > 0 else cells - 1)
+            parts[move] = [jnp.where(inside, p, 0.0) for p in parts[move]]
+    total, along, solute = (parts[0][n] + parts[1][n] + parts[-1][n] for n in range(3))
+    for c, value in zip(
+        SUMS[axis], (total - along, parts[1][0] - parts[-1][0], along, solute)
+    ):
+        sums_ref[c - SUMS[0][0], where(0), :] = value
+
+
+def pack_face_y(ext, sign, post_ref, kinds_ref, sums_ref, ref):
+    held = reader(post_ref, kinds_ref, sums_ref)
+    put_line_sums(
+        1, ext.cells_x, line_y(ext, inside(ext.cells_y, sign, HALO - 1)), post_ref, sums_ref
+    )
+    for k, (c, d) in enumerate(face_y):
+        ref[pl.ds(k * ext.cells_x, ext.cells_x), :] = held(
+            mirrored(c, 1, sign), line_y(ext, inside(ext.cells_y, sign, d))(0)
+        )
+    for side, sign_x in enumerate((1, -1)):
+        for k, c in enumerate(ends_y):
+            row = ext.row(inside(ext.cells_x, sign_x, 1), inside(ext.cells_y, sign, HALO - 1))
+            to = len(face_y) * ext.cells_x + side * len(ends_y) + k
+            ref[pl.ds(to, 1), :] = held(mirrored(c, sign_x, 1), pl.ds(row, 1))
+
+
+def first_kernel(ext, groups, odd_ref, flow_hbm, solute_hbm, kind_hbm, post_ref, kinds_ref,
+                 up_ref, down_ref, yb_ref, cup_ref, cdown_ref,
                  flow_ref, solute_ref, kind_ref, sums_ref, sems):
     cells_x, cells_y = ext.cells_x, ext.cells_y
     depth = kind_ref.shape[-1]
     lane = lax.broadcasted_iota(jnp.int32, (cells_y, depth), 1)
-    copies = []
-    for g in range(cells_x // group):
-        planes = pl.ds(g * group, group)
-        copies.append([
-            pltpu.make_async_copy(kind_hbm.at[planes], kind_ref.at[planes], sems.at[g, 0]),
-            pltpu.make_async_copy(flow_hbm.at[:, planes], flow_ref.at[:, planes], sems.at[g, 1]),
+    copies = {}
+    for g, (first, count) in enumerate(groups):
+        planes = pl.ds(first, count)
+        copies[first] = [
+            pltpu.make_async_copy(flow_hbm.at[:, planes], flow_ref.at[:, planes], sems.at[g, 0]),
             pltpu.make_async_copy(
-                solute_hbm.at[:, planes], solute_ref.at[:, planes], sems.at[g, 2]
+                solute_hbm.at[:, planes], solute_ref.at[:, planes], sems.at[g, 1]
             ),
-        ])
-        for copy in copies[-1]:
-            copy.start()
+        ]
+    copies[0].append(pltpu.make_async_copy(kind_hbm, kind_ref, sems.at[0, 2]))
+    for copy in [copy for group in copies.values() for copy in group]:
+        copy.start()
 
     for x in range(cells_x):
-        if x % group == 0:
-            for copy in copies[x // group]:
-                copy.wait()
+        for copy in copies.get(x, []):
+            copy.wait()
         kind = kind_ref[x].astype(jnp.float32)
         rows = pl.ds(ext.row(x, 0), cells_y)
         kinds_ref[rows, :] = kind
@@ -220,105 +289,44 @@
 
         store_shifted(values, lane, store)
 
-    def sums(axis, where):
-        across = 1 - axis
-        cells = (cells_x, cells_y)[across]
-        place = lax.broadcasted_iota(jnp.int32, (cells, depth), 0)
-        parts = {}
-        for move in (0, 1, -1):
-            total = along = solute = None
-            for c in moving(axis, 0):
-                if all_velocity[c][across] != move:
-                    continue
-                value = post_ref[c, where(-move), :]
-                if c >= FLOW:
-                    solute = value if solute is None else solute + value
-                    continue
-                total = value if total is None else total + value
-                cz = all_velocity[c][2]
-                if cz != 0:
-                    signed = value if cz > 0 else -value
-                    along = signed if along is None else along + signed
-            parts[move] = [total, along, solute]
-            if move != 0:
-                inside = place != (0 if move > 0 else cells - 1)
-                parts[move] = [jnp.where(inside, p, 0.0) for p in parts[move]]
-        total, along, solute = (parts[0][n] + parts[1][n] + parts[-1][n] for n in range(3))
-        for c, value in zip(
-            SUMS[axis], (total - along, parts[1][0] - parts[-1][0], along, solute)
-        ):
-            sums_ref[c - SUMS[0][0], where(0), :] = value
-
-    def at(cells, sign, d):
-        return cells - d if sign > 0 else d - 1
-
-    def line_x(x):
-        return lambda y: pl.ds(ext.row(x, y), cells_y)
-
-    def line_y(y):
-        return lambda x: pl.ds(ext.row(x, y), cells_x, stride=ext.pitch)
-
-    zero = jnp.zeros((8, depth), jnp.float32)
-    zeros = jnp.zeros((cells_x, depth), jnp.float32)
+    held = reader(post_ref, kinds_ref, sums_ref)
     for sign in (1, -1):
-        sums(0, line_x(at(cells_x, sign, HALO - 1)))
-        sums(1, line_y(at(cells_y, sign, HALO - 1)))
-        for c in moving(0, 0):
-            first = ext.row(beyond(cells_x, sign, HALO - 1), -HALO)
-            for start in [*range(0, ext.pitch - 8, 8), ext.pitch - 8]:
-                post_ref[c, pl.ds(first + start, 8), :] = zero
-        for c in moving(1, 0):
-            post_ref[c, line_y(beyond(cells_y, sign, HALO - 1))(0), :] = zeros
-
-    def held(c, where):
-        if c > KIND:
-            return sums_ref[c - SUMS[0][0], where, :]
-        return kinds_ref[where, :] if c == KIND else post_ref[c, where, :]
-
+        put_line_sums(
+            0, cells_y, line_x(ext, inside(cells_x, sign, HALO - 1)), post_ref, sums_ref
+        )
     for odd_y in (0, 1):
 
         @pl.when(odd_ref[0] == odd_y)
         def _():
             pair = 1 - 2 * odd_y
+            pack_face_y(ext, -pair, post_ref, kinds_ref, sums_ref, yb_ref)
             for ref, sign_x in ((cup_ref, 1), (cdown_ref, -1)):
                 for side, sign_y in enumerate((pair, -pair)):
                     for k, (c, d) in enumerate(face_x):
                         y = cells_y - reach(c) if sign_y > 0 else 0
-                        where = pl.ds(ext.row(at(cells_x, sign_x, d), y), reach(c))
+                        where = pl.ds(ext.row(inside(cells_x, sign_x, d), y), reach(c))
                         ref[side, pl.ds(corner_start[k], reach(c)), :] = held(
                             mirrored(c, sign_x, sign_y), where
                         )
                     for k, c in enumerate(ends_x):
-                        row = ext.row(at(cells_x, sign_x, HALO - 1), at(cells_y, sign_y, 1))
+                        row = ext.row(
+                            inside(cells_x, sign_x, HALO - 1), inside(cells_y, sign_y, 1)
+                        )
                         ref[side, pl.ds(ENDS_START + k, 1), :] = held(
                             mirrored(c, 1, sign_y), pl.ds(row, 1)
                         )
-            for ref, sign in ((ya_ref, pair), (yb_ref, -pair)):
-                for k, (c, d) in enumerate(face_y):
-                    ref[pl.ds(k * cells_x, cells_x), :] = held(
-                        mirrored(c, 1, sign), line_y(at(cells_y, sign, d))(0)
-                    )
-                for side, sign_x in enumerate((1, -1)):
-                    for k, c in enumerate(ends_y):
-                        row = ext.row(at(cells_x, sign_x, 1), at(cells_y, sign, HALO - 1))
-                        to = len(face_y) * cells_x + side * len(ends_y) + k
-                        ref[pl.ds(to, 1), :] = held(mirrored(c, sign_x, 1), pl.ds(row, 1))
 
     for ref, sign in ((up_ref, 1), (down_ref, -1)):
         for k, (c, d) in enumerate(face_x):
-            where = pl.ds(ext.row(at(cells_x, sign, d), ext.inner(c)), ext.inner_rows)
+            where = pl.ds(ext.row(inside(cells_x, sign, d), ext.inner(c)), ext.inner_rows)
             ref[pl.ds(k * ext.inner_rows, ext.inner_rows), :] = held(mirrored(c, sign, 1), where)
 
 
-def forward_kernel(cup_ref, cdown_ref, _, __, ya_ref, far_ref):
+def forward_kernel(cup_ref, cdown_ref, _, ya_ref, far_ref):
     first = ya_ref.shape[0] - 2 * CORNER_ROWS
     for side, ref in enumerate((cup_ref, cdown_ref)):
         ya_ref[pl.ds(first + side * CORNER_ROWS, CORNER_ROWS), :] = ref[0]
         far_ref[side] = ref[1]
-
-
-def beyond(cells, sign, d):
-    return cells - 1 + d if sign > 0 else -d
 
 
 def putter(one_ref, kinds_ref):
@@ -465,19 +473,34 @@
     concentration_ref[x] = summed({c: 1 for c in range(FLOW, COUNT)})
 
 
-def interior_kernel(ext, near, post_ref, kinds_ref, two_ref, three_ref, token_ref):
+def interior_kernel(ext, near, odd_ref, post_ref, kinds_ref, two_ref, three_ref, ya_ref, sums_ref):
+    for odd_y in (0, 1):
+
+        @pl.when(odd_ref[0] == odd_y)
+        def _():
+            pack_face_y(ext, 1 - 2 * odd_y, post_ref, kinds_ref, sums_ref, ya_ref)
+
     for x in range(1, ext.cells_x - 1):
         second_step(ext, near, post_ref, two_ref, kinds_ref, ext.row(x, 0))
     for x in range(2, ext.cells_x - 2):
         kind = kinds_ref[pl.ds(ext.row(x, 0), ext.cells_y), :]
         third_step(near, two_ref, three_ref, kind, near.row(x, 0))
-    token_ref[...] = jnp.zeros_like(token_ref)
 
 
 def middle_kernel(ext, near, odd_ref, _, __, ___, ____, up_ref, down_ref, cup_ref, cdown_ref,
                   yb_ref, ya_ref, one_ref, kinds_ref, two_ref, three_ref,
                   density_ref, momentum_ref, concentration_ref, near_kinds_ref):
     put = putter(one_ref, kinds_ref)
+    cells_x, cells_y, depth = ext.cells_x, ext.cells_y, one_ref.shape[-1]
+    zero = jnp.zeros((8, depth), jnp.float32)
+    zeros = jnp.zeros((cells_x, depth), jnp.float32)
+    for sign in (1, -1):
+        for c in moving(0, 0):
+            first = ext.row(beyond(cells_x, sign, HALO - 1), -HALO)
+            for start in [*range(0, ext.pitch - 8, 8), ext.pitch - 8]:
+                put(c, pl.ds(first + start, 8), zero)
+        for c in moving(1, 0):
+            put(c, line_y(ext, beyond(cells_y, sign, HALO - 1))(0), zeros)
     put_inner(ext, put, up_ref, -1)
     put_inner(ext, put, down_ref, 1)
     for odd_y in (0, 1):
@@ -516,20 +539,31 @@
                 else:
                     kind = near_kinds_ref[pl.ds(first, 8), :]
                     third_step(near, two_ref, three_ref, kind, first)
-    for x in range(ext.cells_x):
+    for x in range(HALO, ext.cells_x - HALO):
         finish(near, three_ref, x, density_ref, momentum_ref, concentration_ref)
 
 
 def last_kernel(ext, near, odd_ref, _, __, ___, ____, far_ref, early_density_ref, early_momentum_ref,
-                early_concentration_ref, density_ref, momentum_ref, concentration_ref,
-                one_ref, kinds_ref, two_ref, three_ref):
+                early_concentration_ref, density_hbm, momentum_hbm, concentration_hbm,
+                one_ref, kinds_ref, two_ref, three_ref,
+                density_ref, momentum_ref, concentration_ref, sems):
     cells_x, cells_y = ext.cells_x, ext.cells_y
     put = putter(one_ref, kinds_ref)
-    for x in range(HALO, cells_x - HALO):
-        density_ref[x] = early_density_ref[x]
-        for axis in range(3):
-            momentum_ref[axis, x] = early_momentum_ref[axis, x]
-        concentration_ref[x] = early_concentration_ref[x]
+    copies = []
+
+    def send(planes, density, momentum, concentration):
+        for source, target in (
+            (density.at[planes], density_hbm.at[planes]),
+            (momentum.at[:, planes], momentum_hbm.at[:, planes]),
+            (concentration.at[planes], concentration_hbm.at[planes]),
+        ):
+            copies.append(pltpu.make_async_copy(source, target, sems.at[len(copies)]))
+            copies[-1].start()
+
+    send(
+        pl.ds(HALO, cells_x - 2 * HALO),
+        early_density_ref, early_momentum_ref, early_concentration_ref,
+    )
     for odd_y in (0, 1):
 
         @pl.when(odd_ref[0] == odd_y)
@@ -547,9 +581,12 @@
                             kind = kinds_ref[pl.ds(ext.row(x, y), 8), :]
                             third_step(near, two_ref, three_ref, kind, near.row(x, y))
 
-    for k in range(HALO):
-        for x in (k, cells_x - 1 - k):
+    for first in (0, cells_x - HALO):
+        for x in range(first, first + HALO):
             finish(near, three_ref, x, density_ref, momentum_ref, concentration_ref)
+        send(pl.ds(first, HALO), density_ref, momentum_ref, concentration_ref)
+    for copy in copies:
+        copy.wait()
 
 
 def higher(i, count):
@@ -588,30 +625,30 @@
         params = pltpu.CompilerParams(vmem_limit_bytes=16 * 1024 * 1024)
         odd = jnp.reshape(lax.axis_index("gy") % 2, (1,)).astype(jnp.int32)
         ext = Extended(cells_x, cells_y)
-        group = math.gcd(cells_x, 4)
+        split = cells_x * 5 // 8
+        groups = [(0, split), (split, cells_x - split)]
         flow, solute, kind = (
             pltpu.with_memory_space_constraint(a, pltpu.HBM) for a in (flow, solute, kind)
         )
-        post, kinds, up, down, ya, yb, cup, cdown = pl.pallas_call(
-            functools.partial(first_kernel, ext, group),
+        post, kinds, up, down, yb, cup, cdown = pl.pallas_call(
+            functools.partial(first_kernel, ext, groups),
             out_shape=[
                 shape(COUNT, ext.rows, depth),
                 shape(ext.rows, depth),
                 shape(len(face_x) * ext.inner_rows, depth),
                 shape(len(face_x) * ext.inner_rows, depth),
-                shape(ext.face_y_rows + 2 * CORNER_ROWS, depth),
                 shape(ext.face_y_rows, depth),
                 shape(2, CORNER_ROWS, depth),
                 shape(2, CORNER_ROWS, depth),
             ],
             in_specs=[smem, hbm, hbm, hbm],
-            out_specs=[vmem] * 8,
+            out_specs=[vmem] * 7,
             scratch_shapes=[
                 pltpu.VMEM(flow.shape, f32),
                 pltpu.VMEM(solute.shape, f32),
                 pltpu.VMEM(kind.shape, kind.dtype),
                 pltpu.VMEM((8, ext.rows, depth), f32),
-                pltpu.SemaphoreType.DMA((cells_x // group, 3)),
+                pltpu.SemaphoreType.DMA((len(groups), 3)),
             ],
             compiler_params=params,
         )(odd, flow, solute, kind)
@@ -624,21 +661,22 @@
         near = Extended(cells_x, cells_y, HALO - 1)
         one = shape(COUNT, ext.rows, depth)
         two_shape = shape(COUNT, near.rows, depth)
-        two, three, token = pl.pallas_call(
+        two, three, ya = pl.pallas_call(
             functools.partial(interior_kernel, ext, near),
-            out_shape=[two_shape, two_shape, shape(8, depth)],
-            in_specs=[vmem] * 2,
+            out_shape=[two_shape, two_shape, shape(ext.face_y_rows + 2 * CORNER_ROWS, depth)],
+            in_specs=[smem] + [vmem] * 2,
             out_specs=[vmem] * 3,
+            scratch_shapes=[pltpu.VMEM((8, ext.rows, depth), f32)],
             compiler_params=params,
-        )(post, kinds)
+        )(odd, post, kinds)
         ya, far = pl.pallas_call(
             forward_kernel,
             out_shape=[shape(*ya.shape), shape(2, CORNER_ROWS, depth)],
-            in_specs=[vmem] * 4,
+            in_specs=[vmem] * 3,
             out_specs=[vmem] * 2,
-            input_output_aliases={3: 0},
+            input_output_aliases={2: 0},
             compiler_params=params,
-        )(cup, cdown, token, ya)
+        )(cup, cdown, ya)
         far = move(far, move_x=None, move_y=across)
         ya = lax.all_gather(ya, "gy", axis_index_groups=[[j, j + 1] for j in range(0, count_y, 2)])
         moments = [
@@ -659,7 +697,9 @@
             functools.partial(last_kernel, ext, near),
             out_shape=moments + [one, shape(ext.rows, depth), two_shape, two_shape],
             in_specs=[smem] + [vmem] * 8,
-            out_specs=[vmem] * 7,
+            out_specs=[hbm] * 3 + [vmem] * 4,
+            scratch_shapes=[pltpu.VMEM(m.shape, f32) for m in moments]
+            + [pltpu.SemaphoreType.DMA((9,))],
             input_output_aliases={1: 3, 2: 4, 3: 5, 4: 6},
             compiler_params=params,
         )(odd, post, kinds, two, three, far, *early)

time: 22 us -> 21.8 us (level)
  no operation moved by 1% of the time
where the time goes in v7:
time: 21.8 us; the launch traced here: 21.7 us
  starting transfers between devices  11.1 us (51%)
  Pallas kernels  6.07 us (28%)
  blocking collectives  2.47 us (11%)
  waiting for transfers between devices  1.29 us (6%)
  between operations  0.69 us (3%)
    ppermute x6, starting transfers between devices, swapped(): return lax.ppermute(block, ('gx', 'gy'), pairs)  11.1 us
    all_gather x1, blocking collectives, local(): lax.all_gather(ya, 'gy', axis_index_groups=[[j, j + 1] for j in range(0,...  2.47 us
    pallas_call x1, Pallas kernels, local(): pl.pallas_call(functools.partial(first_kernel, ext, groups), out_shape=[s...  1.97 us
    pallas_call x1, Pallas kernels, local(): pl.pallas_call(functools.partial(middle_kernel, ext, near), out_shape=[on...  1.95 us
    ppermute x6, waiting for transfers between devices, swapped(): return lax.ppermute(block, ('gx', 'gy'), pairs)  1.29 us
    pallas_call x1, Pallas kernels, local(): pl.pallas_call(functools.partial(last_kernel, ext, near), out_shape=momen...  1.26 us
    pallas_call x1, Pallas kernels, local(): pl.pallas_call(functools.partial(interior_kernel, ext, near), out_shape=[...  0.87 us
  transfers between devices with their start and end apart: 6, of which 2 were waited for; matrix products, arithmetic and copies ran while one was open for 0% of the time, Pallas kernels for 13%

profile of v7, /device:TPU:0, one launch (start us, length us, event | category | flops | bytes accessed | tf_op | source)
XLA Modules:
  0.0 21.7 jit_solution(10445587388750250959)
XLA Ops:
  0.6 2.0 %shard_map.58 = (f32[26,328,128]{2,1,0:T(8,128)S(1)}, f32[328,128]{1,0:T(8,128)S(1)}, f32[176,128]{1,0:T(8,128)S(1)}, f32[176,128]{1,0:T(8,128)S(1)}, f32[712,12...) custom-call(s32[1]{0:T(128)} %bitcast.odd_ref, f32[19,16,8,128]{3,2,1,0:T(8,128)} %flow_hbm.1, ...), custom_call_target="tpu_custom_call" | custom-call | tf_op jit(solution)/shard_map/pallas_call | solution.py:633
  2.6 3.4 %collective-permute-start.4 = (f32[712,128]{1,0:T(8,128)S(1)}, f32[712,128]{1,0:T(8,128)S(1)}, u32[]{:S(2)}, u32[]{:S(2)}) collective-permute-start(f32[712,128]{1,0:T(8,128)S(1)} %get-tuple-element.33), channel_id=1, source_target_pairs={{0,7},{1,2},{2,1},{3,4},{4,3},{5,6},{6,5},{7,0},{8,15},{9,10},{10,... | collective-permute-start | bytes 1093640 | tf_op jit(solution)/shard_map/ppermute | solution.py:611
  6.0 1.6 %collective-permute-start.2 = (f32[2,96,128]{2,1,0:T(8,128)S(1)}, f32[2,96,128]{2,1,0:T(8,128)S(1)}, u32[]{:S(2)}, u32[]{:S(2)}) collective-permute-start(f32[2,96,128]{2,1,0:T(8,128)S(1)} %get-tuple-element.31), channel_id=1, source_target_pairs={{0,8},{1,9},{2,10},{3,11},{4,12},{5,13},{6,14},{7,15},{8,16},{9,17... | collective-permute-start | bytes 294920 | tf_op jit(solution)/shard_map/ppermute | solution.py:611
  7.6 2.2 %collective-permute-start.3 = (f32[2,96,128]{2,1,0:T(8,128)S(1)}, f32[2,96,128]{2,1,0:T(8,128)S(1)}, u32[]{:S(2)}, u32[]{:S(2)}) collective-permute-start(f32[2,96,128]{2,1,0:T(8,128)S(1)} %get-tuple-element.32), channel_id=1, source_target_pairs={{0,24},{1,25},{2,26},{3,27},{4,28},{5,29},{6,30},{7,31},{8,0},{9,1... | collective-permute-start | bytes 294920 | tf_op jit(solution)/shard_map/ppermute | solution.py:611
  9.9 0.0 collective-permute-start
  9.9 3.8 %collective-permute-start.1 = (f32[176,128]{1,0:T(8,128)S(1)}, f32[176,128]{1,0:T(8,128)S(1)}, u32[]{:S(2)}, u32[]{:S(2)}) collective-permute-start(f32[176,128]{1,0:T(8,128)S(1)} %get-tuple-element.30), channel_id=1, source_target_pairs={{0,24},{1,25},{2,26},{3,27},{4,28},{5,29},{6,30},{7,31},{8,0},{9,1... | collective-permute-start | bytes 270344 | tf_op jit(solution)/shard_map/ppermute | solution.py:611
  13.7 0.9 %shard_map.59 = (f32[26,256,128]{2,1,0:T(8,128)S(1)}, f32[26,256,128]{2,1,0:T(8,128)S(1)}, f32[904,128]{1,0:T(8,128)S(1)}) custom-call(s32[1]{0:T(128)} %bitcast.odd_ref, f32[26,328,128]{2,1,0:T(8,128)S(1)} %get-tuple-element.25.post_ref._, f32[328,128]{1,0:T(8,128)S(1)} %get-tuple-element.26.kinds_ref.__), custom_call_target="tpu_custom_call" | custom-call | tf_op jit(solution)/shard_map/pallas_call | solution.py:664
  14.6 0.0 collective-permute-done.2.cup_ref
  14.6 0.8 %collective-permute-done.3.cdown_ref = f32[2,96,128]{2,1,0:T(8,128)S(1)} collective-permute-done((f32[2,96,128]{2,1,0:T(8,128)S(1)}, f32[2,96,128]{2,1,0:T(8,128)S(1)}, u32[]{:S(2)}, u32[]{:S(2)}) %collective-permute-start.3) | collective-permute-done | bytes 98336 | tf_op jit(solution)/shard_map/ppermute | solution.py:611
  15.4 0.1 collective-permute-start.5
  15.5 2.5 %all-gather = f32[1808,128]{1,0:T(8,128)S(1)} all-gather(f32[904,128]{1,0:T(8,128)S(1)} %get-tuple-element.35), channel_id=2, replica_groups={{0,1},{2,3},{4,5},{6,7},{8,9},{10,11},{12,13},{14,15},{16,17},{18,19},{..., dimensions={0}, use_global_device_ids=true | all-gather | bytes 1388544 | tf_op jit(solution)/shard_map/all_gather | solution.py:681
  17.9 0.0 collective-permute-done.up_ref
  17.9 0.0 collective-permute-done.1.down_ref
  17.9 0.0 collective-permute-done.4.yb_ref
  17.9 1.9 %shard_map.61 = (f32[26,328,128]{2,1,0:T(8,128)S(1)}, f32[328,128]{1,0:T(8,128)S(1)}, f32[26,256,128]{2,1,0:T(8,128)S(1)}, f32[26,256,128]{2,1,0:T(8,128)S(1)}, ...) custom-call(s32[1]{0:T(128)} %bitcast.odd_ref, ...), custom_call_target="tpu_custom_call", output_to_operand_aliasing={{0}: (1, {}), {1}: (2, {}), {2}: (3, {}), {3}: (4, {})} | custom-call | tf_op jit(solution)/shard_map/pallas_call | solution.py:687
  19.9 0.5 %collective-permute-done.5.far_ref = f32[2,96,128]{2,1,0:T(8,128)S(1)} collective-permute-done((f32[2,96,128]{2,1,0:T(8,128)S(1)}, f32[2,96,128]{2,1,0:T(8,128)S(1)}, u32[]{:S(2)}, u32[]{:S(2)}) %collective-permute-start.5) | collective-permute-done | bytes 98336 | tf_op jit(solution)/shard_map/ppermute | solution.py:611
  20.4 1.3 %shard_map.62 = (f32[16,8,128]{2,1,0:T(8,128)}, f32[3,16,8,128]{3,2,1,0:T(8,128)}, f32[16,8,128]{2,1,0:T(8,128)}, f32[26,328,128]{2,1,0:T(8,128)S(1)}, f32[328,1...) custom-call(s32[1]{0:T(128)} %bitcast.odd_ref, ...), custom_call_target="tpu_custom_call", output_to_operand_aliasing={{3}: (1, {}), {4}: (2, {}), {5}: (3, {}), {6}: (4, {})} | custom-call | tf_op jit(solution)/shard_map/pallas_call | solution.py:696
  (1 shorter events, 0.0 us)
Async XLA Ops:
  2.6 15.3 %collective-permute-start.4 = (f32[712,128]{1,0:T(8,128)S(1)}, f32[712,128]{1,0:T(8,128)S(1)}, u32[]{:S(2)}, u32[]{:S(2)}) collective-permute-start(f32[712,128]{1,0:T(8,128)S(1)} %get-tuple-element.33), channel_id=1, source_target_pairs={{0,7},{1,2},{2,1},{3,4},{4,3},{5,6},{6,5},{7,0},{8,15},{9,10},{10,... | collective-permute-start | bytes 1093640 | tf_op jit(solution)/shard_map/ppermute | solution.py:611
  6.0 8.5 %collective-permute-start.2 = (f32[2,96,128]{2,1,0:T(8,128)S(1)}, f32[2,96,128]{2,1,0:T(8,128)S(1)}, u32[]{:S(2)}, u32[]{:S(2)}) collective-permute-start(f32[2,96,128]{2,1,0:T(8,128)S(1)} %get-tuple-element.31), channel_id=1, source_target_pairs={{0,8},{1,9},{2,10},{3,11},{4,12},{5,13},{6,14},{7,15},{8,16},{9,17... | collective-permute-start | bytes 294920 | tf_op jit(solution)/shard_map/ppermute | solution.py:611
  7.6 7.8 %collective-permute-start.3 = (f32[2,96,128]{2,1,0:T(8,128)S(1)}, f32[2,96,128]{2,1,0:T(8,128)S(1)}, u32[]{:S(2)}, u32[]{:S(2)}) collective-permute-start(f32[2,96,128]{2,1,0:T(8,128)S(1)} %get-tuple-element.32), channel_id=1, source_target_pairs={{0,24},{1,25},{2,26},{3,27},{4,28},{5,29},{6,30},{7,31},{8,0},{9,1... | collective-permute-start | bytes 294920 | tf_op jit(solution)/shard_map/ppermute | solution.py:611
  9.9 8.1 %collective-permute-start = (f32[176,128]{1,0:T(8,128)S(1)}, f32[176,128]{1,0:T(8,128)S(1)}, u32[]{:S(2)}, u32[]{:S(2)}) collective-permute-start(f32[176,128]{1,0:T(8,128)S(1)} %get-tuple-element.29), channel_id=1, source_target_pairs={{0,8},{1,9},{2,10},{3,11},{4,12},{5,13},{6,14},{7,15},{8,16},{9,17... | collective-permute-start | bytes 270344 | tf_op jit(solution)/shard_map/ppermute | solution.py:611
  9.9 8.1 %collective-permute-start.1 = (f32[176,128]{1,0:T(8,128)S(1)}, f32[176,128]{1,0:T(8,128)S(1)}, u32[]{:S(2)}, u32[]{:S(2)}) collective-permute-start(f32[176,128]{1,0:T(8,128)S(1)} %get-tuple-element.30), channel_id=1, source_target_pairs={{0,24},{1,25},{2,26},{3,27},{4,28},{5,29},{6,30},{7,31},{8,0},{9,1... | collective-permute-start | bytes 270344 | tf_op jit(solution)/shard_map/ppermute | solution.py:611
  15.4 5.0 %collective-permute-start.5 = (f32[2,96,128]{2,1,0:T(8,128)S(1)}, f32[2,96,128]{2,1,0:T(8,128)S(1)}, u32[]{:S(2)}, u32[]{:S(2)}) collective-permute-start(f32[2,96,128]{2,1,0:T(8,128)S(1)} %get-tuple-element.40), channel_id=1, source_target_pairs={{0,7},{1,2},{2,1},{3,4},{4,3},{5,6},{6,5},{7,0},{8,15},{9,10},{10,... | collective-permute-start | bytes 294920 | tf_op jit(solution)/shard_map/ppermute | solution.py:611

commit v8 on v7

--- a/solution.py
+++ b/solution.py
@@ -82,7 +82,7 @@
 
 corner_start = [sum(reach(c) for c, _ in face_x[:k]) for k in range(len(face_x) + 1)]
 ENDS_START = corner_start[-1]
-CORNER_ROWS = -(-(ENDS_START + len(ends_x)) // 8) * 8
+CORNER_ROWS = ENDS_START + len(ends_x)
 FACE_X_SUMS = face_x.index((SUMS[0][0], HALO - 1))
 FACE_Y_SUMS = face_y.index((SUMS[1][0], HALO - 1))
 
@@ -305,14 +305,14 @@
                     for k, (c, d) in enumerate(face_x):
                         y = cells_y - reach(c) if sign_y > 0 else 0
                         where = pl.ds(ext.row(inside(cells_x, sign_x, d), y), reach(c))
-                        ref[side, pl.ds(corner_start[k], reach(c)), :] = held(
+                        ref[pl.ds(side * CORNER_ROWS + corner_start[k], reach(c)), :] = held(
                             mirrored(c, sign_x, sign_y), where
                         )
                     for k, c in enumerate(ends_x):
                         row = ext.row(
                             inside(cells_x, sign_x, HALO - 1), inside(cells_y, sign_y, 1)
                         )
-                        ref[side, pl.ds(ENDS_START + k, 1), :] = held(
+                        ref[pl.ds(side * CORNER_ROWS + ENDS_START + k, 1), :] = held(
                             mirrored(c, 1, sign_y), pl.ds(row, 1)
                         )
 
@@ -325,8 +325,9 @@
 def forward_kernel(cup_ref, cdown_ref, _, ya_ref, far_ref):
     first = ya_ref.shape[0] - 2 * CORNER_ROWS
     for side, ref in enumerate((cup_ref, cdown_ref)):
-        ya_ref[pl.ds(first + side * CORNER_ROWS, CORNER_ROWS), :] = ref[0]
-        far_ref[side] = ref[1]
+        rows = pl.ds(side * CORNER_ROWS, CORNER_ROWS)
+        ya_ref[pl.ds(first + side * CORNER_ROWS, CORNER_ROWS), :] = ref[pl.ds(0, CORNER_ROWS), :]
+        far_ref[rows, :] = ref[pl.ds(CORNER_ROWS, CORNER_ROWS), :]
 
 
 def putter(one_ref, kinds_ref):
@@ -349,7 +350,7 @@
     put(FLOW, rows, solute)
 
 
-def put_corner(ext, put, ref, sign_x, sign_y, origin):
+def put_corner(ext, put, ref, base, sign_x, sign_y, origin):
     for k, (c, d) in enumerate(face_x):
         x = beyond(ext.cells_x, sign_x, d)
         y = origin + (ext.cells_y - reach(c) if sign_y > 0 else 0)
@@ -357,17 +358,17 @@
             put(
                 mirrored(c, -sign_x, sign_y),
                 pl.ds(ext.row(x, y), reach(c)),
-                ref[pl.ds(corner_start[k], reach(c)), :],
+                ref[pl.ds(base + corner_start[k], reach(c)), :],
             )
         elif k == FACE_X_SUMS:
             for n in range(reach(c)):
-                values = [ref[pl.ds(corner_start[k + i] + n, 1), :] for i in range(4)]
+                values = [ref[pl.ds(base + corner_start[k + i] + n, 1), :] for i in range(4)]
                 carry = 1 if y + n < 0 or y + n == ext.cells_y - 1 else -1
                 put_sums(ext, put, x, y + n, 1, values, carry)
     x = beyond(ext.cells_x, sign_x, HALO - 1)
     y = origin + (ext.cells_y - 1 if sign_y > 0 else 0)
     for k, c in enumerate(ends_x):
-        put(mirrored(c, 1, sign_y), pl.ds(ext.row(x, y), 1), ref[pl.ds(ENDS_START + k, 1), :])
+        put(mirrored(c, 1, sign_y), pl.ds(ext.row(x, y), 1), ref[pl.ds(base + ENDS_START + k, 1), :])
 
 
 def put_inner(ext, put, ref, sign_x):
@@ -512,11 +513,10 @@
             put_face_y(ext, put, yb_ref, -pair)
             put_face_y(ext, put, partner, pair)
             for side, (ref, sign_x) in enumerate(((cup_ref, -1), (cdown_ref, 1))):
-                put_corner(ext, put, ref.at[0], sign_x, pair, 0)
-                put_corner(ext, put, ref.at[1], sign_x, -pair, 0)
+                put_corner(ext, put, ref, 0, sign_x, pair, 0)
+                put_corner(ext, put, ref, CORNER_ROWS, sign_x, -pair, 0)
                 first = partner.shape[0] - (2 - side) * CORNER_ROWS
-                corners = partner.at[pl.ds(first, CORNER_ROWS)]
-                put_corner(ext, put, corners, sign_x, -pair, pair * ext.cells_y)
+                put_corner(ext, put, partner, first, sign_x, -pair, pair * ext.cells_y)
 
     last_x, last_y = ext.cells_x - 1, ext.cells_y - 1
     for space, depth in ((ext, 1), (near, 2)):
@@ -570,7 +570,9 @@
         def _():
             far = 2 * odd_y - 1
             for side, sign_x in enumerate((-1, 1)):
-                put_corner(ext, put, far_ref.at[side], sign_x, -far, far * cells_y)
+                put_corner(
+                    ext, put, far_ref, side * CORNER_ROWS, sign_x, -far, far * cells_y
+                )
             for width in (2, 1):
                 y = cells_y + width - 8 if far > 0 else -width
                 for k in range(HALO):
@@ -638,8 +640,8 @@
                 shape(len(face_x) * ext.inner_rows, depth),
                 shape(len(face_x) * ext.inner_rows, depth),
                 shape(ext.face_y_rows, depth),
-                shape(2, CORNER_ROWS, depth),
-                shape(2, CORNER_ROWS, depth),
+                shape(2 * CORNER_ROWS, depth),
+                shape(2 * CORNER_ROWS, depth),
             ],
             in_specs=[smem, hbm, hbm, hbm],
             out_specs=[vmem] * 7,
@@ -671,7 +673,7 @@
         )(odd, post, kinds)
         ya, far = pl.pallas_call(
             forward_kernel,
-            out_shape=[shape(*ya.shape), shape(2, CORNER_ROWS, depth)],
+            out_shape=[shape(*ya.shape), shape(2 * CORNER_ROWS, depth)],
             in_specs=[vmem] * 3,
             out_specs=[vmem] * 2,
             input_output_aliases={2: 0},

time: 21.8 us -> 21.6 us (level)
  no operation moved by 1% of the time
where the time goes in v8:
time: 21.6 us; the launch traced here: 21.5 us
  starting transfers between devices  11.1 us (51%)
  Pallas kernels  6.08 us (28%)
  blocking collectives  2.46 us (11%)
  waiting for transfers between devices  1.09 us (5%)
  between operations  0.69 us (3%)
    ppermute x6, starting transfers between devices, swapped(): return lax.ppermute(block, ('gx', 'gy'), pairs)  11.1 us
    all_gather x1, blocking collectives, local(): lax.all_gather(ya, 'gy', axis_index_groups=[[j, j + 1] for j in range(0,...  2.46 us
    pallas_call x1, Pallas kernels, local(): pl.pallas_call(functools.partial(first_kernel, ext, groups), out_shape=[s...  1.97 us
    pallas_call x1, Pallas kernels, local(): pl.pallas_call(functools.partial(middle_kernel, ext, near), out_shape=[on...  1.95 us
    pallas_call x1, Pallas kernels, local(): pl.pallas_call(functools.partial(last_kernel, ext, near), out_shape=momen...  1.26 us
    ppermute x6, waiting for transfers between devices, swapped(): return lax.ppermute(block, ('gx', 'gy'), pairs)  1.09 us
    pallas_call x1, Pallas kernels, local(): pl.pallas_call(functools.partial(interior_kernel, ext, near), out_shape=[...  0.87 us
  transfers between devices with their start and end apart: 6, of which 2 were waited for; matrix products, arithmetic and copies ran while one was open for 0% of the time, Pallas kernels for 13%

profile of v8, /device:TPU:0, one launch (start us, length us, event | category | flops | bytes accessed | tf_op | source)
XLA Modules:
  0.0 21.5 jit_solution(8025327636601760266)
XLA Ops:
  0.6 2.0 %shard_map.58 = (f32[26,328,128]{2,1,0:T(8,128)S(1)}, f32[328,128]{1,0:T(8,128)S(1)}, f32[176,128]{1,0:T(8,128)S(1)}, f32[176,128]{1,0:T(8,128)S(1)}, f32[712,12...) custom-call(s32[1]{0:T(128)} %bitcast.odd_ref, f32[19,16,8,128]{3,2,1,0:T(8,128)} %flow_hbm.1, ...), custom_call_target="tpu_custom_call" | custom-call | tf_op jit(solution)/shard_map/pallas_call | solution.py:635
  2.6 3.4 %collective-permute-start.4 = (f32[712,128]{1,0:T(8,128)S(1)}, f32[712,128]{1,0:T(8,128)S(1)}, u32[]{:S(2)}, u32[]{:S(2)}) collective-permute-start(f32[712,128]{1,0:T(8,128)S(1)} %get-tuple-element.33), channel_id=1, source_target_pairs={{0,7},{1,2},{2,1},{3,4},{4,3},{5,6},{6,5},{7,0},{8,15},{9,10},{10,... | collective-permute-start | bytes 1093640 | tf_op jit(solution)/shard_map/ppermute | solution.py:613
  6.0 1.6 %collective-permute-start.2 = (f32[184,128]{1,0:T(8,128)S(1)}, f32[184,128]{1,0:T(8,128)S(1)}, u32[]{:S(2)}, u32[]{:S(2)}) collective-permute-start(f32[184,128]{1,0:T(8,128)S(1)} %get-tuple-element.31), channel_id=1, source_target_pairs={{0,8},{1,9},{2,10},{3,11},{4,12},{5,13},{6,14},{7,15},{8,16},{9,17... | collective-permute-start | bytes 282632 | tf_op jit(solution)/shard_map/ppermute | solution.py:613
  7.6 2.2 %collective-permute-start.3 = (f32[184,128]{1,0:T(8,128)S(1)}, f32[184,128]{1,0:T(8,128)S(1)}, u32[]{:S(2)}, u32[]{:S(2)}) collective-permute-start(f32[184,128]{1,0:T(8,128)S(1)} %get-tuple-element.32), channel_id=1, source_target_pairs={{0,24},{1,25},{2,26},{3,27},{4,28},{5,29},{6,30},{7,31},{8,0},{9,1... | collective-permute-start | bytes 282632 | tf_op jit(solution)/shard_map/ppermute | solution.py:613
  9.9 0.0 collective-permute-start
  9.9 3.8 %collective-permute-start.1 = (f32[176,128]{1,0:T(8,128)S(1)}, f32[176,128]{1,0:T(8,128)S(1)}, u32[]{:S(2)}, u32[]{:S(2)}) collective-permute-start(f32[176,128]{1,0:T(8,128)S(1)} %get-tuple-element.30), channel_id=1, source_target_pairs={{0,24},{1,25},{2,26},{3,27},{4,28},{5,29},{6,30},{7,31},{8,0},{9,1... | collective-permute-start | bytes 270344 | tf_op jit(solution)/shard_map/ppermute | solution.py:613
  13.7 0.9 %shard_map.59 = (f32[26,256,128]{2,1,0:T(8,128)S(1)}, f32[26,256,128]{2,1,0:T(8,128)S(1)}, f32[896,128]{1,0:T(8,128)S(1)}) custom-call(s32[1]{0:T(128)} %bitcast.odd_ref, f32[26,328,128]{2,1,0:T(8,128)S(1)} %get-tuple-element.25.post_ref._, f32[328,128]{1,0:T(8,128)S(1)} %get-tuple-element.26.kinds_ref.__), custom_call_target="tpu_custom_call" | custom-call | tf_op jit(solution)/shard_map/pallas_call | solution.py:666
  14.6 0.0 collective-permute-done.2.cup_ref
  14.6 0.6 %collective-permute-done.3.cdown_ref = f32[184,128]{1,0:T(8,128)S(1)} collective-permute-done((f32[184,128]{1,0:T(8,128)S(1)}, f32[184,128]{1,0:T(8,128)S(1)}, u32[]{:S(2)}, u32[]{:S(2)}) %collective-permute-start.3) | collective-permute-done | bytes 94240 | tf_op jit(solution)/shard_map/ppermute | solution.py:613
  15.2 0.1 collective-permute-start.5
  15.3 2.5 %all-gather = f32[1792,128]{1,0:T(8,128)S(1)} all-gather(f32[896,128]{1,0:T(8,128)S(1)} %get-tuple-element.35), channel_id=2, replica_groups={{0,1},{2,3},{4,5},{6,7},{8,9},{10,11},{12,13},{14,15},{16,17},{18,19},{..., dimensions={0}, use_global_device_ids=true | all-gather | bytes 1376256 | tf_op jit(solution)/shard_map/all_gather | solution.py:683
  17.8 0.0 collective-permute-done.up_ref
  17.8 0.0 collective-permute-done.1.down_ref
  17.8 0.0 collective-permute-done.4.yb_ref
  17.8 2.0 %shard_map.61 = (f32[26,328,128]{2,1,0:T(8,128)S(1)}, f32[328,128]{1,0:T(8,128)S(1)}, f32[26,256,128]{2,1,0:T(8,128)S(1)}, f32[26,256,128]{2,1,0:T(8,128)S(1)}, ...) custom-call(s32[1]{0:T(128)} %bitcast.odd_ref, ...), custom_call_target="tpu_custom_call", output_to_operand_aliasing={{0}: (1, {}), {1}: (2, {}), {2}: (3, {}), {3}: (4, {})} | custom-call | tf_op jit(solution)/shard_map/pallas_call | solution.py:689
  19.7 0.4 %collective-permute-done.5.far_ref = f32[184,128]{1,0:T(8,128)S(1)} collective-permute-done((f32[184,128]{1,0:T(8,128)S(1)}, f32[184,128]{1,0:T(8,128)S(1)}, u32[]{:S(2)}, u32[]{:S(2)}) %collective-permute-start.5) | collective-permute-done | bytes 94240 | tf_op jit(solution)/shard_map/ppermute | solution.py:613
  20.2 1.3 %shard_map.62 = (f32[16,8,128]{2,1,0:T(8,128)}, f32[3,16,8,128]{3,2,1,0:T(8,128)}, f32[16,8,128]{2,1,0:T(8,128)}, f32[26,328,128]{2,1,0:T(8,128)S(1)}, f32[328,1...) custom-call(s32[1]{0:T(128)} %bitcast.odd_ref, ...), custom_call_target="tpu_custom_call", output_to_operand_aliasing={{3}: (1, {}), {4}: (2, {}), {5}: (3, {}), {6}: (4, {})} | custom-call | tf_op jit(solution)/shard_map/pallas_call | solution.py:698
  (1 shorter events, 0.0 us)
Async XLA Ops:
  2.6 15.2 %collective-permute-start.4 = (f32[712,128]{1,0:T(8,128)S(1)}, f32[712,128]{1,0:T(8,128)S(1)}, u32[]{:S(2)}, u32[]{:S(2)}) collective-permute-start(f32[712,128]{1,0:T(8,128)S(1)} %get-tuple-element.33), channel_id=1, source_target_pairs={{0,7},{1,2},{2,1},{3,4},{4,3},{5,6},{6,5},{7,0},{8,15},{9,10},{10,... | collective-permute-start | bytes 1093640 | tf_op jit(solution)/shard_map/ppermute | solution.py:613
  6.0 8.5 %collective-permute-start.2 = (f32[184,128]{1,0:T(8,128)S(1)}, f32[184,128]{1,0:T(8,128)S(1)}, u32[]{:S(2)}, u32[]{:S(2)}) collective-permute-start(f32[184,128]{1,0:T(8,128)S(1)} %get-tuple-element.31), channel_id=1, source_target_pairs={{0,8},{1,9},{2,10},{3,11},{4,12},{5,13},{6,14},{7,15},{8,16},{9,17... | collective-permute-start | bytes 282632 | tf_op jit(solution)/shard_map/ppermute | solution.py:613
  7.6 7.6 %collective-permute-start.3 = (f32[184,128]{1,0:T(8,128)S(1)}, f32[184,128]{1,0:T(8,128)S(1)}, u32[]{:S(2)}, u32[]{:S(2)}) collective-permute-start(f32[184,128]{1,0:T(8,128)S(1)} %get-tuple-element.32), channel_id=1, source_target_pairs={{0,24},{1,25},{2,26},{3,27},{4,28},{5,29},{6,30},{7,31},{8,0},{9,1... | collective-permute-start | bytes 282632 | tf_op jit(solution)/shard_map/ppermute | solution.py:613
  9.9 7.9 %collective-permute-start = (f32[176,128]{1,0:T(8,128)S(1)}, f32[176,128]{1,0:T(8,128)S(1)}, u32[]{:S(2)}, u32[]{:S(2)}) collective-permute-start(f32[176,128]{1,0:T(8,128)S(1)} %get-tuple-element.29), channel_id=1, source_target_pairs={{0,8},{1,9},{2,10},{3,11},{4,12},{5,13},{6,14},{7,15},{8,16},{9,17... | collective-permute-start | bytes 270344 | tf_op jit(solution)/shard_map/ppermute | solution.py:613
  9.9 7.9 %collective-permute-start.1 = (f32[176,128]{1,0:T(8,128)S(1)}, f32[176,128]{1,0:T(8,128)S(1)}, u32[]{:S(2)}, u32[]{:S(2)}) collective-permute-start(f32[176,128]{1,0:T(8,128)S(1)} %get-tuple-element.30), channel_id=1, source_target_pairs={{0,24},{1,25},{2,26},{3,27},{4,28},{5,29},{6,30},{7,31},{8,0},{9,1... | collective-permute-start | bytes 270344 | tf_op jit(solution)/shard_map/ppermute | solution.py:613
  15.2 5.0 %collective-permute-start.5 = (f32[184,128]{1,0:T(8,128)S(1)}, f32[184,128]{1,0:T(8,128)S(1)}, u32[]{:S(2)}, u32[]{:S(2)}) collective-permute-start(f32[184,128]{1,0:T(8,128)S(1)} %get-tuple-element.40), channel_id=1, source_target_pairs={{0,7},{1,2},{2,1},{3,4},{4,3},{5,6},{6,5},{7,0},{8,15},{9,10},{10,... | collective-permute-start | bytes 282632 | tf_op jit(solution)/shard_map/ppermute | solution.py:613

commit v9 on v8

--- a/solution.py
+++ b/solution.py
@@ -100,17 +100,18 @@
     mom_x = (gap[1] + gap[7]) + (gap[9] + gap[11]) + gap[13]
     mom_y = (gap[3] + gap[7]) + (gap[15] - gap[9]) + gap[17]
     mom_z = (gap[5] + gap[11]) + (gap[15] - gap[13]) - gap[17]
-    square = mom_x * mom_x + mom_y * mom_y + mom_z * mom_z
     wall = jnp.where(solid, 0.5, zero)
     even = jnp.where(pore, (1.0 - flow_plus) / 2.0, wall)
     odd = jnp.where(pore, (1.0 - flow_minus) / 2.0, -wall)
     border = jnp.where(inlet, inlet_density, jnp.where(solid, 0.0, outlet_density))
-    base = jnp.where(pore, flow_plus * density - (1.5 * flow_plus) * square, border)
-    base_18 = base * (1.0 / 18.0)
-    base_36 = base * (1.0 / 36.0)
     scale = math.sqrt(4.5 * flow_plus / 36.0)
     held = jnp.where(pore, scale, zero)
     vel = (mom_x * held, mom_y * held, mom_z * held)
+    squares = [v * v for v in vel]
+    square = squares[0] + squares[1] + squares[2]
+    base = jnp.where(pore, flow_plus * density - (1.5 * flow_plus / scale**2) * square, border)
+    base_18 = base * (1.0 / 18.0)
+    base_36 = base * (1.0 / 36.0)
     along = 3.0 * flow_minus / (36.0 * scale)
     out = [None] * COUNT
     out[0] = (even + even) * flow[0] + base * (1.0 / 3.0)
@@ -119,7 +120,7 @@
         parts = [(c, v) for c, v in zip((cx, cy, cz), vel) if c != 0]
         if len(parts) == 1:
             t = parts[0][1]
-            a = even * total[i] + (base_18 + 2.0 * (t * t))
+            a = even * total[i] + (base_18 + 2.0 * squares[i // 2])
             b = odd * gap[i] + (2.0 * along) * t
         else:
             t = parts[0][1] + parts[1][1] if parts[1][0] > 0 else parts[0][1] - parts[1][1]

time: 21.6 us -> 21.6 us (level)
  no operation moved by 1% of the time
where the time goes in v9:
time: 21.6 us; the launch traced here: 21.4 us
  starting transfers between devices  11.1 us (51%)
  Pallas kernels  6.01 us (28%)
  blocking collectives  2.46 us (11%)
  waiting for transfers between devices  1.13 us (5%)
  between operations  0.69 us (3%)
    ppermute x6, starting transfers between devices, swapped(): return lax.ppermute(block, ('gx', 'gy'), pairs)  11.1 us
    all_gather x1, blocking collectives, local(): lax.all_gather(ya, 'gy', axis_index_groups=[[j, j + 1] for j in range(0,...  2.46 us
    pallas_call x1, Pallas kernels, local(): pl.pallas_call(functools.partial(first_kernel, ext, groups), out_shape=[s...  1.96 us
    pallas_call x1, Pallas kernels, local(): pl.pallas_call(functools.partial(middle_kernel, ext, near), out_shape=[on...  1.93 us
    pallas_call x1, Pallas kernels, local(): pl.pallas_call(functools.partial(last_kernel, ext, near), out_shape=momen...  1.25 us
    ppermute x6, waiting for transfers between devices, swapped(): return lax.ppermute(block, ('gx', 'gy'), pairs)  1.13 us
    pallas_call x1, Pallas kernels, local(): pl.pallas_call(functools.partial(interior_kernel, ext, near), out_shape=[...  0.86 us
  transfers between devices with their start and end apart: 6, of which 2 were waited for; matrix products, arithmetic and copies ran while one was open for 0% of the time, Pallas kernels for 13%

profile of v9, /device:TPU:0, one launch (start us, length us, event | category | flops | bytes accessed | tf_op | source)
XLA Modules:
  0.0 21.4 jit_solution(10517819751836765912)
XLA Ops:
  0.6 2.0 %shard_map.58 = (f32[26,328,128]{2,1,0:T(8,128)S(1)}, f32[328,128]{1,0:T(8,128)S(1)}, f32[176,128]{1,0:T(8,128)S(1)}, f32[176,128]{1,0:T(8,128)S(1)}, f32[712,12...) custom-call(s32[1]{0:T(128)} %bitcast.odd_ref, f32[19,16,8,128]{3,2,1,0:T(8,128)} %flow_hbm.1, ...), custom_call_target="tpu_custom_call" | custom-call | tf_op jit(solution)/shard_map/pallas_call | solution.py:636
  2.6 3.4 %collective-permute-start.4 = (f32[712,128]{1,0:T(8,128)S(1)}, f32[712,128]{1,0:T(8,128)S(1)}, u32[]{:S(2)}, u32[]{:S(2)}) collective-permute-start(f32[712,128]{1,0:T(8,128)S(1)} %get-tuple-element.33), channel_id=1, source_target_pairs={{0,7},{1,2},{2,1},{3,4},{4,3},{5,6},{6,5},{7,0},{8,15},{9,10},{10,... | collective-permute-start | bytes 1093640 | tf_op jit(solution)/shard_map/ppermute | solution.py:614
  6.0 1.6 %collective-permute-start.2 = (f32[184,128]{1,0:T(8,128)S(1)}, f32[184,128]{1,0:T(8,128)S(1)}, u32[]{:S(2)}, u32[]{:S(2)}) collective-permute-start(f32[184,128]{1,0:T(8,128)S(1)} %get-tuple-element.31), channel_id=1, source_target_pairs={{0,8},{1,9},{2,10},{3,11},{4,12},{5,13},{6,14},{7,15},{8,16},{9,17... | collective-permute-start | bytes 282632 | tf_op jit(solution)/shard_map/ppermute | solution.py:614
  7.6 2.2 %collective-permute-start.3 = (f32[184,128]{1,0:T(8,128)S(1)}, f32[184,128]{1,0:T(8,128)S(1)}, u32[]{:S(2)}, u32[]{:S(2)}) collective-permute-start(f32[184,128]{1,0:T(8,128)S(1)} %get-tuple-element.32), channel_id=1, source_target_pairs={{0,24},{1,25},{2,26},{3,27},{4,28},{5,29},{6,30},{7,31},{8,0},{9,1... | collective-permute-start | bytes 282632 | tf_op jit(solution)/shard_map/ppermute | solution.py:614
  9.9 0.0 collective-permute-start
  9.9 3.8 %collective-permute-start.1 = (f32[176,128]{1,0:T(8,128)S(1)}, f32[176,128]{1,0:T(8,128)S(1)}, u32[]{:S(2)}, u32[]{:S(2)}) collective-permute-start(f32[176,128]{1,0:T(8,128)S(1)} %get-tuple-element.30), channel_id=1, source_target_pairs={{0,24},{1,25},{2,26},{3,27},{4,28},{5,29},{6,30},{7,31},{8,0},{9,1... | collective-permute-start | bytes 270344 | tf_op jit(solution)/shard_map/ppermute | solution.py:614
  13.7 0.9 %shard_map.59 = (f32[26,256,128]{2,1,0:T(8,128)S(1)}, f32[26,256,128]{2,1,0:T(8,128)S(1)}, f32[896,128]{1,0:T(8,128)S(1)}) custom-call(s32[1]{0:T(128)} %bitcast.odd_ref, f32[26,328,128]{2,1,0:T(8,128)S(1)} %get-tuple-element.25.post_ref._, f32[328,128]{1,0:T(8,128)S(1)} %get-tuple-element.26.kinds_ref.__), custom_call_target="tpu_custom_call" | custom-call | tf_op jit(solution)/shard_map/pallas_call | solution.py:667
  14.5 0.0 collective-permute-done.2.cup_ref
  14.6 0.7 %collective-permute-done.3.cdown_ref = f32[184,128]{1,0:T(8,128)S(1)} collective-permute-done((f32[184,128]{1,0:T(8,128)S(1)}, f32[184,128]{1,0:T(8,128)S(1)}, u32[]{:S(2)}, u32[]{:S(2)}) %collective-permute-start.3) | collective-permute-done | bytes 94240 | tf_op jit(solution)/shard_map/ppermute | solution.py:614
  15.2 0.1 collective-permute-start.5
  15.3 2.5 %all-gather = f32[1792,128]{1,0:T(8,128)S(1)} all-gather(f32[896,128]{1,0:T(8,128)S(1)} %get-tuple-element.35), channel_id=2, replica_groups={{0,1},{2,3},{4,5},{6,7},{8,9},{10,11},{12,13},{14,15},{16,17},{18,19},{..., dimensions={0}, use_global_device_ids=true | all-gather | bytes 1376256 | tf_op jit(solution)/shard_map/all_gather | solution.py:684
  17.8 0.0 collective-permute-done.up_ref
  17.8 0.0 collective-permute-done.1.down_ref
  17.8 0.0 collective-permute-done.4.yb_ref
  17.8 1.9 %shard_map.61 = (f32[26,328,128]{2,1,0:T(8,128)S(1)}, f32[328,128]{1,0:T(8,128)S(1)}, f32[26,256,128]{2,1,0:T(8,128)S(1)}, f32[26,256,128]{2,1,0:T(8,128)S(1)}, ...) custom-call(s32[1]{0:T(128)} %bitcast.odd_ref, ...), custom_call_target="tpu_custom_call", output_to_operand_aliasing={{0}: (1, {}), {1}: (2, {}), {2}: (3, {}), {3}: (4, {})} | custom-call | tf_op jit(solution)/shard_map/pallas_call | solution.py:690
  19.7 0.5 %collective-permute-done.5.far_ref = f32[184,128]{1,0:T(8,128)S(1)} collective-permute-done((f32[184,128]{1,0:T(8,128)S(1)}, f32[184,128]{1,0:T(8,128)S(1)}, u32[]{:S(2)}, u32[]{:S(2)}) %collective-permute-start.5) | collective-permute-done | bytes 94240 | tf_op jit(solution)/shard_map/ppermute | solution.py:614
  20.2 1.2 %shard_map.62 = (f32[16,8,128]{2,1,0:T(8,128)}, f32[3,16,8,128]{3,2,1,0:T(8,128)}, f32[16,8,128]{2,1,0:T(8,128)}, f32[26,328,128]{2,1,0:T(8,128)S(1)}, f32[328,1...) custom-call(s32[1]{0:T(128)} %bitcast.odd_ref, ...), custom_call_target="tpu_custom_call", output_to_operand_aliasing={{3}: (1, {}), {4}: (2, {}), {5}: (3, {}), {6}: (4, {})} | custom-call | tf_op jit(solution)/shard_map/pallas_call | solution.py:699
  (1 shorter events, 0.0 us)
Async XLA Ops:
  2.6 15.2 %collective-permute-start.4 = (f32[712,128]{1,0:T(8,128)S(1)}, f32[712,128]{1,0:T(8,128)S(1)}, u32[]{:S(2)}, u32[]{:S(2)}) collective-permute-start(f32[712,128]{1,0:T(8,128)S(1)} %get-tuple-element.33), channel_id=1, source_target_pairs={{0,7},{1,2},{2,1},{3,4},{4,3},{5,6},{6,5},{7,0},{8,15},{9,10},{10,... | collective-permute-start | bytes 1093640 | tf_op jit(solution)/shard_map/ppermute | solution.py:614
  6.0 8.5 %collective-permute-start.2 = (f32[184,128]{1,0:T(8,128)S(1)}, f32[184,128]{1,0:T(8,128)S(1)}, u32[]{:S(2)}, u32[]{:S(2)}) collective-permute-start(f32[184,128]{1,0:T(8,128)S(1)} %get-tuple-element.31), channel_id=1, source_target_pairs={{0,8},{1,9},{2,10},{3,11},{4,12},{5,13},{6,14},{7,15},{8,16},{9,17... | collective-permute-start | bytes 282632 | tf_op jit(solution)/shard_map/ppermute | solution.py:614
  7.6 7.6 %collective-permute-start.3 = (f32[184,128]{1,0:T(8,128)S(1)}, f32[184,128]{1,0:T(8,128)S(1)}, u32[]{:S(2)}, u32[]{:S(2)}) collective-permute-start(f32[184,128]{1,0:T(8,128)S(1)} %get-tuple-element.32), channel_id=1, source_target_pairs={{0,24},{1,25},{2,26},{3,27},{4,28},{5,29},{6,30},{7,31},{8,0},{9,1... | collective-permute-start | bytes 282632 | tf_op jit(solution)/shard_map/ppermute | solution.py:614
  9.9 7.9 %collective-permute-start = (f32[176,128]{1,0:T(8,128)S(1)}, f32[176,128]{1,0:T(8,128)S(1)}, u32[]{:S(2)}, u32[]{:S(2)}) collective-permute-start(f32[176,128]{1,0:T(8,128)S(1)} %get-tuple-element.29), channel_id=1, source_target_pairs={{0,8},{1,9},{2,10},{3,11},{4,12},{5,13},{6,14},{7,15},{8,16},{9,17... | collective-permute-start | bytes 270344 | tf_op jit(solution)/shard_map/ppermute | solution.py:614
  9.9 7.9 %collective-permute-start.1 = (f32[176,128]{1,0:T(8,128)S(1)}, f32[176,128]{1,0:T(8,128)S(1)}, u32[]{:S(2)}, u32[]{:S(2)}) collective-permute-start(f32[176,128]{1,0:T(8,128)S(1)} %get-tuple-element.30), channel_id=1, source_target_pairs={{0,24},{1,25},{2,26},{3,27},{4,28},{5,29},{6,30},{7,31},{8,0},{9,1... | collective-permute-start | bytes 270344 | tf_op jit(solution)/shard_map/ppermute | solution.py:614
  15.2 5.0 %collective-permute-start.5 = (f32[184,128]{1,0:T(8,128)S(1)}, f32[184,128]{1,0:T(8,128)S(1)}, u32[]{:S(2)}, u32[]{:S(2)}) collective-permute-start(f32[184,128]{1,0:T(8,128)S(1)} %get-tuple-element.40), channel_id=1, source_target_pairs={{0,7},{1,2},{2,1},{3,4},{4,3},{5,6},{6,5},{7,0},{8,15},{9,10},{10,... | collective-permute-start | bytes 282632 | tf_op jit(solution)/shard_map/ppermute | solution.py:614
